TPU v7x, 128 devices: a whole 4x4x4 slice. The times are simulated.
128 devices in a mesh: wide: 32 (over y, x, core), samp: 4 (over z).
Axes of the slice: x: 4, y: 4, z: 4, core: 2. Of those that a mesh axis runs over, the one named last changes fastest.
Arguments:
- features: bfloat16 [4, 128, 96, 128], P('samp', 'wide'), may hold values from -6 to 6
- labels: int32 [4, 128, 96], P('samp', 'wide'), may hold values from 0 to 8
- conv_weight: bfloat16 [3, 3, 128, 128], replicated, may hold values from -0.1875 to 0.1875
- down_weight: bfloat16 [512, 1024], replicated, may hold values from -0.25 to 0.25
- expand_weight: bfloat16 [3, 3, 1024, 2048], P(None, None, None, 'wide'), may hold values from -0.0625 to 0.0625
- reduce_weight: bfloat16 [3, 3, 2048, 1024], P(None, None, 'wide'), may hold values from -0.046875 to 0.046875
- up_weight: bfloat16 [1024, 512], replicated, may hold values from -0.1875 to 0.1875
- class_weight: bfloat16 [128, 9], replicated, may hold values from -3 to 3
Outputs:
- conv_grad: float32 [3, 3, 128, 128], replicated
- down_grad: float32 [512, 1024], replicated
- expand_grad: float32 [3, 3, 1024, 2048], P(None, None, 'samp', 'wide')
- reduce_grad: float32 [3, 3, 2048, 1024], P(None, None, 'wide', 'samp')
- up_grad: float32 [1024, 512], replicated
- class_grad: float32 [128, 9], replicated
All inputs are finite; a program needn't handle non-finite values.
Results may differ from a plain program's by a relative error of at most 0.012.
Values may be sent and summed in bfloat16 or wider, within the bound.
A program may use at most 192 MiB of HBM per device.

v0:
```python
import math

import jax
import jax.numpy as jnp
from jax import lax
from jax.sharding import PartitionSpec as P


def split_up(x, dim, length):
    before, after = (x.shape[:dim], x.shape[dim + 1 :])
    return jnp.moveaxis(x.reshape(*before, length, -1, *after), dim, 0)


def sum_at_owner(x, axis, dim):
    length = lax.axis_size(axis)
    pieces = lax.all_to_all(split_up(x, dim, length), axis, 0, 0, tiled=True)
    return jnp.sum(pieces.astype(jnp.float32), axis=0)


def extended(block, sides, width):
    for axis, dim in sides:
        count = lax.axis_size(axis)
        forward = [(i, i + 1) for i in range(count - 1)]
        backward = [(target, source) for source, target in forward]
        low = lax.ppermute(
            lax.slice_in_dim(block, block.shape[dim] - width, None, axis=dim), axis, forward
        )
        high = lax.ppermute(lax.slice_in_dim(block, 0, width, axis=dim), axis, backward)
        block = jnp.concatenate([low, block, high], axis=dim)
    return block


def silu_slope(value):
    logistic = jax.nn.sigmoid(value)
    return logistic * (1.0 + value * (1.0 - logistic))


def pad_both(values):
    return jnp.pad(values, ((1, 1), (1, 1), (0, 0)))


def to_depth(grid):
    height, across, channels = grid.shape
    blocks = grid.reshape(height // 2, 2, across // 2, 2, channels)
    return jnp.transpose(blocks, (0, 2, 1, 3, 4)).reshape(height // 2, across // 2, 4 * channels)


def from_depth(grid):
    height, across, channels = grid.shape
    blocks = grid.reshape(height, across, 2, 2, channels // 4)
    return jnp.transpose(blocks, (0, 2, 1, 3, 4)).reshape(2 * height, 2 * across, channels // 4)


def taps_in(padded, height, across):
    return jnp.concatenate(
        [padded[p : p + height, q : q + across] for p in range(3) for q in range(3)], axis=-1
    )


def taps_out(values):
    return jnp.concatenate(
        [jnp.pad(values, ((p, 2 - p), (q, 2 - q), (0, 0))) for p in range(3) for q in range(3)],
        axis=-1,
    )


def conv_padded(padded, weight):
    height = padded.shape[0] - 2
    across = padded.shape[1] - 2
    inward = weight.shape[2]
    outward = weight.shape[3]
    if inward <= outward:
        window = taps_in(padded, height, across).reshape(height * across, 9 * inward)
        result = jnp.dot(
            window, weight.reshape(9 * inward, outward), preferred_element_type=jnp.float32
        )
        return result.reshape(height, across, outward)
    flattened = padded.reshape((height + 2) * (across + 2), inward)
    stacked = jnp.transpose(weight, (2, 0, 1, 3)).reshape(inward, 9 * outward)
    spread_out = jnp.dot(flattened, stacked, preferred_element_type=jnp.float32).reshape(
        height + 2, across + 2, 9, outward
    )
    summed = spread_out[0:height, 0:across, 0]
    for offset in range(1, 9):
        p = offset // 3
        q = offset % 3
        summed = summed + spread_out[p : p + height, q : q + across, offset]
    return summed


def correlate(padded, values):
    height, across, outward = values.shape
    inward = padded.shape[-1]
    if inward <= outward:
        window = taps_in(padded, height, across).reshape(height * across, 9 * inward)
        result = lax.dot_general(
            window,
            values.reshape(height * across, outward),
            (((0,), (0,)), ((), ())),
            preferred_element_type=jnp.float32,
        )
        return result.reshape(3, 3, inward, outward)
    shifted = taps_out(values).reshape((height + 2) * (across + 2), 9 * outward)
    result = lax.dot_general(
        padded.reshape(-1, inward),
        shifted,
        (((0,), (0,)), ((), ())),
        preferred_element_type=jnp.float32,
    )
    return jnp.transpose(result.reshape(inward, 3, 3, outward), (1, 2, 0, 3))


def contract_rows(left, right):
    left_flat = left.reshape(-1, left.shape[-1])
    right_flat = right.reshape(-1, right.shape[-1])
    return lax.dot_general(
        left_flat, right_flat, (((0,), (0,)), ((), ())), preferred_element_type=jnp.float32
    )


def flip_kernel(weight):
    return jnp.transpose(weight[::-1, ::-1], (0, 1, 3, 2))


def keep_rows(block_rows, first_row):
    return block_rows


def project_rows(values, weight):
    return jnp.dot(values, weight, preferred_element_type=jnp.float32).astype(jnp.bfloat16)


def widen_rows(values, weight):
    return lax.dot_general(
        values, weight, (((2,), (1,)), ((), ())), preferred_element_type=jnp.float32
    ).astype(jnp.bfloat16)


def collect(values, transform):
    return transform(lax.all_gather(values, "wide", axis=0, tiled=True), jnp.int32(0))


def spread_sum(term_rows, row_total):
    return sum_at_owner(
        term_rows(jnp.int32(0), row_total * lax.axis_size("wide")).astype(jnp.bfloat16), "wide", 0
    )


def local(
    features,
    labels,
    conv_weight,
    down_weight,
    expand_weight,
    reduce_weight,
    up_weight,
    class_weight,
):
    crop_rows = features[0]
    label_map = labels[0]
    height, across, channels = crop_rows.shape
    half_rows = height // 2
    pixel_count = lax.axis_size("wide") * lax.axis_size("samp") * height * across
    loss_scale = 8.0 / math.sqrt(pixel_count)
    classes = lax.broadcasted_iota(jnp.int32, (1, 1, class_weight.shape[1]), 2)
    near_rows = extended(crop_rows, (("wide", 0),), 1)
    padded_in = jnp.pad(near_rows, ((0, 0), (1, 1), (0, 0)))
    hidden_pre = conv_padded(padded_in, conv_weight)
    hidden = jax.nn.silu(hidden_pre).astype(jnp.bfloat16)
    stacked = to_depth(hidden)
    coarse = project_rows(stacked, down_weight)
    coarse_all = collect(coarse, keep_rows)
    coarse_pad = pad_both(coarse_all)
    expand_pre = conv_padded(coarse_pad, expand_weight)
    expanded = jax.nn.silu(expand_pre).astype(jnp.bfloat16)
    expand_pad = pad_both(expanded)

    def reduce_block(first_row, row_count):
        return conv_padded(expand_pad, reduce_weight)

    bottom = (coarse.astype(jnp.float32) + spread_sum(reduce_block, half_rows)).astype(jnp.bfloat16)
    upward = from_depth(jnp.dot(bottom, up_weight, preferred_element_type=jnp.float32))
    joined_pre = upward + hidden.astype(jnp.float32)
    joined = jax.nn.silu(joined_pre).astype(jnp.bfloat16)
    logits = jnp.dot(joined, class_weight, preferred_element_type=jnp.float32)
    exp_logits = jnp.exp(logits)
    probability = exp_logits / jnp.sum(exp_logits, axis=-1, keepdims=True)
    onehot = (label_map[:, :, None] == classes).astype(jnp.float32)
    logit_grad = ((probability - onehot) * loss_scale).astype(jnp.bfloat16)
    class_grad = contract_rows(joined, logit_grad)
    joined_grad = lax.dot_general(
        logit_grad, class_weight, (((2,), (1,)), ((), ())), preferred_element_type=jnp.float32
    )
    upward_grad = (joined_grad * silu_slope(joined_pre)).astype(jnp.bfloat16)
    stacked_grad = to_depth(upward_grad)
    up_grad = contract_rows(bottom, stacked_grad)
    bottom_grad = widen_rows(stacked_grad, up_weight)
    bottom_all = collect(bottom_grad, keep_rows)
    reduce_grad = correlate(expand_pad, bottom_all)
    expanded_back = conv_padded(pad_both(bottom_all), flip_kernel(reduce_weight))
    expanded_grad = (expanded_back * silu_slope(expand_pre)).astype(jnp.bfloat16)
    expand_grad = correlate(coarse_pad, expanded_grad)
    grad_pad = pad_both(expanded_grad)
    back_expand = flip_kernel(expand_weight)

    def expand_back_block(first_row, row_count):
        return conv_padded(grad_pad, back_expand)

    coarse_grad = (
        bottom_grad.astype(jnp.float32) + spread_sum(expand_back_block, half_rows)
    ).astype(jnp.bfloat16)
    down_grad = contract_rows(stacked, coarse_grad)
    down_back = lax.dot_general(
        coarse_grad, down_weight, (((2,), (1,)), ((), ())), preferred_element_type=jnp.float32
    )
    hidden_sum = from_depth(down_back) + upward_grad.astype(jnp.float32)
    hidden_grad = (hidden_sum * silu_slope(hidden_pre)).astype(jnp.bfloat16)
    conv_grad = correlate(padded_in, hidden_grad)
    conv_grad, down_grad, up_grad, class_grad = lax.psum(
        (conv_grad, down_grad, up_grad, class_grad), ("wide", "samp")
    )
    expand_grad, reduce_grad = (
        sum_at_owner(expand_grad.astype(jnp.bfloat16), "samp", 2),
        sum_at_owner(reduce_grad.astype(jnp.bfloat16), "samp", 3),
    )
    return (conv_grad, down_grad, expand_grad, reduce_grad, up_grad, class_grad)


def solution(mesh):
    return jax.shard_map(
        local,
        mesh=mesh,
        in_specs=(
            P("samp", "wide", None, None),
            P("samp", "wide", None),
            P(),
            P(),
            P(None, None, None, "wide"),
            P(None, None, "wide", None),
            P(),
            P(),
        ),
        out_specs=(
            P(),
            P(),
            P(None, None, "samp", "wide"),
            P(None, None, "wide", "samp"),
            P(),
            P(),
        ),
        check_vma=False,
    )
```

profile of v0, /device:TPU:1, one launch (start us, length us, event | category | flops | bytes accessed | tf_op | source)
XLA Modules:
  0.0 589.7 jit_solution(12321008439119090654)
XLA Ops:
  8.1 4.5 collective-permute-start
  12.6 1.9 collective-permute-start.1
  14.5 3.2 collective-permute-done.1
  18.7 1.6 constant_dynamic-update-slice_fusion.16
  21.3 1.5 constant_dynamic-update-slice_fusion.10
  23.7 2.0 multiply_convert_fusion.3
  25.9 2.2 convolution_convert_fusion.4
  28.2 52.9 %all-gather.3.cloned.1.call-done = bf16[64,48,1024]{2,1,0:T(8,128)(2,1)} async-done(((bf16[2,48,1024]{2,1,0:T(8,128)(2,1)}), bf16[64,48,1024]{2,1,0:T(8,128)(2,1)}) %all-gather.3.cloned.1.call-update) | async-done | bytes 6291472 | tf_op jit(solution)/shard_map/all_gather | solution.py:140
  81.1 6.3 %copy.56 = bf16[64,48,1024]{2,0,1:T(8,128)(2,1)S(1)} copy(bf16[64,48,1024]{2,1,0:T(8,128)(2,1)} %all-gather.3.cloned.1.call-done) | data formatting | bytes 12582912 | tf_op jit(solution)/shard_map/all_gather | solution.py:140
  87.4 11.4 %fusion.1 = f32[66,50,9,64]{0,3,2,1:T(8,128)} fusion(bf16[9,64,1024,1]{2,1,0,3:T(8,128)(2,1)S(1)} %bitcast.176, bf16[64,48,1024]{2,0,1:T(8,128)(2,1)S(1)} %copy.56), kind=kOutput, calls=%fused_computation.3 | convolution fusion | flops 3892838400 | bytes 15074304 | tf_op jit(solution)/shard_map/dot_general | solution.py:80
  98.8 7.6 %multiply_convert_fusion = (bf16[64,48,64]{0,2,1:T(8,128)(2,1)S(1)}, f32[64,48,64]{0,2,1:T(8,128)S(1)}) fusion(f32[66,50,9,64]{0,3,2,1:T(8,128)} %fusion.1), kind=kLoop, calls=%fused_computation.34 | loop fusion | flops 2555904 | bytes 8257536 | tf_op jit(solution)/shard_map/convert_element_type | solution.py:175
  106.5 1.2 slice_dynamic-update-slice_fusion.15
  107.7 1.3 slice_dynamic-update-slice_fusion.14
  109.0 1.3 slice_dynamic-update-slice_fusion.13
  113.5 1.2 slice_dynamic-update-slice_fusion.10
  114.8 1.2 slice_dynamic-update-slice_fusion.9
  116.0 1.2 slice_dynamic-update-slice_fusion.8
  117.2 10.7 %copy.57 = bf16[64,48,576]{2,1,0:T(8,128)(2,1)} copy(bf16[64,48,576]{0,2,1:T(8,128)(2,1)} %slice_dynamic-update-slice_fusion.8) | data formatting | bytes 7077888 | tf_op jit(solution)/shard_map/concatenate | solution.py:55
  127.9 7.1 %convolution_convert_fusion.1 = bf16[64,48,1024]{2,1,0:T(8,128)(2,1)S(1)} fusion(bf16[64,48,576]{2,1,0:T(8,128)(2,1)} %copy.57, bf16[576,1024,1]{1,0,2:T(8,128)(2,1)} %bitcast.177), kind=kOutput, calls=%fused_computation.11 | convolution fusion | flops 3627024384 | bytes 11010048 | tf_op jit(solution)/shard_map/dot_general | solution.py:74
  135.0 78.0 %all_to_all.20 = bf16[32,2,48,1024]{3,2,1,0:T(8,128)(2,1)S(1)} all-to-all(bf16[32,2,48,1024]{3,2,1,0:T(8,128)(2,1)S(1)} %bitcast.166), channel_id=1, replica_groups=mesh['wide'=32,'samp'=4] {'wide'}, dimensions={0} | all-to-all | bytes 12582912 | tf_op jit(solution)/shard_map/all_to_all | solution.py:16
  213.1 1.5 convert_reduce_fusion.1
  217.4 2.4 rev.7
  219.8 2.4 rev.6
  222.2 43.3 %all-gather.5.cloned.1.call-done = bf16[64,48,1024]{2,1,0:T(8,128)(2,1)} async-done(((bf16[2,48,1024]{2,1,0:T(8,128)(2,1)}), bf16[64,48,1024]{2,1,0:T(8,128)(2,1)}) %all-gather.5.cloned.1.call-update) | async-done | bytes 6291472 | tf_op jit(solution)/shard_map/all_gather | solution.py:140
  265.4 6.4 %copy.60 = bf16[64,48,1024]{2,0,1:T(8,128)(2,1)S(1)} copy(bf16[64,48,1024]{2,1,0:T(8,128)(2,1)} %all-gather.5.cloned.1.call-done) | data formatting | bytes 12582912 | tf_op jit(solution)/shard_map/all_gather | solution.py:140
  271.9 8.4 %fusion.3 = f32[66,50,9,64]{0,3,1,2:T(8,128)S(1)} fusion(bf16[9,64,1024,1]{2,1,3,0:T(8,128)(2,1)S(1)} %bitcast.179, bf16[64,48,1024]{2,0,1:T(8,128)(2,1)S(1)} %copy.60), kind=kOutput, calls=%fused_computation.5 | convolution fusion | flops 3892838400 | bytes 15074304 | tf_op jit(solution)/shard_map/dot_general | solution.py:80
  280.2 2.6 fusion.10
  282.9 1.2 slice_dynamic-update-slice_fusion.7
  284.1 1.3 slice_dynamic-update-slice_fusion.6
  285.4 1.3 slice_dynamic-update-slice_fusion.5
  289.9 1.2 slice_dynamic-update-slice_fusion.2
  291.1 1.2 slice_dynamic-update-slice_fusion.1
  292.4 1.2 slice_dynamic-update-slice_fusion
  293.6 10.7 %copy.70 = bf16[64,48,576]{2,1,0:T(8,128)(2,1)} copy(bf16[64,48,576]{0,2,1:T(8,128)(2,1)} %slice_dynamic-update-slice_fusion) | data formatting | bytes 7077888 | tf_op jit(solution)/shard_map/concatenate | solution.py:55
  304.3 9.1 %convolution_convert_fusion = bf16[64,48,1024]{2,1,0:T(8,128)(2,1)} fusion(bf16[64,48,576]{2,1,0:T(8,128)(2,1)} %copy.70, bf16[576,1024,1]{1,0,2:T(8,128)(2,1)S(1)} %bitcast.178), kind=kOutput, calls=%fused_computation.10 | convolution fusion | flops 3627024384 | bytes 11010048 | tf_op jit(solution)/shard_map/dot_general | solution.py:74
  313.4 5.4 all-to-all-start.1
  320.8 6.3 %copy.91 = bf16[64,48,1024]{2,1,0:T(8,128)(2,1)S(1)} copy(bf16[64,48,1024]{2,0,1:T(8,128)(2,1)} %copy-done.2) | data formatting | bytes 12582912
  327.1 7.7 %pad.52.clone = bf16[66,50,1024]{2,1,0:T(8,128)(2,1)} pad(bf16[64,48,1024]{2,1,0:T(8,128)(2,1)S(1)} %copy.91, bf16[]{:T(256)} %constant.4.clone.1), padding=1_1x1_1x0_0 | pad | bytes 13049858 | tf_op jit(solution)/shard_map/jit(_pad)/pad | solution.py:39
  334.8 9.4 %reshape.180 = bf16[3300,1024,1,1]{1,0,2,3:T(8,128)(2,1)} reshape(bf16[66,50,1024]{2,1,0:T(8,128)(2,1)} %pad.52.clone) | data formatting | bytes 13516800 | tf_op jit(solution)/shard_map/reshape | solution.py:78
  344.2 6.2 %copy.77 = bf16[576,3072]{1,0:T(8,128)(2,1)} copy(bf16[576,3072]{0,1:T(8,128)(2,1)} %bitcast.163) | data formatting | bytes 7077888 | tf_op jit(solution)/shard_map/dot_general | solution.py:96
  350.4 1.8 fusion.50
  352.2 7.7 %convolution_convert_fusion.2 = bf16[3,3,64,1024]{3,2,1,0:T(8,128)(2,1)S(1)} fusion(bf16[3,3,64,3072]{3,2,1,0:T(8,128)(2,1)} %bitcast.168, bf16[3072,1024,1,1]{1,0,3,2:T(8,128)(2,1)} %bitcast.164), kind=kOutput, calls=%fused_computation.37 | convolution fusion | flops 3624468480 | bytes 11010048 | tf_op jit(solution)/shard_map/dot_general | solution.py:96
  359.9 1.2 copy.92
  362.2 1.2 pad_dynamic-update-slice_fusion.6
  364.5 1.3 pad_dynamic-update-slice_fusion.4
  365.8 1.3 pad_dynamic-update-slice_fusion.8
  367.0 1.3 pad_dynamic-update-slice_fusion.3
  368.3 1.3 pad_dynamic-update-slice_fusion.2
  369.6 1.3 pad_dynamic-update-slice_fusion.1
  370.8 1.2 pad_dynamic-update-slice_fusion
  372.1 12.9 %copy.73 = bf16[66,50,576]{2,1,0:T(8,128)(2,1)} copy(bf16[66,50,576]{0,2,1:T(8,128)(2,1)} %pad_dynamic-update-slice_fusion) | data formatting | bytes 7603200 | tf_op jit(solution)/shard_map/concatenate | solution.py:61
  385.0 7.9 %reshape.155 = bf16[3300,576]{1,0:T(8,128)(2,1)} reshape(bf16[66,50,576]{2,1,0:T(8,128)(2,1)} %copy.73) | data formatting | bytes 7603200 | tf_op jit(solution)/shard_map/reshape | solution.py:103
  392.9 6.4 %copy.74 = bf16[576,3300]{1,0:T(8,128)(2,1)} copy(bf16[576,3300]{0,1:T(8,128)(2,1)} %bitcast.162) | data formatting | bytes 7603200 | tf_op jit(solution)/shard_map/dot_general | solution.py:104
  399.3 4.3 all-to-all-start.3
  403.8 4.3 convert_reduce_fusion
  410.0 1.2 fusion.48
  411.2 2.7 fusion.49
  413.9 8.2 %fusion.12 = bf16[1024,3,3,64]{0,3,2,1:T(8,128)(2,1)S(1)} fusion(bf16[3,3,64,3300]{3,2,1,0:T(8,128)(2,1)} %bitcast.167, bf16[3300,1024,1,1]{1,0,2,3:T(8,128)(2,1)} %reshape.180), kind=kOutput, calls=%fused_computation.36 | convolution fusion | flops 3893428224 | bytes 11739648 | tf_op jit(solution)/shard_map/dot_general | solution.py:104
  423.2 4.2 all-to-all-start.2
  427.7 77.0 %psum.31 = f32[128,9]{0,1:T(8,128)} all-reduce(f32[128,9]{0,1:T(8,128)S(1)} %convolution_bitcast_fusion), channel_id=1, replica_groups=mesh['wide'=32,'samp'=4] {'wide','samp'}, use_global_device_ids=true, to_apply=%region_8.9 | all-reduce | flops 1152 | bytes 9216 | tf_op jit(solution)/shard_map/psum | solution.py:219
  506.7 69.6 %all-reduce.16.cloned.1.call-done = (f32[3,3,128,128]{3,2,1,0:T(8,128)}, f32[512,1024]{1,0:T(8,128)}, f32[1024,512]{1,0:T(8,128)}) async-done(((f32[3,3,128,128]{3,2,1,0:T(8,128)}, f32[512,1024]{1,0:T(8,128)}, f32[1024,512]{1,0:T(8,128)}), (f32[3,3,128,128]{3,2,1,0:T(8,128)}, f32[512,1024]{1,0:T(8,128)}, f32[1024,512]{1,0:T(8,128)})) %all-reduce.16.cloned.1.call-update) | async-done | bytes 4784144 | tf_op jit(solution)/shard_map/psum | solution.py:219
  576.3 2.1 copy.139
  578.4 3.2 copy.140
  581.6 1.3 copy.141
  (106 shorter events, 22.9 us)
Async XLA Ops:
  7.2 207.5 %copy-start = (bf16[1024,512]{1,0:T(8,128)(2,1)S(1)}, bf16[1024,512]{1,0:T(8,128)(2,1)}, u32[]{:S(2)}) copy-start(bf16[1024,512]{1,0:T(8,128)(2,1)} %param.14) | copy-start | bytes 3145732
  7.2 73.9 %all-gather.3.cloned.1.call-start = ((), (), s32[]{:S(2)}) async-start(), calls=%async_computation.4 | async-start | bytes 6488064 | tf_op jit(solution)/shard_map/all_gather | solution.py:140
  8.1 6.4 %collective-permute-start = (bf16[1,96,128]{2,1,0:T(8,128)(2,1)S(1)}, bf16[1,96,128]{2,1,0:T(8,128)(2,1)S(1)}, u32[]{:S(2)}, u32[]{:S(2)}) collective-permute-start(bf16[1,96,128]{2,1,0:T(8,128)(2,1)S(1)} %get-tuple-element.22), channel_id=1, source_target_pairs={{0,4},{4,8},{8,12},{12,16},{16,20},{20,24},{24,28},{28,32},{32,36}... | collective-permute-start | bytes 73736 | tf_op jit(solution)/shard_map/ppermute | solution.py:25
  12.6 5.1 collective-permute-start.1
  28.1 59.3 %copy-start.8 = (bf16[3,3,1024,64]{2,3,1,0:T(8,128)(2,1)S(1)}, bf16[3,3,1024,64]{2,3,1,0:T(8,128)(2,1)}, u32[]{:S(2)}) copy-start(bf16[3,3,1024,64]{2,3,1,0:T(8,128)(2,1)} %param.12) | copy-start | bytes 3538948
  28.1 237.3 %all-gather.5.cloned.1.call-start = ((), (), s32[]{:S(2)}) async-start(), calls=%async_computation.5 | async-start | bytes 6488064 | tf_op jit(solution)/shard_map/all_gather | solution.py:140
  87.4 11.4 %copy-start.2 = (bf16[64,48,1024]{2,0,1:T(8,128)(2,1)}, bf16[64,48,1024]{2,0,1:T(8,128)(2,1)S(1)}, u32[]{:S(2)}) copy-start(bf16[64,48,1024]{2,0,1:T(8,128)(2,1)S(1)} %copy.56) | copy-start | bytes 18874372
  213.1 1.5 copy-start.7
  213.1 2.2 copy-start.21
  213.1 2.9 copy-start.22
  215.3 0.6 copy-start.19
  216.2 55.7 %copy-start.11 = (bf16[4,96,128]{2,1,0:T(8,128)(2,1)}, bf16[4,96,128]{2,1,0:T(8,128)(2,1)S(1)}, u32[]{:S(2)}) copy-start(bf16[4,96,128]{2,1,0:T(8,128)(2,1)S(1)} %fusion.15) | copy-start | bytes 294916
  265.4 6.4 %copy-start.10 = (bf16[3,3,64,1024]{3,2,1,0:T(8,128)(2,1)S(1)}, bf16[3,3,64,1024]{3,2,1,0:T(8,128)(2,1)}, u32[]{:S(2)}) copy-start(bf16[3,3,64,1024]{3,2,1,0:T(8,128)(2,1)} %rev.6) | copy-start | bytes 3538948
  292.4 11.9 %copy-start.9 = (bf16[3,3,1024,64]{2,3,1,0:T(8,128)(2,1)S(1)}, bf16[3,3,1024,64]{2,3,1,0:T(8,128)(2,1)}, u32[]{:S(2)}) copy-start(bf16[3,3,1024,64]{2,3,1,0:T(8,128)(2,1)} %rev.7) | copy-start | bytes 3538948
  313.4 6.2 %copy-start.16 = (bf16[4,96,128]{2,1,0:T(8,128)(2,1)S(1)}, bf16[4,96,128]{2,1,0:T(8,128)(2,1)}, u32[]{:S(2)}) copy-start(bf16[4,96,128]{2,1,0:T(8,128)(2,1)} %get-tuple-element.20) | copy-start | bytes 294916
  313.4 6.2 %copy-start.18 = (bf16[4,96,128]{2,1,0:T(8,128)(2,1)S(1)}, bf16[4,96,128]{2,1,0:T(8,128)(2,1)}, u32[]{:S(2)}) copy-start(bf16[4,96,128]{2,1,0:T(8,128)(2,1)} %get-tuple-element.14) | copy-start | bytes 294916
  313.4 6.2 %copy-start.15 = (bf16[4,96,128]{2,1,0:T(8,128)(2,1)S(1)}, bf16[4,96,128]{2,1,0:T(8,128)(2,1)}, u32[]{:S(2)}) copy-start(bf16[4,96,128]{2,1,0:T(8,128)(2,1)} %get-tuple-element.19) | copy-start | bytes 294916
  313.4 6.3 %copy-start.14 = (bf16[4,96,128]{2,1,0:T(8,128)(2,1)S(1)}, bf16[4,96,128]{2,1,0:T(8,128)(2,1)}, u32[]{:S(2)}) copy-start(bf16[4,96,128]{2,1,0:T(8,128)(2,1)} %get-tuple-element.18) | copy-start | bytes 294916
  313.4 6.3 %copy-start.4 = (bf16[1,4,96,128]{3,2,1,0:T(8,128)(2,1)S(1)}, bf16[1,4,96,128]{3,2,1,0:T(8,128)(2,1)}, u32[]{:S(2)}) copy-start(bf16[1,4,96,128]{3,2,1,0:T(8,128)(2,1)} %param.8) | copy-start | bytes 294916
  313.4 6.3 %copy-start.13 = (bf16[4,96,128]{2,1,0:T(8,128)(2,1)S(1)}, bf16[4,96,128]{2,1,0:T(8,128)(2,1)}, u32[]{:S(2)}) copy-start(bf16[4,96,128]{2,1,0:T(8,128)(2,1)} %get-tuple-element.17) | copy-start | bytes 294916
  313.4 6.4 %copy-start.12 = (bf16[4,96,128]{2,1,0:T(8,128)(2,1)S(1)}, bf16[4,96,128]{2,1,0:T(8,128)(2,1)}, u32[]{:S(2)}) copy-start(bf16[4,96,128]{2,1,0:T(8,128)(2,1)} %get-tuple-element.16) | copy-start | bytes 294916
  313.4 6.4 %copy-start.17 = (bf16[4,96,128]{2,1,0:T(8,128)(2,1)S(1)}, bf16[4,96,128]{2,1,0:T(8,128)(2,1)}, u32[]{:S(2)}) copy-start(bf16[4,96,128]{2,1,0:T(8,128)(2,1)} %get-tuple-element.12) | copy-start | bytes 294916
  313.4 85.8 %all-to-all-start.1 = ((bf16[32,2,48,1024]{3,2,1,0:T(8,128)(2,1)}), bf16[32,2,48,1024]{3,2,1,0:T(8,128)(2,1)}, u32[]{:S(2)}, u32[]{:S(2)}) async-start(bf16[32,2,48,1024]{3,2,1,0:T(8,128)(2,1)} %bitcast.165), calls=%async_computation.1 | async-start | bytes 12582912 | tf_op jit(solution)/shard_map/all_to_all | solution.py:16
  399.2 8.9 %copy-start.6 = (bf16[2,48,1024]{2,1,0:T(8,128)(2,1)S(1)}, bf16[2,48,1024]{2,1,0:T(8,128)(2,1)}, u32[]{:S(2)}) copy-start(bf16[2,48,1024]{2,1,0:T(8,128)(2,1)} %convolution_convert_fusion.3) | copy-start | bytes 589828
  399.2 9.0 %copy-start.3 = (bf16[512,1024]{1,0:T(8,128)(2,1)S(1)}, bf16[512,1024]{1,0:T(8,128)(2,1)}, u32[]{:S(2)}) copy-start(bf16[512,1024]{1,0:T(8,128)(2,1)} %param.11) | copy-start | bytes 3145732
  399.3 24.0 %all-to-all-start.3 = ((bf16[4,3,3,64,256]{4,3,2,1,0:T(8,128)(2,1)}), bf16[4,3,3,64,256]{4,3,2,1,0:T(8,128)(2,1)S(1)}, u32[]{:S(2)}, u32[]{:S(2)}) async-start(bf16[4,3,3,64,256]{4,3,2,1,0:T(8,128)(2,1)} %bitcast.157), calls=%async_computation.3 | async-start | bytes 2359296 | tf_op jit(solution)/shard_map/all_to_all | solution.py:16
  403.5 172.8 %all-reduce.16.cloned.1.call-start = ((), (), s32[]{:S(2)}) async-start(), calls=%async_computation.6 | async-start | bytes 9568256 | tf_op jit(solution)/shard_map/psum | solution.py:219
  413.9 13.6 %copy-start.20 = (bf16[4,96,128]{2,1,0:T(8,128)(2,1)S(1)}, bf16[4,96,128]{2,1,0:T(8,128)(2,1)}, u32[]{:S(2)}) copy-start(bf16[4,96,128]{2,1,0:T(8,128)(2,1)} %copy-done.19) | copy-start | bytes 294916
  423.2 82.5 %all-to-all-start.2 = ((bf16[4,3,3,256,64]{3,4,2,1,0:T(8,128)(2,1)}), bf16[4,3,3,256,64]{3,4,2,1,0:T(8,128)(2,1)S(1)}, u32[]{:S(2)}, u32[]{:S(2)}) async-start(bf16[4,3,3,256,64]{3,4,2,1,0:T(8,128)(2,1)} %bitcast.159), calls=%async_computation.2 | async-start | bytes 2359296 | tf_op jit(solution)/shard_map/all_to_all | solution.py:16
  427.7 155.2 %copy-start.1 = (bf16[1024,512]{1,0:T(8,128)(2,1)S(1)}, bf16[1024,512]{1,0:T(8,128)(2,1)}, u32[]{:S(2)}) copy-start(bf16[1024,512]{1,0:T(8,128)(2,1)} %param.14) | copy-start | bytes 3145732
  576.3 5.2 copy-start.5
Sparse Core Ops, SparseCore 0:
  28.2 52.8 all-gather.2
  217.6 47.8 all-gather.4
  414.0 162.2 all-reduce.15
where the time goes:
time: 596 us; the launch traced here: 590 us
  waiting for transfers between devices  169 us (28%)
  blocking collectives  155 us (26%)
  local copies, waits for them, and re-layouts  143 us (24%)
  matrix products  64.2 us (11%)
  other arithmetic  23.4 us (4%)
  starting transfers between devices  20.7 us (3%)
  between operations  14.6 us (2%)
    all_gather x2, waiting for transfers between devices, collect(): lax.all_gather(values, 'wide', axis=0, tiled=True)  96.2 us
    all_to_all x1, blocking collectives, sum_at_owner(): pieces = lax.all_to_all(split_up(x, dim, length), axis, 0, 0, tiled=True)  78 us
    psum x1, blocking collectives, local(): lax.psum((conv_grad, down_grad, up_grad, class_grad), ('wide', 'samp'))  77 us
    psum x1, waiting for transfers between devices, local(): lax.psum((conv_grad, down_grad, up_grad, class_grad), ('wide', 'samp'))  69.6 us
    unnamed x88, local copies, waits for them, and re-layouts  43.5 us
    concatenate x6, local copies, waits for them, and re-layouts, taps_in(): jnp.concatenate([padded[p:p + height, q:q + across] for p in range(3) for...  24.7 us
    dot_general x2, matrix products, conv_padded(): jnp.dot(flattened, stacked, preferred_element_type=jnp.float32)  19.8 us
    dot_general x3, matrix products, conv_padded(): jnp.dot(window, weight.reshape(9 * inward, outward), preferred_element_ty...  18.2 us
  transfers between devices with their start and end apart: 8, of which 4 were waited for; matrix products, arithmetic and copies ran while one was open for 18% of the time, Pallas kernels for 0%

commit v1 on v0

--- a/solution.py
+++ b/solution.py
@@ -1,8 +1,11 @@
+import functools
 import math
 
 import jax
 import jax.numpy as jnp
 from jax import lax
+from jax.experimental import pallas as pl
+from jax.experimental.pallas import tpu as pltpu
 from jax.sharding import PartitionSpec as P
 
 
@@ -144,6 +147,482 @@
     return sum_at_owner(
         term_rows(jnp.int32(0), row_total * lax.axis_size("wide")).astype(jnp.bfloat16), "wide", 0
     )
+
+
+ROWS = 64
+ACROSS = 48
+SPOTS = ROWS * ACROSS
+PIECE = 192
+HALF = 96
+PART = 512
+INNER = 128
+WIDE_ROWS = 3 * INNER
+
+
+def place():
+    wide = lax.axis_index("wide")
+    core = wide % 2
+    x = (wide // 2) % 4
+    y = wide // 8
+    first = x + core * (y - x)
+    second = y + core * (x - y)
+    return core, first % 4, second % 4
+
+
+def block_of(core, first, second):
+    x = first + core * (second - first)
+    y = second + core * (first - second)
+    return y * 4 + x
+
+
+def rows_of(block, length=PIECE):
+    return pl.ds(pl.multiple_of(block * PIECE, 64), length)
+
+
+def edge_masks(length):
+    column = lax.broadcasted_iota(jnp.int32, (length, INNER), 0) % ACROSS
+    return column == 0, column == ACROSS - 1
+
+
+def from_left(values, at_left):
+    return jnp.where(at_left, 0.0, pltpu.roll(values, 1, axis=0))
+
+
+def from_right(values, at_right):
+    return jnp.where(at_right, 0.0, pltpu.roll(values, values.shape[0] - 1, axis=0))
+
+
+class Copies:
+    def __init__(self, send_sems, recv_sems):
+        self.send_sems = send_sems
+        self.recv_sems = recv_sems
+        self.sent = []
+
+    def remote(self, index, source, target, device):
+        copy = pltpu.make_async_remote_copy(
+            src_ref=source,
+            dst_ref=target,
+            send_sem=self.send_sems.at[index],
+            recv_sem=self.recv_sems.at[index],
+            device_id={"wide": device},
+            device_id_type=pl.DeviceIdType.MESH,
+        )
+        return copy
+
+    def start(self, index, source, target, device):
+        copy = self.remote(index, source, target, device)
+        copy.start()
+        self.sent.append(copy)
+
+    def arrived(self, index, target, device):
+        self.remote(index, target, target, device).wait_recv()
+
+    def finish(self):
+        for copy in self.sent:
+            copy.wait_send()
+
+
+def phase_kernel(backward, *refs):
+    if backward:
+        (x_ref, wa_hbm, wb_hbm, pre_hbm, ef_hbm, xf_hbm, out_ref, ge_ref, gf_ref) = refs[:9]
+        scratch = refs[9:]
+    else:
+        (x_ref, wa_hbm, wb_hbm, out_ref, pre_hbm, ef_hbm, xf_hbm) = refs[:7]
+        scratch = refs[7:]
+    (
+        xall, wa, wb, total, pre, other, padded, chunk, window,
+        far_out, up_out, down_out, far_in, up_in, down_in, reduced,
+        far2_out, up2_out, down2_out, far2_in, up2_in, down2_in, swap_out, swap_in,
+        send_sems, recv_sems, local_sems,
+    ) = scratch[:27]
+    core, first, second = place()
+    me = block_of(core, first, second)
+    partner = me * 2 + 1 - core
+    f_up = block_of(core, (first + 1) % 4, second) * 2 + core
+    f_down = block_of(core, (first + 3) % 4, second) * 2 + core
+    s_up = block_of(core, first, (second + 1) % 4) * 2 + core
+    s_down = block_of(core, first, (second + 3) % 4) * 2 + core
+    copies = Copies(send_sems, recv_sems)
+
+    loads = [
+        pltpu.make_async_copy(wa_hbm, wa, local_sems.at[0]),
+        pltpu.make_async_copy(wb_hbm, wb, local_sems.at[1]),
+    ]
+    if backward:
+        pre_f, ef, xf, grad = scratch[27:]
+        loads += [
+            pltpu.make_async_copy(pre_hbm, pre_f, local_sems.at[2]),
+            pltpu.make_async_copy(ef_hbm, ef, local_sems.at[3]),
+            pltpu.make_async_copy(xf_hbm, xf, local_sems.at[4]),
+        ]
+    for load in loads:
+        load.start()
+
+    barrier = pltpu.get_barrier_semaphore()
+    for device in (partner, f_up, f_down, s_up, s_down):
+        pl.semaphore_signal(
+            barrier, inc=1, device_id={"wide": device}, device_id_type=pl.DeviceIdType.MESH
+        )
+    pl.semaphore_wait(barrier, 5)
+
+    mine = pl.ds(pl.multiple_of(me * PIECE + core * HALF, 32), HALF)
+    theirs = pl.ds(pl.multiple_of(me * PIECE + (1 - core) * HALF, 32), HALF)
+    copies.start(0, x_ref.at[1 - core], xall.at[mine, :], partner)
+    xall[mine, :] = x_ref[core]
+    copies.arrived(0, xall.at[theirs, :], partner)
+
+    def piece(first_at, second_at, low=0, length=PIECE):
+        block = block_of(core, first_at % 4, second_at % 4)
+        return xall.at[pl.ds(pl.multiple_of(block * PIECE + low, 32), length), :]
+
+    def send_second(order, first_at):
+        copies.start(5 + order, piece(first_at, second), piece(first_at, second), s_up)
+        copies.start(9 + order, piece(first_at, second), piece(first_at, second), s_down)
+
+    own = piece(first, second)
+    copies.start(1, own, own, f_up)
+    copies.start(2, own, own, f_down)
+    send_second(0, first)
+
+    def clear(step, carry):
+        total[pl.ds(pl.multiple_of(step * 96, 32), 96), :] = jnp.zeros((96, WIDE_ROWS), jnp.float32)
+        return carry
+
+    lax.fori_loop(0, 33, clear, 0)
+    padded[0:ACROSS, :] = jnp.zeros((ACROSS, WIDE_ROWS), jnp.bfloat16)
+    padded[SPOTS + ACROSS :, :] = jnp.zeros((ACROSS, WIDE_ROWS), jnp.bfloat16)
+
+    left = piece(first + 3, second)
+    right = piece(first + 1, second)
+    copies.arrived(1, left, f_up)
+    low = piece(first + 3, second, 0, HALF)
+    copies.start(3, low, low, f_up)
+    copies.arrived(2, right, f_down)
+    high = piece(first + 1, second, HALF, HALF)
+    copies.start(4, high, high, f_down)
+    send_second(1, first + 3)
+    send_second(2, first + 1)
+    copies.arrived(3, piece(first + 2, second, 0, HALF), f_up)
+    copies.arrived(4, piece(first + 2, second, HALF, HALF), f_down)
+    send_second(3, first + 2)
+    for load in loads:
+        load.wait()
+
+    offsets = (0, 3, 1, 2)
+
+    def product(step, carry):
+        @pl.when(step == 1)
+        def _():
+            for order in range(4):
+                here = piece(first + offsets[order], second + 3)
+                copies.arrived(5 + order, here, s_up)
+                if order < 2:
+                    copies.remote(13 + order, here, here, s_up).start()
+
+        @pl.when(step == 2)
+        def _():
+            for order in range(4):
+                here = piece(first + offsets[order], second + 1)
+                copies.arrived(9 + order, here, s_down)
+                if order >= 2:
+                    copies.remote(13 + order, here, here, s_down).start()
+
+        @pl.when(step == 3)
+        def _():
+            for order in range(4):
+                here = piece(first + offsets[order], second + 2)
+                copies.arrived(13 + order, here, s_up)
+
+        turn = (3 * step + (step // 2) * (7 - 2 * step)) % 4
+        row = (second + turn) % 4
+        for position in range(4):
+            block = block_of(core, position, row)
+            chunk[position * PIECE : (position + 1) * PIECE, :] = xall[rows_of(block), :]
+        result = jnp.dot(chunk[...], wa[...], preferred_element_type=jnp.float32)
+        for position in range(4):
+            block = block_of(core, position, row)
+            for p in range(3):
+                where = pl.ds(pl.multiple_of(block * PIECE + (2 - p) * ACROSS, 16), PIECE)
+                total[where, :] += result[
+                    position * PIECE : (position + 1) * PIECE, p * WIDE_ROWS : (p + 1) * WIDE_ROWS
+                ]
+        return carry
+
+    lax.fori_loop(0, 4, product, 0)
+    for order in range(4):
+        here = piece(first + offsets[order], second + (3 if order < 2 else 1))
+        copies.sent.append(copies.remote(13 + order, here, here, s_up))
+
+    at_left, at_right = edge_masks(PIECE)
+
+    def fold(step, carry):
+        rows = rows_of(step)
+        padded_rows = pl.ds(pl.multiple_of(step * PIECE + ACROSS, 16), PIECE)
+        pre[rows, :] = (
+            total[padded_rows, INNER : 2 * INNER]
+            + from_left(total[padded_rows, 0:INNER], at_left)
+            + from_right(total[padded_rows, 2 * INNER :], at_right)
+        )
+        return carry
+
+    for quarter in range(4):
+        lax.fori_loop(quarter * 4, quarter * 4 + 4, fold, 0)
+        rows = pl.ds(quarter * 768, 768)
+        copies.start(17 + quarter, pre.at[rows, :], other.at[rows, :], partner)
+
+    def shape(step, carry):
+        rows = rows_of(step)
+        padded_rows = pl.ds(pl.multiple_of(step * PIECE + ACROSS, 16), PIECE)
+        value = pre[rows, :] + other[rows, :]
+        if backward:
+            value = value * silu_slope(pre_f[rows, :])
+        else:
+            other[rows, :] = value
+            value = jax.nn.silu(value)
+        value = value.astype(jnp.bfloat16).astype(jnp.float32)
+        padded[padded_rows, 0:INNER] = from_left(value, at_left).astype(jnp.bfloat16)
+        padded[padded_rows, INNER : 2 * INNER] = value.astype(jnp.bfloat16)
+        padded[padded_rows, 2 * INNER :] = from_right(value, at_right).astype(jnp.bfloat16)
+        return carry
+
+    for quarter in range(4):
+        copies.arrived(17 + quarter, other.at[pl.ds(quarter * 768, 768), :], partner)
+        lax.fori_loop(quarter * 4, quarter * 4 + 4, shape, 0)
+
+    stores = []
+    if not backward:
+        stores = [
+            pltpu.make_async_copy(other, pre_hbm, local_sems.at[2]),
+            pltpu.make_async_copy(padded, ef_hbm, local_sems.at[3]),
+            pltpu.make_async_copy(xall, xf_hbm, local_sems.at[4]),
+        ]
+        for store in stores:
+            store.start()
+
+    def gradients(left_ref, right_ref, out):
+        def clear_grad(step, carry):
+            grad[pl.ds(pl.multiple_of(step * 128, 128), 128), :] = jnp.zeros((128, PART), jnp.float32)
+            return carry
+
+        lax.fori_loop(0, 9, clear_grad, 0)
+
+        def step_of(step, carry):
+            p = step // 4
+            part = step % 4
+            window_rows = pl.ds(pl.multiple_of(part * 768 + p * ACROSS, 16), 768)
+            value_rows = pl.ds(pl.multiple_of(part * 768, 256), 768)
+            to = pl.ds(pl.multiple_of(p * WIDE_ROWS, 128), WIDE_ROWS)
+            grad[to, :] += lax.dot_general(
+                left_ref[window_rows, :],
+                right_ref[value_rows, :],
+                (((0,), (0,)), ((), ())),
+                preferred_element_type=jnp.float32,
+            )
+            return carry
+
+        lax.fori_loop(0, 12, step_of, 0)
+
+        def cast(step, carry):
+            rows = pl.ds(pl.multiple_of(step * 128, 128), 128)
+            out[rows, :] = grad[rows, :].astype(jnp.bfloat16)
+            return carry
+
+        lax.fori_loop(0, 9, cast, 0)
+
+    def narrow(values):
+        return values.astype(jnp.bfloat16)
+
+    def spread(step, carry):
+        turn = (2 - step + (step // 2) * (7 - 2 * step)) % 4
+        row = (second + turn) % 4
+        for position in range(4):
+            block = block_of(core, position, row)
+            for p in range(3):
+                window[
+                    position * PIECE : (position + 1) * PIECE, p * WIDE_ROWS : (p + 1) * WIDE_ROWS
+                ] = padded[pl.ds(pl.multiple_of(block * PIECE + p * ACROSS, 16), PIECE), :]
+        result = jnp.dot(window[...], wb[...], preferred_element_type=jnp.float32)
+        for position in range(4):
+            reduced[position] = result[position * PIECE : (position + 1) * PIECE, :]
+
+        @pl.when(step == 0)
+        def _():
+            for position in range(4):
+                far_out[position] = narrow(reduced[position])
+                copies.remote(
+                    21 + position,
+                    far_out.at[position],
+                    far_in.at[position],
+                    s_up if position < 2 else s_down,
+                ).start()
+
+        @pl.when(step == 1)
+        def _():
+            for position in (2, 3, 0, 1):
+                value = reduced[position]
+                if position < 2:
+                    copies.arrived(21 + position, far_in.at[position], s_up)
+                    value = value + far_in[position].astype(jnp.float32)
+                up_out[position] = narrow(value)
+                copies.remote(25 + position, up_out.at[position], up_in.at[position], s_up).start()
+
+        @pl.when(step == 2)
+        def _():
+            for position in (0, 1, 2, 3):
+                value = reduced[position]
+                if position >= 2:
+                    copies.arrived(21 + position, far_in.at[position], s_down)
+                    value = value + far_in[position].astype(jnp.float32)
+                down_out[position] = narrow(value)
+                copies.remote(
+                    29 + position, down_out.at[position], down_in.at[position], s_down
+                ).start()
+            if backward:
+                gradients(ef, xall, ge_ref)
+                gradients(padded, xf, gf_ref)
+
+        return carry
+
+    lax.fori_loop(0, 4, spread, 0)
+    for position in range(4):
+        copies.sent.append(
+            copies.remote(21 + position, far_out.at[position], far_in.at[position], s_up)
+        )
+        copies.sent.append(
+            copies.remote(25 + position, up_out.at[position], up_in.at[position], s_up)
+        )
+        copies.sent.append(
+            copies.remote(29 + position, down_out.at[position], down_in.at[position], s_down)
+        )
+    for position in range(4):
+        copies.arrived(25 + position, up_in.at[position], s_up)
+        copies.arrived(29 + position, down_in.at[position], s_down)
+
+    def gathered(at, low, length):
+        rows = pl.ds(low, length)
+        return (
+            reduced[at, rows, :]
+            + up_in[at, rows, :].astype(jnp.float32)
+            + down_in[at, rows, :].astype(jnp.float32)
+        )
+
+    opposite = (first + 2) % 4
+    far2_out[0] = narrow(gathered(opposite, 0, HALF))
+    copies.start(33, far2_out.at[0], far2_in.at[0], f_up)
+    far2_out[1] = narrow(gathered(opposite, HALF, HALF))
+    copies.start(34, far2_out.at[1], far2_in.at[1], f_down)
+    above = (first + 1) % 4
+    below = (first + 3) % 4
+    up2_out[HALF:, :] = narrow(gathered(above, HALF, HALF))
+    down2_out[:HALF, :] = narrow(gathered(below, 0, HALF))
+    copies.arrived(33, far2_in.at[0], f_up)
+    up2_out[:HALF, :] = narrow(gathered(above, 0, HALF) + far2_in[0].astype(jnp.float32))
+    copies.start(35, up2_out, up2_in, f_up)
+    copies.arrived(34, far2_in.at[1], f_down)
+    down2_out[HALF:, :] = narrow(gathered(below, HALF, HALF) + far2_in[1].astype(jnp.float32))
+    copies.start(36, down2_out, down2_in, f_down)
+    copies.arrived(35, up2_in, f_up)
+    copies.arrived(36, down2_in, f_down)
+
+    def settled(which):
+        rows = pl.ds(pl.multiple_of(which * HALF, 32), HALF)
+        return (
+            reduced[first, rows, :]
+            + up_in[first, rows, :].astype(jnp.float32)
+            + down_in[first, rows, :].astype(jnp.float32)
+            + up2_in[rows, :].astype(jnp.float32)
+            + down2_in[rows, :].astype(jnp.float32)
+        )
+
+    swap_out[...] = narrow(settled(1 - core))
+    copies.start(37, swap_out, swap_in, partner)
+    out_ref[core] = narrow(x_ref[core].astype(jnp.float32) + settled(core))
+    copies.arrived(37, swap_in, partner)
+    out_ref[1 - core] = narrow(x_ref[1 - core].astype(jnp.float32) + swap_in[...].astype(jnp.float32))
+    copies.finish()
+    for store in stores:
+        store.wait()
+
+
+def bottleneck(values, wa, wb, saved=None):
+    backward = saved is not None
+    b16, f32 = jnp.bfloat16, jnp.float32
+    vmem = pl.BlockSpec(memory_space=pltpu.VMEM)
+    anywhere = pl.BlockSpec(memory_space=pl.ANY)
+    padded_rows = SPOTS + 2 * ACROSS
+    keep = [
+        jax.ShapeDtypeStruct((SPOTS, INNER), f32),
+        jax.ShapeDtypeStruct((padded_rows, WIDE_ROWS), b16),
+        jax.ShapeDtypeStruct((SPOTS, PART), b16),
+    ]
+    out = jax.ShapeDtypeStruct((2, HALF, PART), b16)
+    grad = jax.ShapeDtypeStruct((9 * INNER, PART), b16)
+    scratch = [
+        pltpu.VMEM((SPOTS, PART), b16),
+        pltpu.VMEM((PART, 9 * INNER), b16),
+        pltpu.VMEM((9 * INNER, PART), b16),
+        pltpu.VMEM((padded_rows, WIDE_ROWS), f32),
+        pltpu.VMEM((SPOTS, INNER), f32),
+        pltpu.VMEM((SPOTS, INNER), f32),
+        pltpu.VMEM((padded_rows, WIDE_ROWS), b16),
+        pltpu.VMEM((4 * PIECE, PART), b16),
+        pltpu.VMEM((4 * PIECE, 9 * INNER), b16),
+        *[pltpu.VMEM((4, PIECE, PART), b16) for _ in range(6)],
+        pltpu.VMEM((4, PIECE, PART), f32),
+        pltpu.VMEM((2, HALF, PART), b16),
+        pltpu.VMEM((PIECE, PART), b16),
+        pltpu.VMEM((PIECE, PART), b16),
+        pltpu.VMEM((2, HALF, PART), b16),
+        pltpu.VMEM((PIECE, PART), b16),
+        pltpu.VMEM((PIECE, PART), b16),
+        pltpu.VMEM((HALF, PART), b16),
+        pltpu.VMEM((HALF, PART), b16),
+        pltpu.SemaphoreType.DMA((38,)),
+        pltpu.SemaphoreType.DMA((38,)),
+        pltpu.SemaphoreType.DMA((5,)),
+    ]
+    if backward:
+        scratch += [
+            pltpu.VMEM((SPOTS, INNER), f32),
+            pltpu.VMEM((padded_rows, WIDE_ROWS), b16),
+            pltpu.VMEM((SPOTS, PART), b16),
+            pltpu.VMEM((9 * INNER, PART), f32),
+        ]
+    blocks = jnp.transpose(values.reshape(HALF, 2, PART), (1, 0, 2))
+    results = pl.pallas_call(
+        functools.partial(phase_kernel, backward),
+        out_shape=[out, grad, grad] if backward else [out, *keep],
+        in_specs=[vmem] + [anywhere] * (5 if backward else 2),
+        out_specs=[vmem] * 3 if backward else [vmem] + [anywhere] * 3,
+        scratch_shapes=scratch,
+        compiler_params=pltpu.CompilerParams(
+            collective_id=2 if backward else 1,
+            has_side_effects=True,
+            vmem_limit_bytes=60 * 1024 * 1024,
+        ),
+        name="backward_phase" if backward else "forward_phase",
+    )(blocks, wa, wb, *(saved or ()))
+    total = jnp.transpose(results[0], (1, 0, 2)).reshape(HALF, 2 * PART)
+    return total, results[1:]
+
+
+def swap_cores(values):
+    count = lax.axis_size("wide")
+    return lax.ppermute(values, "wide", [(i, i ^ 1) for i in range(count)])
+
+
+def pair_part(values, dim, core):
+    own = lax.dynamic_slice_in_dim(values, core * PART, PART, axis=dim)
+    theirs = swap_cores(lax.dynamic_slice_in_dim(values, (1 - core) * PART, PART, axis=dim))
+    return jnp.where(core == 0, own, theirs), jnp.where(core == 0, theirs, own)
+
+
+def own_inner(grad, core):
+    grad = grad.reshape(9, 2, INNER // 2, PART)
+    own = lax.dynamic_index_in_dim(grad, core, axis=1, keepdims=False)
+    theirs = swap_cores(lax.dynamic_index_in_dim(grad, 1 - core, axis=1, keepdims=False))
+    low, high = jnp.where(core == 0, own, theirs), jnp.where(core == 0, theirs, own)
+    return jnp.concatenate([low, high], axis=-1)
 
 
 def local(
@@ -160,25 +639,31 @@
     label_map = labels[0]
     height, across, channels = crop_rows.shape
     half_rows = height // 2
+    half_across = across // 2
+    core = lax.axis_index("wide") % 2
     pixel_count = lax.axis_size("wide") * lax.axis_size("samp") * height * across
     loss_scale = 8.0 / math.sqrt(pixel_count)
     classes = lax.broadcasted_iota(jnp.int32, (1, 1, class_weight.shape[1]), 2)
+
+    expand_both = jnp.concatenate(
+        pair_part(expand_weight.reshape(9, 2 * PART, INNER // 2), 1, core), axis=2
+    )
+    reduce_both = jnp.concatenate(
+        pair_part(reduce_weight.reshape(9, INNER // 2, 2 * PART), 2, core), axis=1
+    )
+    wa_forward = jnp.transpose(expand_both, (1, 0, 2)).reshape(PART, 9 * INNER)
+    wb_forward = reduce_both.reshape(9 * INNER, PART)
+    wa_backward = jnp.transpose(reduce_both[::-1], (2, 0, 1)).reshape(PART, 9 * INNER)
+    wb_backward = jnp.transpose(expand_both[::-1], (0, 2, 1)).reshape(9 * INNER, PART)
+
     near_rows = extended(crop_rows, (("wide", 0),), 1)
     padded_in = jnp.pad(near_rows, ((0, 0), (1, 1), (0, 0)))
     hidden_pre = conv_padded(padded_in, conv_weight)
     hidden = jax.nn.silu(hidden_pre).astype(jnp.bfloat16)
     stacked = to_depth(hidden)
     coarse = project_rows(stacked, down_weight)
-    coarse_all = collect(coarse, keep_rows)
-    coarse_pad = pad_both(coarse_all)
-    expand_pre = conv_padded(coarse_pad, expand_weight)
-    expanded = jax.nn.silu(expand_pre).astype(jnp.bfloat16)
-    expand_pad = pad_both(expanded)
-
-    def reduce_block(first_row, row_count):
-        return conv_padded(expand_pad, reduce_weight)
-
-    bottom = (coarse.astype(jnp.float32) + spread_sum(reduce_block, half_rows)).astype(jnp.bfloat16)
+    bottom, saved = bottleneck(coarse.reshape(-1, 2 * PART), wa_forward, wb_forward)
+    bottom = bottom.reshape(half_rows, half_across, 2 * PART)
     upward = from_depth(jnp.dot(bottom, up_weight, preferred_element_type=jnp.float32))
     joined_pre = upward + hidden.astype(jnp.float32)
     joined = jax.nn.silu(joined_pre).astype(jnp.bfloat16)
@@ -195,20 +680,10 @@
     stacked_grad = to_depth(upward_grad)
     up_grad = contract_rows(bottom, stacked_grad)
     bottom_grad = widen_rows(stacked_grad, up_weight)
-    bottom_all = collect(bottom_grad, keep_rows)
-    reduce_grad = correlate(expand_pad, bottom_all)
-    expanded_back = conv_padded(pad_both(bottom_all), flip_kernel(reduce_weight))
-    expanded_grad = (expanded_back * silu_slope(expand_pre)).astype(jnp.bfloat16)
-    expand_grad = correlate(coarse_pad, expanded_grad)
-    grad_pad = pad_both(expanded_grad)
-    back_expand = flip_kernel(expand_weight)
-
-    def expand_back_block(first_row, row_count):
-        return conv_padded(grad_pad, back_expand)
-
-    coarse_grad = (
-        bottom_grad.astype(jnp.float32) + spread_sum(expand_back_block, half_rows)
-    ).astype(jnp.bfloat16)
+    coarse_grad, (reduce_grad, expand_grad) = bottleneck(
+        bottom_grad.reshape(-1, 2 * PART), wa_backward, wb_backward, saved
+    )
+    coarse_grad = coarse_grad.reshape(half_rows, half_across, 2 * PART)
     down_grad = contract_rows(stacked, coarse_grad)
     down_back = lax.dot_general(
         coarse_grad, down_weight, (((2,), (1,)), ((), ())), preferred_element_type=jnp.float32
@@ -219,10 +694,10 @@
     conv_grad, down_grad, up_grad, class_grad = lax.psum(
         (conv_grad, down_grad, up_grad, class_grad), ("wide", "samp")
     )
-    expand_grad, reduce_grad = (
-        sum_at_owner(expand_grad.astype(jnp.bfloat16), "samp", 2),
-        sum_at_owner(reduce_grad.astype(jnp.bfloat16), "samp", 3),
-    )
+    reduce_grad = sum_at_owner(own_inner(reduce_grad, core), "samp", 2)
+    expand_grad = sum_at_owner(own_inner(expand_grad, core)[::-1], "samp", 2)
+    reduce_grad = reduce_grad.reshape(3, 3, INNER // 2, -1)
+    expand_grad = jnp.transpose(expand_grad, (0, 2, 1)).reshape(3, 3, -1, INNER // 2)
     return (conv_grad, down_grad, expand_grad, reduce_grad, up_grad, class_grad)
 
 

time: 596 us -> 377 us (0.63)
  Pallas kernels: 0 us -> 138 us
  waiting for transfers between devices: 169 us -> 67.8 us
  local copies, waits for them, and re-layouts: 143 us -> 45.3 us
  blocking collectives: 155 us -> 73.1 us
  matrix products: 64.2 us -> 13.1 us
  other arithmetic: 23.4 us -> 7.86 us
    pallas_call x0 -> x2, Pallas kernels: none -> 138 us  [bottleneck(): pl.pallas_call(functools.partial(phase_kernel, backward), out_shape=[out,...]
    all_gather x2 -> x0, waiting for transfers between devices: 96.2 us -> none  [collect(): lax.all_gather(values, 'wide', axis=0, tiled=True)]
    all_to_all x1 -> x0, blocking collectives: 78 us -> none  [sum_at_owner(): pieces = lax.all_to_all(split_up(x, dim, length), axis, 0, 0, tiled=True)]
    dot_general x3 -> x0, matrix products: 27.9 us -> none  [the longest x2 19.8 us: conv_padded(): jnp.dot(flattened, stacked, preferred_element_type=jnp.float32)]
    unnamed x88 -> x69, local copies, waits for them, and re-layouts: 43.5 us -> 17.6 us
    concatenate x6 -> x2, local copies, waits for them, and re-layouts: 24.7 us -> 1.44 us  [taps_in(): jnp.concatenate([padded[p:p + height, q:q + across] for p in range(3) for...]
    psum x1, waiting for transfers between devices: 69.6 us -> 51.7 us  [local(): lax.psum((conv_grad, down_grad, up_grad, class_grad), ('wide', 'samp'))]
    dot_general x3 -> x1, matrix products: 18.2 us -> 1.08 us  [conv_padded(): jnp.dot(window, weight.reshape(9 * inward, outward), preferred_element_ty...]
  transfers between devices with their start and end apart: 8 -> 9, of which waited for: 4 -> 3; matrix products, arithmetic and copies ran while one was open for 18% -> 11% of each run, Pallas kernels for 0% -> 0%
where the time goes in v1:
time: 377 us; the launch traced here: 376 us
  Pallas kernels  138 us (37%)
  blocking collectives  73.1 us (19%)
  waiting for transfers between devices  67.8 us (18%)
  local copies, waits for them, and re-layouts  45.3 us (12%)
  starting transfers between devices  15.8 us (4%)
  between operations  14.5 us (4%)
  matrix products  13.1 us (3%)
  other arithmetic  7.86 us (2%)
    pallas_call x2, Pallas kernels, bottleneck(): pl.pallas_call(functools.partial(phase_kernel, backward), out_shape=[out,...  138 us
    psum x1, blocking collectives, local(): lax.psum((conv_grad, down_grad, up_grad, class_grad), ('wide', 'samp'))  73.1 us
    psum x1, waiting for transfers between devices, local(): lax.psum((conv_grad, down_grad, up_grad, class_grad), ('wide', 'samp'))  51.7 us
    unnamed x69, local copies, waits for them, and re-layouts  17.6 us
    all_to_all x2, waiting for transfers between devices, sum_at_owner(): pieces = lax.all_to_all(split_up(x, dim, length), axis, 0, 0, tiled=True)  15.1 us
    all_to_all x2, starting transfers between devices, sum_at_owner(): pieces = lax.all_to_all(split_up(x, dim, length), axis, 0, 0, tiled=True)  8.7 us
  transfers between devices with their start and end apart: 9, of which 3 were waited for; matrix products, arithmetic and copies ran while one was open for 11% of the time, Pallas kernels for 0%

profile of v1, /device:TPU:1, one launch (start us, length us, event | category | flops | bytes accessed | tf_op | source)
XLA Modules:
  0.0 375.5 jit_solution(16587734149187924700)
XLA Ops:
  7.3 2.1 constant_dynamic-slice_fusion.1
  9.3 1.4 collective-permute-start.2
  10.8 3.1 collective-permute-start
  13.9 1.9 collective-permute-start.1
  15.8 0.9 constant_dynamic-slice_fusion
  16.7 1.4 copy.61
  18.1 1.0 collective-permute-done.1
  19.1 0.7 constant_dynamic-update-slice_fusion.16
  20.0 0.7 constant_dynamic-update-slice_fusion.10
  20.6 0.8 constant_dynamic-update-slice_fusion.9
  21.4 1.1 multiply_convert_fusion.2
  22.6 0.7 reshape.101
  23.3 0.9 constant_dynamic-update-slice_fusion.8
  24.2 1.9 convolution_convert_fusion.1
  26.1 0.9 constant_dynamic-update-slice_fusion.7
  27.0 0.9 constant_dynamic-update-slice_fusion.6
  28.0 0.7 reshape_reshape.22
  28.6 1.1 reshape_reshape.18
  29.7 0.7 copy.75
  30.4 0.9 constant_dynamic-update-slice_fusion.3
  31.4 0.9 copy-done.12
  32.3 1.6 constant_dynamic-update-slice_fusion.2
  33.9 1.5 constant_dynamic-update-slice_fusion.1
  35.4 0.6 constant_dynamic-update-slice_fusion
  36.1 2.2 copy.42
  38.3 1.3 broadcast_select_fusion.3
  39.7 1.2 rev.10
  40.9 1.4 copy.45.refs_1_
  42.3 1.3 broadcast_select_fusion.1
  43.8 0.9 copy-done.1
  44.7 65.6 %forward_phase.1 = (bf16[2,96,512]{2,1,0:T(8,128)(2,1)}, f32[3072,128]{1,0:T(8,128)}, bf16[3168,384]{1,0:T(8,128)(2,1)}, bf16[3072,512]{1,0:T(8,128)(2,1)}) custom-call(bf16[2,96,512]{2,1,0:T(8,128)(2,1)} %bitcast.163, bf16[512,1152]{1,0:T(8,128)(2,1)} %copy.45.refs_1_, bf16[1152,512]{1,0:T(8,128)(2,1)} %bitcast.137), custom_call_target="tpu_custom_call" | custom-call | tf_op jit(solution)/shard_map/forward_phase/pallas_call | solution.py:592
  110.4 1.1 copy.46
  111.5 0.8 reshape.121
  112.3 1.4 convolution_bitcast_fusion.1
  113.9 0.6 copy-done.20
  114.8 1.8 fusion.1
  116.5 1.0 copy.76
  117.5 0.7 reshape.108
  118.2 0.7 reshape_reshape.23
  118.9 1.3 convolution_convert_fusion
  120.4 0.7 copy.74
  121.1 1.4 copy.51.refs_1_
  122.5 72.4 %backward_phase.1 = (bf16[2,96,512]{2,1,0:T(8,128)(2,1)}, bf16[1152,512]{1,0:T(8,128)(2,1)}, bf16[1152,512]{1,0:T(8,128)(2,1)}) custom-call(bf16[2,96,512]{2,1,0:T(8,128)(2,1)} %bitcast.173, bf16[512,1152]{1,0:T(8,128)(2,1)} %copy.51.refs_1_, bf16[1152,512]{1,0:T(8,128)(2,1)} %bitcast.142, f32[3072,128]{1,0:T(8,128)} %get-tuple-element.14.refs_3_, ...), custom_call_target="tpu_custom_call" | custom-call | tf_op jit(solution)/shard_map/backward_phase/pallas_call | solution.py:592
  194.9 1.2 dynamic-slice_bitcast_fusion
  196.6 0.5 convolution_bitcast_fusion
  197.4 1.8 fusion.30
  199.3 1.2 fusion.28
  200.5 1.8 fusion.29
  202.3 1.2 copy-done.10
  203.6 0.9 dynamic-slice_bitcast_fusion.1
  205.1 1.2 copy.72
  206.3 5.0 %all-to-all-start.1 = ((bf16[4,9,64,256]{3,2,1,0:T(8,128)(2,1)}), bf16[4,9,64,256]{3,2,1,0:T(8,128)(2,1)S(1)}, u32[]{:S(2)}, u32[]{:S(2)}) async-start(bf16[4,9,64,256]{3,2,1,0:T(8,128)(2,1)} %bitcast.129), calls=%async_computation.1 | async-start | bytes 2359296 | tf_op jit(solution)/shard_map/all_to_all | solution.py:19
  211.4 1.1 bitcast_select_fusion.3
  212.7 1.2 rev.11
  213.8 2.5 copy.73
  216.3 15.1 %all-to-all-done.1 = bf16[4,9,64,256]{3,2,1,0:T(8,128)(2,1)S(1)} async-done(((bf16[4,9,64,256]{3,2,1,0:T(8,128)(2,1)}), bf16[4,9,64,256]{3,2,1,0:T(8,128)(2,1)S(1)}, u32[]{:S(2)}, u32[]{:S(2)}) %all-to-all-start.1) | async-done | bytes 1179680 | tf_op jit(solution)/shard_map/all_to_all | solution.py:19
  231.5 3.7 all-to-all-start
  235.3 73.1 %psum.31 = f32[128,9]{0,1:T(8,128)} all-reduce(f32[128,9]{0,1:T(8,128)S(1)} %convolution_bitcast_fusion.2), channel_id=1, replica_groups=mesh['wide'=32,'samp'=4] {'wide','samp'}, use_global_device_ids=true, to_apply=%region_6.7 | all-reduce | flops 1152 | bytes 9216 | tf_op jit(solution)/shard_map/psum | solution.py:694
  308.4 1.0 convert_reduce_fusion
  309.4 1.0 convert_reduce_fusion.1
  310.4 51.7 %all-reduce.4.cloned.1.call-done = (f32[3,3,128,128]{3,2,1,0:T(8,128)}, f32[512,1024]{1,0:T(8,128)}, f32[1024,512]{1,0:T(8,128)}) async-done(((f32[3,3,128,128]{3,2,1,0:T(8,128)}, f32[512,1024]{1,0:T(8,128)}, f32[1024,512]{1,0:T(8,128)}), (f32[3,3,128,128]{3,2,1,0:T(8,128)}, f32[512,1024]{1,0:T(8,128)}, f32[1024,512]{1,0:T(8,128)})) %all-reduce.4.cloned.1.call-update) | async-done | bytes 4784144 | tf_op jit(solution)/shard_map/psum | solution.py:694
  362.1 1.9 copy.97
  364.0 3.3 copy.98
  367.3 1.3 copy.99
  (87 shorter events, 3.1 us)
Async XLA Ops:
  7.2 17.0 %copy-start = (bf16[512,1024]{1,0:T(8,128)(2,1)S(1)}, bf16[512,1024]{1,0:T(8,128)(2,1)}, u32[]{:S(2)}) copy-start(bf16[512,1024]{1,0:T(8,128)(2,1)} %param.11) | copy-start | bytes 3145732
  7.2 3.6 copy-start.6
  7.2 8.6 %copy-start.9 = (bf16[3,3,64,1024]{3,2,1,0:T(8,128)(2,1)S(1)}, bf16[3,3,64,1024]{3,2,1,0:T(8,128)(2,1)}, u32[]{:S(2)}) copy-start(bf16[3,3,64,1024]{3,2,1,0:T(8,128)(2,1)} %param.13) | copy-start | bytes 3538948
  7.2 354.9 %all-reduce.4.cloned.1.call-start = ((), (), s32[]{:S(2)}) async-start(), calls=%async_computation.2 | async-start | bytes 9568256 | tf_op jit(solution)/shard_map/psum | solution.py:694
  7.3 9.4 %copy-start.2 = (bf16[1024,512]{1,0:T(8,128)(2,1)S(1)}, bf16[1024,512]{1,0:T(8,128)(2,1)}, u32[]{:S(2)}) copy-start(bf16[1024,512]{1,0:T(8,128)(2,1)} %param.14) | copy-start | bytes 3145732
  9.3 28.9 %collective-permute-start.2 = (bf16[9,512,64]{1,2,0:T(8,128)(2,1)}, bf16[9,512,64]{1,2,0:T(8,128)(2,1)}, u32[]{:S(2)}, u32[]{:S(2)}) collective-permute-start(bf16[9,512,64]{1,2,0:T(8,128)(2,1)} %constant_dynamic-slice_fusion.1), channel_id=1, source_target_pairs={{0,4},{4,0},{8,12},{12,8},{16,20},{20,16},{24,28},{28,24},{32,36},... | collective-permute-start | bytes 1769480 | tf_op jit(solution)/shard_map/ppermute | solution.py:611
  10.8 7.3 %collective-permute-start = (bf16[1,96,128]{2,1,0:T(8,128)(2,1)S(1)}, bf16[1,96,128]{2,1,0:T(8,128)(2,1)S(1)}, u32[]{:S(2)}, u32[]{:S(2)}) collective-permute-start(bf16[1,96,128]{2,1,0:T(8,128)(2,1)S(1)} %get-tuple-element.42), channel_id=1, source_target_pairs={{0,4},{4,8},{8,12},{12,16},{16,20},{20,24},{24,28},{28,32},{32,36}... | collective-permute-start | bytes 73736 | tf_op jit(solution)/shard_map/ppermute | solution.py:28
  13.9 5.1 %collective-permute-start.1 = (bf16[1,96,128]{2,1,0:T(8,128)(2,1)S(1)}, bf16[1,96,128]{2,1,0:T(8,128)(2,1)S(1)}, u32[]{:S(2)}, u32[]{:S(2)}) collective-permute-start(bf16[1,96,128]{2,1,0:T(8,128)(2,1)S(1)} %get-tuple-element.43), channel_id=1, source_target_pairs={{4,0},{8,4},{12,8},{16,12},{20,16},{24,20},{28,24},{32,28},{36,32}... | collective-permute-start | bytes 73736 | tf_op jit(solution)/shard_map/ppermute | solution.py:31
  16.7 25.6 %collective-permute-start.3 = (bf16[9,64,512]{2,1,0:T(8,128)(2,1)}, bf16[9,64,512]{2,1,0:T(8,128)(2,1)}, u32[]{:S(2)}, u32[]{:S(2)}) collective-permute-start(bf16[9,64,512]{2,1,0:T(8,128)(2,1)} %constant_dynamic-slice_fusion), channel_id=1, source_target_pairs={{0,4},{4,0},{8,12},{12,8},{16,20},{20,16},{24,28},{28,24},{32,36},... | collective-permute-start | bytes 1769480 | tf_op jit(solution)/shard_map/ppermute | solution.py:611
  19.8 1.6 copy-start.24
  22.5 0.8 copy-start.18
  31.3 0.9 copy-start.12
  32.3 6.0 %copy-start.8 = (bf16[3,3,1024,64]{2,3,1,0:T(8,128)(2,1)S(1)}, bf16[3,3,1024,64]{2,3,1,0:T(8,128)(2,1)}, u32[]{:S(2)}) copy-start(bf16[3,3,1024,64]{2,3,1,0:T(8,128)(2,1)} %param.12) | copy-start | bytes 3538948
  43.7 1.0 copy-start.1
  44.7 67.6 %copy-start.4 = (bf16[512,1024]{1,0:T(8,128)(2,1)S(1)}, bf16[512,1024]{1,0:T(8,128)(2,1)}, u32[]{:S(2)}) copy-start(bf16[512,1024]{1,0:T(8,128)(2,1)} %copy.61) | copy-start | bytes 3145732
  112.3 1.5 copy-start.19
  112.3 2.3 copy-start.23
  112.3 2.5 copy-start.25
  113.9 5.0 %copy-start.3 = (bf16[1024,512]{1,0:T(8,128)(2,1)S(1)}, bf16[1024,512]{1,0:T(8,128)(2,1)}, u32[]{:S(2)}) copy-start(bf16[1024,512]{1,0:T(8,128)(2,1)} %param.14) | copy-start | bytes 3145732
  113.9 0.6 copy-start.20
  194.9 1.3 copy-start.13
  194.9 1.4 copy-start.14
  196.1 8.8 %collective-permute-start.5 = (bf16[9,64,512]{2,1,0:T(8,128)(2,1)S(1)}, bf16[9,64,512]{2,1,0:T(8,128)(2,1)S(1)}, u32[]{:S(2)}, u32[]{:S(2)}) collective-permute-start(bf16[9,64,512]{2,1,0:T(8,128)(2,1)S(1)} %dynamic-slice_bitcast_fusion), channel_id=1, source_target_pairs={{0,4},{4,0},{8,12},{12,8},{16,20},{20,16},{24,28},{28,24},{32,36},... | collective-permute-start | bytes 1769480 | tf_op jit(solution)/shard_map/ppermute | solution.py:611
  196.5 0.9 copy-start.16
  197.4 1.8 copy-start.17
  197.4 1.8 copy-start.22
  197.4 1.9 copy-start.5
  199.2 1.3 copy-start.15
  202.3 1.3 copy-start.10
  202.3 2.6 copy-start.11
  204.4 6.9 %collective-permute-start.4 = (bf16[9,64,512]{2,1,0:T(8,128)(2,1)}, bf16[9,64,512]{2,1,0:T(8,128)(2,1)}, u32[]{:S(2)}, u32[]{:S(2)}) collective-permute-start(bf16[9,64,512]{2,1,0:T(8,128)(2,1)} %dynamic-slice_bitcast_fusion.1), channel_id=1, source_target_pairs={{0,4},{4,0},{8,12},{12,8},{16,20},{20,16},{24,28},{28,24},{32,36},... | collective-permute-start | bytes 1769480 | tf_op jit(solution)/shard_map/ppermute | solution.py:611
  206.3 25.1 %all-to-all-start.1 = ((bf16[4,9,64,256]{3,2,1,0:T(8,128)(2,1)}), bf16[4,9,64,256]{3,2,1,0:T(8,128)(2,1)S(1)}, u32[]{:S(2)}, u32[]{:S(2)}) async-start(bf16[4,9,64,256]{3,2,1,0:T(8,128)(2,1)} %bitcast.129), calls=%async_computation.1 | async-start | bytes 2359296 | tf_op jit(solution)/shard_map/all_to_all | solution.py:19
  231.5 3.7 copy-start.21
  231.5 78.0 %all-to-all-start = ((bf16[4,9,64,256]{3,2,1,0:T(8,128)(2,1)}), bf16[4,9,64,256]{3,2,1,0:T(8,128)(2,1)S(1)}, u32[]{:S(2)}, u32[]{:S(2)}) async-start(bf16[4,9,64,256]{3,2,1,0:T(8,128)(2,1)} %bitcast.131), calls=%async_computation | async-start | bytes 2359296 | tf_op jit(solution)/shard_map/all_to_all | solution.py:19
  364.0 3.3 copy-start.7
Sparse Core Ops, SparseCore 0:
  202.4 159.6 all-reduce.3

commit v2 on v1

--- a/solution.py
+++ b/solution.py
@@ -204,7 +204,7 @@
             dst_ref=target,
             send_sem=self.send_sems.at[index],
             recv_sem=self.recv_sems.at[index],
-            device_id={"wide": device},
+            device_id=device if isinstance(device, dict) else {"wide": device},
             device_id_type=pl.DeviceIdType.MESH,
         )
         return copy
@@ -249,7 +249,7 @@
         pltpu.make_async_copy(wb_hbm, wb, local_sems.at[1]),
     ]
     if backward:
-        pre_f, ef, xf, grad = scratch[27:]
+        pre_f, ef, xf, grad, full, give, zfar_in, zup_out, zdown_out, zup_in, zdown_in = scratch[27:]
         loads += [
             pltpu.make_async_copy(pre_hbm, pre_f, local_sems.at[2]),
             pltpu.make_async_copy(ef_hbm, ef, local_sems.at[3]),
@@ -258,12 +258,18 @@
     for load in loads:
         load.start()
 
+    peers = [{"wide": device} for device in (partner, f_up, f_down, s_up, s_down)]
+    if backward:
+        depth = lax.axis_index("samp")
+        z_up = {"samp": (depth + 1) % 4}
+        z_down = {"samp": (depth + 3) % 4}
+        peers += [z_up, z_down]
     barrier = pltpu.get_barrier_semaphore()
-    for device in (partner, f_up, f_down, s_up, s_down):
+    for device in peers:
         pl.semaphore_signal(
-            barrier, inc=1, device_id={"wide": device}, device_id_type=pl.DeviceIdType.MESH
-        )
-    pl.semaphore_wait(barrier, 5)
+            barrier, inc=1, device_id=device, device_id_type=pl.DeviceIdType.MESH
+        )
+    pl.semaphore_wait(barrier, len(peers))
 
     mine = pl.ds(pl.multiple_of(me * PIECE + core * HALF, 32), HALF)
     theirs = pl.ds(pl.multiple_of(me * PIECE + (1 - core) * HALF, 32), HALF)
@@ -288,7 +294,79 @@
         total[pl.ds(pl.multiple_of(step * 96, 32), 96), :] = jnp.zeros((96, WIDE_ROWS), jnp.float32)
         return carry
 
+    def clear_grad(step, carry):
+        grad[pl.ds(pl.multiple_of(step * INNER, 128), INNER), :] = jnp.zeros((INNER, PART), jnp.float32)
+        return carry
+
+    def add_gradient():
+        grad[...] += lax.dot_general(
+            window[...], chunk[...], (((0,), (0,)), ((), ())), preferred_element_type=jnp.float32
+        )
+
+    def fill_window(source, row):
+        for position in range(4):
+            block = block_of(core, position, row)
+            for p in range(3):
+                window[
+                    position * PIECE : (position + 1) * PIECE, p * WIDE_ROWS : (p + 1) * WIDE_ROWS
+                ] = source[pl.ds(pl.multiple_of(block * PIECE + p * ACROSS, 16), PIECE), :]
+
+    def fill_chunk(source, row):
+        for position in range(4):
+            block = block_of(core, position, row)
+            chunk[position * PIECE : (position + 1) * PIECE, :] = source[rows_of(block), :]
+
+    def hand_over(which):
+        def pack(tap, carry):
+            to = pl.ds(pl.multiple_of(tap * 64, 64), 64)
+            own_rows = pl.ds(pl.multiple_of(tap * INNER + core * 64, 64), 64)
+            other_rows = pl.ds(pl.multiple_of(tap * INNER + (1 - core) * 64, 64), 64)
+            full[which, core, to, :] = grad[own_rows, :].astype(jnp.bfloat16)
+            give[which, to, :] = grad[other_rows, :].astype(jnp.bfloat16)
+            return carry
+
+        lax.fori_loop(0, 9, pack, 0)
+        copies.start(38 + which, give.at[which], full.at[which, core], partner)
+
+    def share(which, at, low, length):
+        at = at % 4
+        lanes = pl.ds(pl.multiple_of((at % 2) * 256, 256), 256)
+        return full.at[which, at // 2, pl.ds(low, length), lanes]
+
+    def depth_far(which):
+        copies.arrived(38 + which, full.at[which, 1 - core], partner)
+        copies.start(40 + which, share(which, depth + 2, 0, 288), zfar_in.at[which, 0], z_up)
+        copies.start(42 + which, share(which, depth + 2, 288, 288), zfar_in.at[which, 1], z_down)
+
+    def depth_near(which):
+        near = share(which, depth + 1, 288, 288)[...]
+        zup_out[which, 288:576, :] = near
+        near = share(which, depth + 3, 0, 288)[...]
+        zdown_out[which, 0:288, :] = near
+        copies.arrived(40 + which, zfar_in.at[which, 0], z_up)
+        near = share(which, depth + 1, 0, 288)[...].astype(jnp.float32)
+        zup_out[which, 0:288, :] = narrow(near + zfar_in[which, 0].astype(jnp.float32))
+        copies.start(44 + which, zup_out.at[which], zup_in.at[which], z_up)
+        copies.arrived(42 + which, zfar_in.at[which, 1], z_down)
+        near = share(which, depth + 3, 288, 288)[...].astype(jnp.float32)
+        zdown_out[which, 288:576, :] = narrow(near + zfar_in[which, 1].astype(jnp.float32))
+        copies.start(46 + which, zdown_out.at[which], zdown_in.at[which], z_down)
+
+    def depth_own(which, out):
+        copies.arrived(44 + which, zup_in.at[which], z_up)
+        copies.arrived(46 + which, zdown_in.at[which], z_down)
+        out[...] = (
+            share(which, depth, 0, 576)[...].astype(jnp.float32)
+            + zup_in[which].astype(jnp.float32)
+            + zdown_in[which].astype(jnp.float32)
+        )
+
+    def narrow(values):
+        return values.astype(jnp.bfloat16)
+
     lax.fori_loop(0, 33, clear, 0)
+    if backward:
+        lax.fori_loop(0, 9, clear_grad, 0)
     padded[0:ACROSS, :] = jnp.zeros((ACROSS, WIDE_ROWS), jnp.bfloat16)
     padded[SPOTS + ACROSS :, :] = jnp.zeros((ACROSS, WIDE_ROWS), jnp.bfloat16)
 
@@ -335,9 +413,7 @@
 
         turn = (3 * step + (step // 2) * (7 - 2 * step)) % 4
         row = (second + turn) % 4
-        for position in range(4):
-            block = block_of(core, position, row)
-            chunk[position * PIECE : (position + 1) * PIECE, :] = xall[rows_of(block), :]
+        fill_chunk(xall, row)
         result = jnp.dot(chunk[...], wa[...], preferred_element_type=jnp.float32)
         for position in range(4):
             block = block_of(core, position, row)
@@ -346,6 +422,9 @@
                 total[where, :] += result[
                     position * PIECE : (position + 1) * PIECE, p * WIDE_ROWS : (p + 1) * WIDE_ROWS
                 ]
+        if backward:
+            fill_window(ef, row)
+            add_gradient()
         return carry
 
     lax.fori_loop(0, 4, product, 0)
@@ -369,6 +448,10 @@
         lax.fori_loop(quarter * 4, quarter * 4 + 4, fold, 0)
         rows = pl.ds(quarter * 768, 768)
         copies.start(17 + quarter, pre.at[rows, :], other.at[rows, :], partner)
+
+    if backward:
+        hand_over(0)
+        lax.fori_loop(0, 9, clear_grad, 0)
 
     def shape(step, carry):
         rows = rows_of(step)
@@ -399,48 +482,13 @@
         for store in stores:
             store.start()
 
-    def gradients(left_ref, right_ref, out):
-        def clear_grad(step, carry):
-            grad[pl.ds(pl.multiple_of(step * 128, 128), 128), :] = jnp.zeros((128, PART), jnp.float32)
-            return carry
-
-        lax.fori_loop(0, 9, clear_grad, 0)
-
-        def step_of(step, carry):
-            p = step // 4
-            part = step % 4
-            window_rows = pl.ds(pl.multiple_of(part * 768 + p * ACROSS, 16), 768)
-            value_rows = pl.ds(pl.multiple_of(part * 768, 256), 768)
-            to = pl.ds(pl.multiple_of(p * WIDE_ROWS, 128), WIDE_ROWS)
-            grad[to, :] += lax.dot_general(
-                left_ref[window_rows, :],
-                right_ref[value_rows, :],
-                (((0,), (0,)), ((), ())),
-                preferred_element_type=jnp.float32,
-            )
-            return carry
-
-        lax.fori_loop(0, 12, step_of, 0)
-
-        def cast(step, carry):
-            rows = pl.ds(pl.multiple_of(step * 128, 128), 128)
-            out[rows, :] = grad[rows, :].astype(jnp.bfloat16)
-            return carry
-
-        lax.fori_loop(0, 9, cast, 0)
-
-    def narrow(values):
-        return values.astype(jnp.bfloat16)
+    if backward:
+        depth_far(0)
 
     def spread(step, carry):
         turn = (2 - step + (step // 2) * (7 - 2 * step)) % 4
         row = (second + turn) % 4
-        for position in range(4):
-            block = block_of(core, position, row)
-            for p in range(3):
-                window[
-                    position * PIECE : (position + 1) * PIECE, p * WIDE_ROWS : (p + 1) * WIDE_ROWS
-                ] = padded[pl.ds(pl.multiple_of(block * PIECE + p * ACROSS, 16), PIECE), :]
+        fill_window(padded, row)
         result = jnp.dot(window[...], wb[...], preferred_element_type=jnp.float32)
         for position in range(4):
             reduced[position] = result[position * PIECE : (position + 1) * PIECE, :]
@@ -477,13 +525,17 @@
                 copies.remote(
                     29 + position, down_out.at[position], down_in.at[position], s_down
                 ).start()
-            if backward:
-                gradients(ef, xall, ge_ref)
-                gradients(padded, xf, gf_ref)
-
+
+        if backward:
+            fill_chunk(xf, row)
+            add_gradient()
         return carry
 
     lax.fori_loop(0, 4, spread, 0)
+    if backward:
+        hand_over(1)
+        depth_near(0)
+        depth_far(1)
     for position in range(4):
         copies.sent.append(
             copies.remote(21 + position, far_out.at[position], far_in.at[position], s_up)
@@ -534,11 +586,16 @@
             + down2_in[rows, :].astype(jnp.float32)
         )
 
+    if backward:
+        depth_near(1)
     swap_out[...] = narrow(settled(1 - core))
     copies.start(37, swap_out, swap_in, partner)
     out_ref[core] = narrow(x_ref[core].astype(jnp.float32) + settled(core))
     copies.arrived(37, swap_in, partner)
     out_ref[1 - core] = narrow(x_ref[1 - core].astype(jnp.float32) + swap_in[...].astype(jnp.float32))
+    if backward:
+        depth_own(0, ge_ref)
+        depth_own(1, gf_ref)
     copies.finish()
     for store in stores:
         store.wait()
@@ -556,7 +613,7 @@
         jax.ShapeDtypeStruct((SPOTS, PART), b16),
     ]
     out = jax.ShapeDtypeStruct((2, HALF, PART), b16)
-    grad = jax.ShapeDtypeStruct((9 * INNER, PART), b16)
+    grad = jax.ShapeDtypeStruct((9 * INNER // 2, PART // 2), f32)
     scratch = [
         pltpu.VMEM((SPOTS, PART), b16),
         pltpu.VMEM((PART, 9 * INNER), b16),
@@ -577,8 +634,8 @@
         pltpu.VMEM((PIECE, PART), b16),
         pltpu.VMEM((HALF, PART), b16),
         pltpu.VMEM((HALF, PART), b16),
-        pltpu.SemaphoreType.DMA((38,)),
-        pltpu.SemaphoreType.DMA((38,)),
+        pltpu.SemaphoreType.DMA((48,)),
+        pltpu.SemaphoreType.DMA((48,)),
         pltpu.SemaphoreType.DMA((5,)),
     ]
     if backward:
@@ -587,6 +644,10 @@
             pltpu.VMEM((padded_rows, WIDE_ROWS), b16),
             pltpu.VMEM((SPOTS, PART), b16),
             pltpu.VMEM((9 * INNER, PART), f32),
+            pltpu.VMEM((2, 2, 576, PART), b16),
+            pltpu.VMEM((2, 576, PART), b16),
+            pltpu.VMEM((2, 2, 288, 256), b16),
+            *[pltpu.VMEM((2, 576, 256), b16) for _ in range(4)],
         ]
     blocks = jnp.transpose(values.reshape(HALF, 2, PART), (1, 0, 2))
     results = pl.pallas_call(
@@ -617,12 +678,155 @@
     return jnp.where(core == 0, own, theirs), jnp.where(core == 0, theirs, own)
 
 
-def own_inner(grad, core):
-    grad = grad.reshape(9, 2, INNER // 2, PART)
-    own = lax.dynamic_index_in_dim(grad, core, axis=1, keepdims=False)
-    theirs = swap_cores(lax.dynamic_index_in_dim(grad, 1 - core, axis=1, keepdims=False))
-    low, high = jnp.where(core == 0, own, theirs), jnp.where(core == 0, theirs, own)
-    return jnp.concatenate([low, high], axis=-1)
+SUM_ROWS = 1280
+
+
+def sum_kernel(down_ref, up_ref, conv_ref, class_ref, out_ref, total, give, pair_in, a_out, a_in,
+               b_out, b_in, z_out, z_in, result, send_sems, recv_sems):
+    core, first, second = place()
+    depth = lax.axis_index("samp")
+    me = block_of(core, first, second)
+    partner = {"wide": me * 2 + 1 - core}
+    first_peers = [
+        {"wide": block_of(core, (first + d) % 4, second) * 2 + core} for d in range(4)
+    ]
+    second_peers = [
+        {"wide": block_of(core, first, (second + d) % 4) * 2 + core} for d in range(4)
+    ]
+    depth_peers = [{"samp": (depth + d) % 4} for d in range(4)]
+    copies = Copies(send_sems, recv_sems)
+    barrier = pltpu.get_barrier_semaphore()
+    for device in [partner, *first_peers[1:], *second_peers[1:], *depth_peers[1:]]:
+        pl.semaphore_signal(
+            barrier, inc=1, device_id=device, device_id_type=pl.DeviceIdType.MESH
+        )
+    pl.semaphore_wait(barrier, 10)
+
+    def own_lanes(half, width):
+        return pl.ds(pl.multiple_of(half * width, 128), width)
+
+    def pack(half, to, kind):
+        to[0:512, :] = down_ref[:, own_lanes(half, 512)].astype(kind)
+        to[512:1024, :] = up_ref[pl.ds(pl.multiple_of(half * 512, 512), 512), :].astype(kind)
+        for piece in range(4):
+            rows = pl.ds(pl.multiple_of((half * 4 + piece) * 144, 16), 144)
+            to[1024:1168, piece * 128 : (piece + 1) * 128] = conv_ref[rows, :].astype(kind)
+        to[1168:1184, :] = class_ref[:, own_lanes(half, 512)].astype(kind)
+        to[1184:, :] = jnp.zeros((SUM_ROWS - 1184, PART), kind)
+
+    def rows320(at):
+        return pl.ds(pl.multiple_of((at % 4) * 320, 64), 320)
+
+    pack(1 - core, give, jnp.bfloat16)
+    for d in range(4):
+        part = rows320(second + (d + 1))
+        copies.start(d, give.at[part, :], pair_in.at[part, :], partner)
+    pack(core, total, jnp.float32)
+    for d in range(1, 4):
+        part = rows320(first + d)
+        copies.arrived(d - 1, pair_in.at[rows320(first + d), :], partner)
+        a_out[d] = (total[part, :] + pair_in[part, :].astype(jnp.float32)).astype(jnp.bfloat16)
+        copies.start(3 + d, a_out.at[d], a_in.at[d], first_peers[d])
+    copies.arrived(3, pair_in.at[rows320(first), :], partner)
+    for d in range(1, 4):
+        copies.arrived(3 + d, a_in.at[d], first_peers[d])
+
+    def after_first(at):
+        base = first * 320 + at * 80
+        rows = pl.ds(pl.multiple_of(base, 16), 80)
+        inner = pl.ds(pl.multiple_of(at * 80, 16), 80)
+        value = total[rows, :] + pair_in[rows, :].astype(jnp.float32)
+        for d in range(1, 4):
+            value = value + a_in[d, inner, :].astype(jnp.float32)
+        return value
+
+    for d in range(1, 4):
+        b_out[d] = after_first((second + d) % 4).astype(jnp.bfloat16)
+        copies.start(6 + d, b_out.at[d], b_in.at[d], second_peers[d])
+    total[0:80, :] = after_first(second)
+    for d in range(1, 4):
+        copies.arrived(6 + d, b_in.at[d], second_peers[d])
+        total[0:80, :] += b_in[d].astype(jnp.float32)
+    for d in range(1, 4):
+        z_out[d] = total[0:80, own_lanes((depth + d) % 4, 128)].astype(jnp.bfloat16)
+        copies.start(9 + d, z_out.at[d], z_in.at[d], depth_peers[d])
+    value = total[0:80, own_lanes(depth, 128)]
+    for d in range(1, 4):
+        copies.arrived(9 + d, z_in.at[d], depth_peers[d])
+        value = value + z_in[d].astype(jnp.float32)
+
+    def at_depth(d):
+        base = first * 320 + second * 80
+        return result.at[
+            core, pl.ds(pl.multiple_of(base, 16), 80), own_lanes((depth + d) % 4, 128)
+        ]
+
+    def at_second(d):
+        base = first * 320 + ((second + d) % 4) * 80
+        return result.at[core, pl.ds(pl.multiple_of(base, 16), 80), :]
+
+    def at_first(d, half):
+        return result.at[half, rows320(first + d), :]
+
+    at_depth(0)[...] = value.astype(jnp.bfloat16)
+    for d in range(1, 4):
+        copies.start(12 + d, at_depth(0), at_depth(0), depth_peers[d])
+    for d in range(1, 4):
+        copies.arrived(12 + d, at_depth(4 - d), depth_peers[d])
+    for d in range(1, 4):
+        copies.start(15 + d, at_second(0), at_second(0), second_peers[d])
+    for d in range(1, 4):
+        copies.arrived(15 + d, at_second(4 - d), second_peers[d])
+    for d in range(1, 4):
+        copies.start(18 + d, at_first(0, core), at_first(0, core), first_peers[d])
+    copies.start(22, at_first(0, core), at_first(0, core), partner)
+    for d in range(1, 4):
+        copies.arrived(18 + d, at_first(4 - d, core), first_peers[d])
+        copies.start(22 + d, at_first(4 - d, core), at_first(4 - d, core), partner)
+    out_ref[core] = result[core]
+    copies.arrived(22, at_first(0, 1 - core), partner)
+    for d in range(1, 4):
+        copies.arrived(22 + d, at_first(4 - d, 1 - core), partner)
+    out_ref[1 - core] = result[1 - core]
+    copies.finish()
+
+
+def sum_everywhere(conv_grad, down_grad, up_grad, class_grad):
+    b16, f32 = jnp.bfloat16, jnp.float32
+    vmem = pl.BlockSpec(memory_space=pltpu.VMEM)
+    classes = class_grad.shape[1]
+    small = jnp.pad(class_grad.T, ((0, 16 - classes), (0, 2 * PART - INNER)))
+    out = pl.pallas_call(
+        sum_kernel,
+        out_shape=jax.ShapeDtypeStruct((2, SUM_ROWS, PART), b16),
+        in_specs=[vmem] * 4,
+        out_specs=vmem,
+        scratch_shapes=[
+            pltpu.VMEM((SUM_ROWS, PART), f32),
+            pltpu.VMEM((SUM_ROWS, PART), b16),
+            pltpu.VMEM((SUM_ROWS, PART), b16),
+            pltpu.VMEM((4, 320, PART), b16),
+            pltpu.VMEM((4, 320, PART), b16),
+            pltpu.VMEM((4, 80, PART), b16),
+            pltpu.VMEM((4, 80, PART), b16),
+            pltpu.VMEM((4, 80, 128), b16),
+            pltpu.VMEM((4, 80, 128), b16),
+            pltpu.VMEM((2, SUM_ROWS, PART), b16),
+            pltpu.SemaphoreType.DMA((26,)),
+            pltpu.SemaphoreType.DMA((26,)),
+        ],
+        compiler_params=pltpu.CompilerParams(
+            collective_id=3, has_side_effects=True, vmem_limit_bytes=60 * 1024 * 1024
+        ),
+        name="sum_everywhere",
+    )(down_grad, up_grad, conv_grad.reshape(9 * INNER, INNER), small)
+    down = jnp.concatenate([out[0, 0:512], out[1, 0:512]], axis=1).astype(f32)
+    up = out[:, 512:1024].astype(f32).reshape(2 * PART, PART)
+    conv = jnp.concatenate(
+        [out[h, 1024:1168, i * 128 : (i + 1) * 128] for h in range(2) for i in range(4)], axis=0
+    )
+    conv = conv.astype(f32).reshape(conv_grad.shape)
+    return conv, down, up, out[0, 1168 : 1168 + classes, 0:INNER].astype(f32).T
 
 
 def local(
@@ -691,13 +895,12 @@
     hidden_sum = from_depth(down_back) + upward_grad.astype(jnp.float32)
     hidden_grad = (hidden_sum * silu_slope(hidden_pre)).astype(jnp.bfloat16)
     conv_grad = correlate(padded_in, hidden_grad)
-    conv_grad, down_grad, up_grad, class_grad = lax.psum(
-        (conv_grad, down_grad, up_grad, class_grad), ("wide", "samp")
-    )
-    reduce_grad = sum_at_owner(own_inner(reduce_grad, core), "samp", 2)
-    expand_grad = sum_at_owner(own_inner(expand_grad, core)[::-1], "samp", 2)
+    conv_grad, down_grad, up_grad, class_grad = sum_everywhere(
+        conv_grad, down_grad, up_grad, class_grad
+    )
     reduce_grad = reduce_grad.reshape(3, 3, INNER // 2, -1)
-    expand_grad = jnp.transpose(expand_grad, (0, 2, 1)).reshape(3, 3, -1, INNER // 2)
+    expand_grad = jnp.transpose(expand_grad.reshape(9, INNER // 2, -1)[::-1], (0, 2, 1))
+    expand_grad = expand_grad.reshape(3, 3, -1, INNER // 2)
     return (conv_grad, down_grad, expand_grad, reduce_grad, up_grad, class_grad)
 
 

time: 377 us -> 254 us (0.67)
  blocking collectives: 73.1 us -> 0 us
  waiting for transfers between devices: 67.8 us -> 0.01 us
  Pallas kernels: 138 us -> 197 us
  local copies, waits for them, and re-layouts: 45.3 us -> 25 us
  between operations: 14.5 us -> 1.13 us
  starting transfers between devices: 15.8 us -> 6.52 us
    psum x1 -> x0, blocking collectives: 73.1 us -> none  [local(): lax.psum((conv_grad, down_grad, up_grad, class_grad), ('wide', 'samp'))]
    pallas_call x0 -> x1, Pallas kernels: none -> 52.5 us  [sum_everywhere(): pl.pallas_call(sum_kernel, out_shape=jax.ShapeDtypeStruct((2, SUM_ROWS, P...]
    psum x1 -> x0, waiting for transfers between devices: 51.7 us -> none  [local(): lax.psum((conv_grad, down_grad, up_grad, class_grad), ('wide', 'samp'))]
    all_to_all x2 -> x0, waiting for transfers between devices: 15.1 us -> none  [sum_at_owner(): pieces = lax.all_to_all(split_up(x, dim, length), axis, 0, 0, tiled=True)]
    unnamed x69 -> x58, local copies, waits for them, and re-layouts: 17.6 us -> 3.56 us
    all_to_all x2 -> x0, starting transfers between devices: 8.7 us -> none  [sum_at_owner(): pieces = lax.all_to_all(split_up(x, dim, length), axis, 0, 0, tiled=True)]
    pallas_call x2, Pallas kernels: 138 us -> 144 us  [bottleneck(): pl.pallas_call(functools.partial(phase_kernel, backward), out_shape=[out,...]
  transfers between devices with their start and end apart: 9 -> 4, of which waited for: 3 -> 0; matrix products, arithmetic and copies ran while one was open for 11% -> 4% of each run, Pallas kernels for 0% -> 0%
where the time goes in v2:
time: 254 us; the launch traced here: 252 us
  Pallas kernels  197 us (78%)
  local copies, waits for them, and re-layouts  25 us (10%)
  matrix products  13.3 us (5%)
  other arithmetic  9.63 us (4%)
  starting transfers between devices  6.52 us (3%)
    pallas_call x2, Pallas kernels, bottleneck(): pl.pallas_call(functools.partial(phase_kernel, backward), out_shape=[out,...  144 us
    pallas_call x1, Pallas kernels, sum_everywhere(): pl.pallas_call(sum_kernel, out_shape=jax.ShapeDtypeStruct((2, SUM_ROWS, P...  52.5 us
  transfers between devices with their start and end apart: 4, of which 0 were waited for; matrix products, arithmetic and copies ran while one was open for 4% of the time, Pallas kernels for 0%

profile of v2, /device:TPU:1, one launch (start us, length us, event | category | flops | bytes accessed | tf_op | source)
XLA Modules:
  0.0 252.3 jit_solution(11873248858688415958)
XLA Ops:
  0.6 0.0 copy-start
  0.6 0.0 copy-start.4
  0.7 0.0 copy-start.5
  0.7 1.3 constant_dynamic-slice_fusion.1
  2.0 1.5 collective-permute-start.2
  3.5 0.8 slice_bitcast_fusion.3
  4.2 3.1 %collective-permute-start = (bf16[1,96,128]{2,1,0:T(8,128)(2,1)S(1)}, bf16[1,96,128]{2,1,0:T(8,128)(2,1)S(1)}, u32[]{:S(2)}, u32[]{:S(2)}) collective-permute-start(bf16[1,96,128]{2,1,0:T(8,128)(2,1)S(1)} %get-tuple-element.26), channel_id=1, source_target_pairs={{0,4},{4,8},{8,12},{12,16},{16,20},{20,24},{24,28},{28,32},{32,36}... | collective-permute-start | bytes 73736 | tf_op jit(solution)/shard_map/ppermute | solution.py:28
  7.3 1.9 collective-permute-start.1
  9.2 1.9 constant_dynamic-slice_fusion
  11.2 1.4 copy.38
  12.5 0.1 fusion.15
  13.0 0.0 copy-start.6
  13.0 1.1 multiply_convert_fusion.2
  14.1 0.1 copy.48
  14.3 0.4 copy-done.13
  14.7 0.3 convolution_convert_fusion.1
  15.0 0.1 reshape_reshape.19
  15.2 0.7 copy.46
  15.9 1.3 broadcast_select_fusion.3
  17.2 0.0 copy-start.7
  17.2 0.1 pad_maximum_fusion
  17.3 1.4 copy.25.refs_1_
  18.7 1.3 broadcast_select_fusion.1
  20.1 1.1 pad_maximum_fusion.1
  21.1 66.6 %forward_phase.1 = (bf16[2,96,512]{2,1,0:T(8,128)(2,1)}, f32[3072,128]{1,0:T(8,128)}, bf16[3168,384]{1,0:T(8,128)(2,1)}, bf16[3072,512]{1,0:T(8,128)(2,1)}) custom-call(bf16[2,96,512]{2,1,0:T(8,128)(2,1)} %bitcast.144, bf16[512,1152]{1,0:T(8,128)(2,1)} %copy.25.refs_1_, bf16[1152,512]{1,0:T(8,128)(2,1)} %bitcast.127), custom_call_target="tpu_custom_call" | custom-call | tf_op jit(solution)/shard_map/forward_phase/pallas_call | solution.py:653
  87.8 0.0 copy-start.18
  87.8 0.0 copy-start.20
  87.8 1.8 copy.26
  89.6 1.8 reshape.112
  91.4 1.8 convolution_bitcast_fusion.2
  93.2 0.1 copy.28
  93.3 0.0 copy-start.10
  93.4 0.7 copy-done.10
  94.0 1.0 multiply_convert_fusion.1
  95.0 0.6 copy-done.14
  95.6 0.2 convolution_exponential_fusion
  95.8 1.1 convolution_bitcast_fusion.3
  96.9 1.9 fusion.1
  98.8 1.1 rev.9
  99.9 1.1 rev.10
  101.1 1.0 copy.47
  102.1 1.7 convolution_convert_fusion
  103.8 0.1 reshape_reshape.21
  104.0 0.7 copy.45
  104.7 1.4 copy.31.refs_1_
  106.1 77.6 %backward_phase.1 = (bf16[2,96,512]{2,1,0:T(8,128)(2,1)}, f32[576,256]{1,0:T(8,128)}, f32[576,256]{1,0:T(8,128)}) custom-call(bf16[2,96,512]{2,1,0:T(8,128)(2,1)} %bitcast.153, bf16[512,1152]{1,0:T(8,128)(2,1)} %copy.31.refs_1_, bf16[1152,512]{1,0:T(8,128)(2,1)} %bitcast.130, f32[3072,128]{1,0:T(8,128)} %get-tuple-element.14.refs_3_, ...), custom_call_target="tpu_custom_call" | custom-call | tf_op jit(solution)/shard_map/backward_phase/pallas_call | solution.py:653
  183.6 0.0 copy-start.15
  183.7 1.2 copy.32
  184.9 0.1 reshape.116
  185.1 0.5 convolution_bitcast_fusion.1
  185.5 0.1 copy.35
  185.7 0.6 pad.9.class_ref
  186.3 1.3 convolution_bitcast_fusion.conv_ref
  187.6 1.8 fusion.33.up_ref
  189.4 1.8 fusion.32.down_ref
  191.2 52.5 %sum_everywhere.1 = bf16[2,1280,512]{2,1,0:T(8,128)(2,1)} custom-call(f32[512,1024]{1,0:T(8,128)} %fusion.32.down_ref, f32[1024,512]{1,0:T(8,128)} %fusion.33.up_ref, f32[1152,128]{1,0:T(8,128)} %convolution_bitcast_fusion.conv_ref, f32[16,1024]{1,0:T(8,128)} %pad.9.class_ref), custom_call_target="tpu_custom_call" | custom-call | tf_op jit(solution)/shard_map/sum_everywhere/pallas_call | solution.py:799
  243.7 1.4 slice_bitcast_fusion.1
  245.1 0.6 copy-done.2
  245.7 0.6 convert_bitcast_fusion
  246.3 1.7 bitcast_convert_fusion
  248.2 0.9 convert.4
  249.0 0.9 rev.11
  249.9 1.6 maximum_convert_fusion
  251.5 0.8 copy.65
  (61 shorter events, 0.7 us)
Async XLA Ops:
  0.6 14.1 %copy-start = (bf16[512,1024]{1,0:T(8,128)(2,1)S(1)}, bf16[512,1024]{1,0:T(8,128)(2,1)}, u32[]{:S(2)}) copy-start(bf16[512,1024]{1,0:T(8,128)(2,1)} %param.11) | copy-start | bytes 3145732
  0.6 10.5 %copy-start.4 = (bf16[1024,512]{1,0:T(8,128)(2,1)S(1)}, bf16[1024,512]{1,0:T(8,128)(2,1)}, u32[]{:S(2)}) copy-start(bf16[1024,512]{1,0:T(8,128)(2,1)} %param.14) | copy-start | bytes 3145732
  0.7 11.9 %copy-start.5 = (bf16[1,4,96,128]{3,2,1,0:T(8,128)(2,1)S(1)}, bf16[1,4,96,128]{3,2,1,0:T(8,128)(2,1)}, u32[]{:S(2)}) copy-start(bf16[1,4,96,128]{3,2,1,0:T(8,128)(2,1)} %param.8) | copy-start | bytes 294916
  2.0 13.9 %collective-permute-start.2 = (bf16[9,512,64]{1,2,0:T(8,128)(2,1)S(1)}, bf16[9,512,64]{1,2,0:T(8,128)(2,1)}, u32[]{:S(2)}, u32[]{:S(2)}) collective-permute-start(bf16[9,512,64]{1,2,0:T(8,128)(2,1)S(1)} %constant_dynamic-slice_fusion.1), channel_id=1, source_target_pairs={{0,4},{4,0},{8,12},{12,8},{16,20},{20,16},{24,28},{28,24},{32,36},... | collective-permute-start | bytes 1769480 | tf_op jit(solution)/shard_map/ppermute | solution.py:672
  4.2 8.3 %collective-permute-start = (bf16[1,96,128]{2,1,0:T(8,128)(2,1)S(1)}, bf16[1,96,128]{2,1,0:T(8,128)(2,1)S(1)}, u32[]{:S(2)}, u32[]{:S(2)}) collective-permute-start(bf16[1,96,128]{2,1,0:T(8,128)(2,1)S(1)} %get-tuple-element.26), channel_id=1, source_target_pairs={{0,4},{4,8},{8,12},{12,16},{16,20},{20,24},{24,28},{28,32},{32,36}... | collective-permute-start | bytes 73736 | tf_op jit(solution)/shard_map/ppermute | solution.py:28
  7.3 5.2 %collective-permute-start.1 = (bf16[1,96,128]{2,1,0:T(8,128)(2,1)S(1)}, bf16[1,96,128]{2,1,0:T(8,128)(2,1)S(1)}, u32[]{:S(2)}, u32[]{:S(2)}) collective-permute-start(bf16[1,96,128]{2,1,0:T(8,128)(2,1)S(1)} %get-tuple-element.27), channel_id=1, source_target_pairs={{4,0},{8,4},{12,8},{16,12},{20,16},{24,20},{28,24},{32,28},{36,32}... | collective-permute-start | bytes 73736 | tf_op jit(solution)/shard_map/ppermute | solution.py:31
  11.2 7.5 %collective-permute-start.3 = (bf16[9,64,512]{2,1,0:T(8,128)(2,1)}, bf16[9,64,512]{2,1,0:T(8,128)(2,1)}, u32[]{:S(2)}, u32[]{:S(2)}) collective-permute-start(bf16[9,64,512]{2,1,0:T(8,128)(2,1)} %constant_dynamic-slice_fusion), channel_id=1, source_target_pairs={{0,4},{4,0},{8,12},{12,8},{16,20},{20,16},{24,28},{28,24},{32,36},... | collective-permute-start | bytes 1769480 | tf_op jit(solution)/shard_map/ppermute | solution.py:672
  11.2 1.8 copy-start.19
  12.9 1.2 copy-start.16
  13.0 2.9 %copy-start.6 = (bf16[3,3,1024,64]{2,3,1,0:T(8,128)(2,1)S(1)}, bf16[3,3,1024,64]{2,3,1,0:T(8,128)(2,1)}, u32[]{:S(2)}) copy-start(bf16[3,3,1024,64]{2,3,1,0:T(8,128)(2,1)} %param.12) | copy-start | bytes 3538948
  14.1 0.6 copy-start.13
  17.2 1.5 copy-start.7
  87.8 7.9 %copy-start.18 = (bf16[128,9]{0,1:T(8,128)(2,1)S(1)}, bf16[128,9]{0,1:T(8,128)(2,1)}, u32[]{:S(2)}) copy-start(bf16[128,9]{0,1:T(8,128)(2,1)} %param.15) | copy-start | bytes 6916
  87.8 8.0 %copy-start.20 = (s32[1,4,96]{2,1,0:T(4,128)S(1)}, s32[1,4,96]{2,1,0:T(4,128)}, u32[]{:S(2)}) copy-start(s32[1,4,96]{2,1,0:T(4,128)} %param.9) | copy-start | bytes 4612
  89.6 9.2 %copy-start.1 = (bf16[9,128,512]{2,1,0:T(8,128)(2,1)S(1)}, bf16[9,128,512]{2,1,0:T(8,128)(2,1)}, u32[]{:S(2)}) copy-start(bf16[9,128,512]{2,1,0:T(8,128)(2,1)} %pad_maximum_fusion.1) | copy-start | bytes 3538948
  93.3 0.7 copy-start.10
  95.0 0.6 copy-start.14
  99.9 4.7 %copy-start.3 = (bf16[9,128,512]{2,1,0:T(8,128)(2,1)S(1)}, bf16[9,128,512]{2,1,0:T(8,128)(2,1)}, u32[]{:S(2)}) copy-start(bf16[9,128,512]{2,1,0:T(8,128)(2,1)} %rev.9) | copy-start | bytes 3538948
  183.6 2.0 copy-start.8
  183.6 2.0 copy-start.9
  183.6 2.7 %copy-start.15 = (bf16[4,96,128]{2,1,0:T(8,128)(2,1)S(1)}, bf16[4,96,128]{2,1,0:T(8,128)(2,1)}, u32[]{:S(2)}) copy-start(bf16[4,96,128]{2,1,0:T(8,128)(2,1)} %fusion.1) | copy-start | bytes 294916
  183.7 2.7 %copy-start.17 = (bf16[4,96,1152]{2,1,0:T(8,128)(2,1)S(1)}, bf16[4,96,1152]{2,1,0:T(8,128)(2,1)}, u32[]{:S(2)}) copy-start(bf16[4,96,1152]{2,1,0:T(8,128)(2,1)} %copy-done.16) | copy-start | bytes 2654212
  183.7 2.7 %copy-start.21 = (f32[4,96,128]{2,1,0:T(8,128)S(1)}, f32[4,96,128]{2,1,0:T(8,128)}, u32[]{:S(2)}) copy-start(f32[4,96,128]{2,1,0:T(8,128)} %get-tuple-element.29) | copy-start | bytes 589828
  243.7 2.1 copy-start.2
  243.7 2.7 %slice-start = ((bf16[2,1280,512]{2,1,0:T(8,128)(2,1)}), bf16[2,512,512]{2,1,0:T(8,128)(2,1)S(1)}, s32[]{:S(2)}) async-start(bf16[2,1280,512]{2,1,0:T(8,128)(2,1)} %sum_everywhere.1), calls=%async_computation | async-start | bytes 2097152 | tf_op jit(solution)/shard_map/slice | solution.py:824
  246.3 2.7 %copy-start.12 = (f32[576,256]{1,0:T(8,128)S(1)}, f32[576,256]{1,0:T(8,128)}, u32[]{:S(2)}) copy-start(f32[576,256]{1,0:T(8,128)} %get-tuple-element.18) | copy-start | bytes 1769476
  249.0 2.5 copy-start.11

commit v3 on v2

--- a/solution.py
+++ b/solution.py
@@ -370,48 +370,57 @@
     padded[0:ACROSS, :] = jnp.zeros((ACROSS, WIDE_ROWS), jnp.bfloat16)
     padded[SPOTS + ACROSS :, :] = jnp.zeros((ACROSS, WIDE_ROWS), jnp.bfloat16)
 
+    offsets = (0, 3, 1, 2)
+
+    def relay(order):
+        first_at = first + offsets[order]
+        here = piece(first_at, second + 3)
+        copies.arrived(5 + order, here, s_up)
+        low = piece(first_at, second + 3, 0, HALF)
+        copies.start(13 + order, low, low, s_up)
+        here = piece(first_at, second + 1)
+        copies.arrived(9 + order, here, s_down)
+        high = piece(first_at, second + 1, HALF, HALF)
+        copies.start(48 + order, high, high, s_down)
+
     left = piece(first + 3, second)
     right = piece(first + 1, second)
     copies.arrived(1, left, f_up)
     low = piece(first + 3, second, 0, HALF)
     copies.start(3, low, low, f_up)
+    send_second(1, first + 3)
     copies.arrived(2, right, f_down)
     high = piece(first + 1, second, HALF, HALF)
     copies.start(4, high, high, f_down)
-    send_second(1, first + 3)
     send_second(2, first + 1)
+    relay(0)
     copies.arrived(3, piece(first + 2, second, 0, HALF), f_up)
     copies.arrived(4, piece(first + 2, second, HALF, HALF), f_down)
     send_second(3, first + 2)
     for load in loads:
         load.wait()
 
-    offsets = (0, 3, 1, 2)
-
     def product(step, carry):
+        turn = (3 * step + (step // 2) * (7 - 2 * step)) % 4
+
         @pl.when(step == 1)
         def _():
-            for order in range(4):
-                here = piece(first + offsets[order], second + 3)
-                copies.arrived(5 + order, here, s_up)
-                if order < 2:
-                    copies.remote(13 + order, here, here, s_up).start()
-
-        @pl.when(step == 2)
-        def _():
-            for order in range(4):
-                here = piece(first + offsets[order], second + 1)
-                copies.arrived(9 + order, here, s_down)
-                if order >= 2:
-                    copies.remote(13 + order, here, here, s_down).start()
+            for order in (1, 2, 3):
+                first_at = first + offsets[order]
+                copies.arrived(5 + order, piece(first_at, second + 3), s_up)
+                low = piece(first_at, second + 3, 0, HALF)
+                copies.remote(13 + order, low, low, s_up).start()
+                copies.arrived(9 + order, piece(first_at, second + 1), s_down)
+                high = piece(first_at, second + 1, HALF, HALF)
+                copies.remote(48 + order, high, high, s_down).start()
 
         @pl.when(step == 3)
         def _():
             for order in range(4):
-                here = piece(first + offsets[order], second + 2)
-                copies.arrived(13 + order, here, s_up)
-
-        turn = (3 * step + (step // 2) * (7 - 2 * step)) % 4
+                first_at = first + offsets[order]
+                copies.arrived(13 + order, piece(first_at, second + 2, 0, HALF), s_up)
+                copies.arrived(48 + order, piece(first_at, second + 2, HALF, HALF), s_down)
+
         row = (second + turn) % 4
         fill_chunk(xall, row)
         result = jnp.dot(chunk[...], wa[...], preferred_element_type=jnp.float32)
@@ -422,15 +431,21 @@
                 total[where, :] += result[
                     position * PIECE : (position + 1) * PIECE, p * WIDE_ROWS : (p + 1) * WIDE_ROWS
                 ]
+
         if backward:
-            fill_window(ef, row)
-            add_gradient()
+
+            @pl.when(step < 3)
+            def _():
+                fill_window(ef, row)
+                add_gradient()
+
         return carry
 
     lax.fori_loop(0, 4, product, 0)
-    for order in range(4):
-        here = piece(first + offsets[order], second + (3 if order < 2 else 1))
+    for order in (1, 2, 3):
+        here = piece(first, second, 0, HALF)
         copies.sent.append(copies.remote(13 + order, here, here, s_up))
+        copies.sent.append(copies.remote(48 + order, here, here, s_down))
 
     at_left, at_right = edge_masks(PIECE)
 
@@ -450,6 +465,8 @@
         copies.start(17 + quarter, pre.at[rows, :], other.at[rows, :], partner)
 
     if backward:
+        fill_window(ef, (second + 2) % 4)
+        add_gradient()
         hand_over(0)
         lax.fori_loop(0, 9, clear_grad, 0)
 
@@ -485,109 +502,122 @@
     if backward:
         depth_far(0)
 
+    def place_of(order):
+        return (first + (2, 1, 3, 0)[order]) % 4
+
     def spread(step, carry):
         turn = (2 - step + (step // 2) * (7 - 2 * step)) % 4
         row = (second + turn) % 4
         fill_window(padded, row)
         result = jnp.dot(window[...], wb[...], preferred_element_type=jnp.float32)
         for position in range(4):
-            reduced[position] = result[position * PIECE : (position + 1) * PIECE, :]
+            reduced[step, position] = result[position * PIECE : (position + 1) * PIECE, :]
 
         @pl.when(step == 0)
         def _():
-            for position in range(4):
-                far_out[position] = narrow(reduced[position])
+            for order in range(4):
+                far_out[order] = narrow(reduced[0, place_of(order)])
+                low = pl.ds(0, HALF)
                 copies.remote(
-                    21 + position,
-                    far_out.at[position],
-                    far_in.at[position],
-                    s_up if position < 2 else s_down,
+                    21 + order, far_out.at[order, low, :], far_in.at[order, low, :], s_up
                 ).start()
-
-        @pl.when(step == 1)
-        def _():
-            for position in (2, 3, 0, 1):
-                value = reduced[position]
-                if position < 2:
-                    copies.arrived(21 + position, far_in.at[position], s_up)
-                    value = value + far_in[position].astype(jnp.float32)
-                up_out[position] = narrow(value)
-                copies.remote(25 + position, up_out.at[position], up_in.at[position], s_up).start()
+                high = pl.ds(HALF, HALF)
+                copies.remote(
+                    33 + order, far_out.at[order, high, :], far_in.at[order, high, :], s_down
+                ).start()
 
         @pl.when(step == 2)
         def _():
-            for position in (0, 1, 2, 3):
-                value = reduced[position]
-                if position >= 2:
-                    copies.arrived(21 + position, far_in.at[position], s_down)
-                    value = value + far_in[position].astype(jnp.float32)
-                down_out[position] = narrow(value)
-                copies.remote(
-                    29 + position, down_out.at[position], down_in.at[position], s_down
-                ).start()
+            for order in range(4):
+                at = place_of(order)
+                low = pl.ds(0, HALF)
+                high = pl.ds(HALF, HALF)
+                up_out[order, high, :] = narrow(reduced[1, at, high, :])
+                down_out[order, low, :] = narrow(reduced[2, at, low, :])
+                copies.arrived(21 + order, far_in.at[order, low, :], s_up)
+                up_out[order, low, :] = narrow(
+                    reduced[1, at, low, :] + far_in[order, low, :].astype(jnp.float32)
+                )
+                copies.remote(25 + order, up_out.at[order], up_in.at[order], s_up).start()
+                copies.arrived(33 + order, far_in.at[order, high, :], s_down)
+                down_out[order, high, :] = narrow(
+                    reduced[2, at, high, :] + far_in[order, high, :].astype(jnp.float32)
+                )
+                copies.remote(29 + order, down_out.at[order], down_in.at[order], s_down).start()
 
         if backward:
-            fill_chunk(xf, row)
-            add_gradient()
+
+            @pl.when(step >= 2)
+            def _():
+                fill_chunk(xf, row)
+                add_gradient()
+
+            @pl.when(step == 3)
+            def _():
+                for turn in (2, 1):
+                    fill_window(padded, (second + turn) % 4)
+                    fill_chunk(xf, (second + turn) % 4)
+                    add_gradient()
+
         return carry
 
     lax.fori_loop(0, 4, spread, 0)
+    for order in range(4):
+        low = pl.ds(0, HALF)
+        half = far_out.at[order, low, :]
+        copies.sent.append(copies.remote(21 + order, half, half, s_up))
+        copies.sent.append(copies.remote(33 + order, half, half, s_down))
+        copies.sent.append(copies.remote(25 + order, up_out.at[order], up_in.at[order], s_up))
+        copies.sent.append(copies.remote(29 + order, down_out.at[order], down_in.at[order], s_down))
     if backward:
         hand_over(1)
         depth_near(0)
-        depth_far(1)
-    for position in range(4):
-        copies.sent.append(
-            copies.remote(21 + position, far_out.at[position], far_in.at[position], s_up)
-        )
-        copies.sent.append(
-            copies.remote(25 + position, up_out.at[position], up_in.at[position], s_up)
-        )
-        copies.sent.append(
-            copies.remote(29 + position, down_out.at[position], down_in.at[position], s_down)
-        )
-    for position in range(4):
-        copies.arrived(25 + position, up_in.at[position], s_up)
-        copies.arrived(29 + position, down_in.at[position], s_down)
-
-    def gathered(at, low, length):
+
+    def arrive_second(order):
+        copies.arrived(25 + order, up_in.at[order], s_up)
+        copies.arrived(29 + order, down_in.at[order], s_down)
+
+    def gathered(order, low, length):
         rows = pl.ds(low, length)
         return (
-            reduced[at, rows, :]
-            + up_in[at, rows, :].astype(jnp.float32)
-            + down_in[at, rows, :].astype(jnp.float32)
-        )
-
-    opposite = (first + 2) % 4
-    far2_out[0] = narrow(gathered(opposite, 0, HALF))
-    copies.start(33, far2_out.at[0], far2_in.at[0], f_up)
-    far2_out[1] = narrow(gathered(opposite, HALF, HALF))
-    copies.start(34, far2_out.at[1], far2_in.at[1], f_down)
-    above = (first + 1) % 4
-    below = (first + 3) % 4
-    up2_out[HALF:, :] = narrow(gathered(above, HALF, HALF))
-    down2_out[:HALF, :] = narrow(gathered(below, 0, HALF))
-    copies.arrived(33, far2_in.at[0], f_up)
-    up2_out[:HALF, :] = narrow(gathered(above, 0, HALF) + far2_in[0].astype(jnp.float32))
-    copies.start(35, up2_out, up2_in, f_up)
-    copies.arrived(34, far2_in.at[1], f_down)
-    down2_out[HALF:, :] = narrow(gathered(below, HALF, HALF) + far2_in[1].astype(jnp.float32))
-    copies.start(36, down2_out, down2_in, f_down)
-    copies.arrived(35, up2_in, f_up)
-    copies.arrived(36, down2_in, f_down)
+            reduced[3, place_of(order), rows, :]
+            + up_in[order, rows, :].astype(jnp.float32)
+            + down_in[order, rows, :].astype(jnp.float32)
+        )
+
+    arrive_second(0)
+    far2_out[0] = narrow(gathered(0, 0, HALF))
+    copies.start(52, far2_out.at[0], far2_in.at[0], f_up)
+    far2_out[1] = narrow(gathered(0, HALF, HALF))
+    copies.start(53, far2_out.at[1], far2_in.at[1], f_down)
+    if backward:
+        depth_far(1)
+    arrive_second(1)
+    up2_out[HALF:, :] = narrow(gathered(1, HALF, HALF))
+    copies.arrived(52, far2_in.at[0], f_up)
+    up2_out[:HALF, :] = narrow(gathered(1, 0, HALF) + far2_in[0].astype(jnp.float32))
+    copies.start(54, up2_out, up2_in, f_up)
+    arrive_second(2)
+    down2_out[:HALF, :] = narrow(gathered(2, 0, HALF))
+    copies.arrived(53, far2_in.at[1], f_down)
+    down2_out[HALF:, :] = narrow(gathered(2, HALF, HALF) + far2_in[1].astype(jnp.float32))
+    copies.start(55, down2_out, down2_in, f_down)
+    if backward:
+        depth_near(1)
+    arrive_second(3)
+    copies.arrived(54, up2_in, f_up)
+    copies.arrived(55, down2_in, f_down)
 
     def settled(which):
         rows = pl.ds(pl.multiple_of(which * HALF, 32), HALF)
         return (
-            reduced[first, rows, :]
-            + up_in[first, rows, :].astype(jnp.float32)
-            + down_in[first, rows, :].astype(jnp.float32)
+            reduced[3, first, rows, :]
+            + up_in[3, rows, :].astype(jnp.float32)
+            + down_in[3, rows, :].astype(jnp.float32)
             + up2_in[rows, :].astype(jnp.float32)
             + down2_in[rows, :].astype(jnp.float32)
         )
 
-    if backward:
-        depth_near(1)
     swap_out[...] = narrow(settled(1 - core))
     copies.start(37, swap_out, swap_in, partner)
     out_ref[core] = narrow(x_ref[core].astype(jnp.float32) + settled(core))
@@ -625,7 +655,7 @@
         pltpu.VMEM((4 * PIECE, PART), b16),
         pltpu.VMEM((4 * PIECE, 9 * INNER), b16),
         *[pltpu.VMEM((4, PIECE, PART), b16) for _ in range(6)],
-        pltpu.VMEM((4, PIECE, PART), f32),
+        pltpu.VMEM((4, 4, PIECE, PART), f32),
         pltpu.VMEM((2, HALF, PART), b16),
         pltpu.VMEM((PIECE, PART), b16),
         pltpu.VMEM((PIECE, PART), b16),
@@ -634,8 +664,8 @@
         pltpu.VMEM((PIECE, PART), b16),
         pltpu.VMEM((HALF, PART), b16),
         pltpu.VMEM((HALF, PART), b16),
-        pltpu.SemaphoreType.DMA((48,)),
-        pltpu.SemaphoreType.DMA((48,)),
+        pltpu.SemaphoreType.DMA((56,)),
+        pltpu.SemaphoreType.DMA((56,)),
         pltpu.SemaphoreType.DMA((5,)),
     ]
     if backward:
@@ -714,79 +744,84 @@
         to[1168:1184, :] = class_ref[:, own_lanes(half, 512)].astype(kind)
         to[1184:, :] = jnp.zeros((SUM_ROWS - 1184, PART), kind)
 
-    def rows320(at):
-        return pl.ds(pl.multiple_of((at % 4) * 320, 64), 320)
-
+    def spot(at_first, at_second):
+        base = (at_first % 4) * 320 + (at_second % 4) * 80
+        return pl.ds(pl.multiple_of(base, 16), 80)
+
+    order = (2, 1, 3, 0)
     pack(1 - core, give, jnp.bfloat16)
-    for d in range(4):
-        part = rows320(second + (d + 1))
-        copies.start(d, give.at[part, :], pair_in.at[part, :], partner)
+    for i, ds in enumerate(order):
+        for df in range(4):
+            part = spot(second + df, first + ds)
+            copies.start(i * 4 + df, give.at[part, :], pair_in.at[part, :], partner)
     pack(core, total, jnp.float32)
-    for d in range(1, 4):
-        part = rows320(first + d)
-        copies.arrived(d - 1, pair_in.at[rows320(first + d), :], partner)
-        a_out[d] = (total[part, :] + pair_in[part, :].astype(jnp.float32)).astype(jnp.bfloat16)
-        copies.start(3 + d, a_out.at[d], a_in.at[d], first_peers[d])
-    copies.arrived(3, pair_in.at[rows320(first), :], partner)
-    for d in range(1, 4):
-        copies.arrived(3 + d, a_in.at[d], first_peers[d])
-
-    def after_first(at):
-        base = first * 320 + at * 80
-        rows = pl.ds(pl.multiple_of(base, 16), 80)
-        inner = pl.ds(pl.multiple_of(at * 80, 16), 80)
-        value = total[rows, :] + pair_in[rows, :].astype(jnp.float32)
-        for d in range(1, 4):
-            value = value + a_in[d, inner, :].astype(jnp.float32)
+    for i, ds in enumerate(order):
+        for df in range(1, 4):
+            part = spot(first + df, second + ds)
+            copies.arrived(i * 4 + df, pair_in.at[part, :], partner)
+            a_out[df, i] = (total[part, :] + pair_in[part, :].astype(jnp.float32)).astype(
+                jnp.bfloat16
+            )
+            copies.start(16 + i * 3 + df - 1, a_out.at[df, i], a_in.at[df, i], first_peers[df])
+
+    def after_first(i):
+        part = spot(first, second + order[i])
+        copies.arrived(i * 4, pair_in.at[part, :], partner)
+        value = total[part, :] + pair_in[part, :].astype(jnp.float32)
+        for df in range(1, 4):
+            copies.arrived(16 + i * 3 + df - 1, a_in.at[df, i], first_peers[df])
+            value = value + a_in[df, i].astype(jnp.float32)
         return value
 
-    for d in range(1, 4):
-        b_out[d] = after_first((second + d) % 4).astype(jnp.bfloat16)
-        copies.start(6 + d, b_out.at[d], b_in.at[d], second_peers[d])
-    total[0:80, :] = after_first(second)
-    for d in range(1, 4):
-        copies.arrived(6 + d, b_in.at[d], second_peers[d])
-        total[0:80, :] += b_in[d].astype(jnp.float32)
+    for i in range(3):
+        b_out[i] = after_first(i).astype(jnp.bfloat16)
+        copies.start(28 + i, b_out.at[i], b_in.at[i], second_peers[order[i]])
+    total[0:80, :] = after_first(3)
+    for i in range(3):
+        copies.arrived(28 + i, b_in.at[i], second_peers[order[i]])
+        total[0:80, :] += b_in[i].astype(jnp.float32)
     for d in range(1, 4):
         z_out[d] = total[0:80, own_lanes((depth + d) % 4, 128)].astype(jnp.bfloat16)
-        copies.start(9 + d, z_out.at[d], z_in.at[d], depth_peers[d])
+        copies.start(30 + d, z_out.at[d], z_in.at[d], depth_peers[d])
     value = total[0:80, own_lanes(depth, 128)]
     for d in range(1, 4):
-        copies.arrived(9 + d, z_in.at[d], depth_peers[d])
+        copies.arrived(30 + d, z_in.at[d], depth_peers[d])
         value = value + z_in[d].astype(jnp.float32)
 
     def at_depth(d):
-        base = first * 320 + second * 80
-        return result.at[
-            core, pl.ds(pl.multiple_of(base, 16), 80), own_lanes((depth + d) % 4, 128)
-        ]
-
-    def at_second(d):
-        base = first * 320 + ((second + d) % 4) * 80
-        return result.at[core, pl.ds(pl.multiple_of(base, 16), 80), :]
-
-    def at_first(d, half):
-        return result.at[half, rows320(first + d), :]
+        return result.at[core, spot(first, second), own_lanes((depth + d) % 4, 128)]
+
+    def at(df, ds, half):
+        return result.at[half, spot(first + df, second + ds), :]
+
+    def pass_on(df, ds):
+        copies.start(52 + df * 4 + ds, at(df, ds, core), at(df, ds, core), partner)
+
+    def along_first(ds):
+        for df in range(1, 4):
+            copies.start(40 + ds * 3 + df - 1, at(0, ds, core), at(0, ds, core), first_peers[df])
 
     at_depth(0)[...] = value.astype(jnp.bfloat16)
     for d in range(1, 4):
-        copies.start(12 + d, at_depth(0), at_depth(0), depth_peers[d])
+        copies.start(33 + d, at_depth(0), at_depth(0), depth_peers[d])
     for d in range(1, 4):
-        copies.arrived(12 + d, at_depth(4 - d), depth_peers[d])
-    for d in range(1, 4):
-        copies.start(15 + d, at_second(0), at_second(0), second_peers[d])
-    for d in range(1, 4):
-        copies.arrived(15 + d, at_second(4 - d), second_peers[d])
-    for d in range(1, 4):
-        copies.start(18 + d, at_first(0, core), at_first(0, core), first_peers[d])
-    copies.start(22, at_first(0, core), at_first(0, core), partner)
-    for d in range(1, 4):
-        copies.arrived(18 + d, at_first(4 - d, core), first_peers[d])
-        copies.start(22 + d, at_first(4 - d, core), at_first(4 - d, core), partner)
+        copies.arrived(33 + d, at_depth(4 - d), depth_peers[d])
+    for ds in range(1, 4):
+        copies.start(36 + ds, at(0, 0, core), at(0, 0, core), second_peers[ds])
+    along_first(0)
+    pass_on(0, 0)
+    for ds in (1, 3, 2):
+        copies.arrived(36 + ds, at(0, 4 - ds, core), second_peers[ds])
+        along_first(4 - ds)
+        pass_on(0, 4 - ds)
+    for ds in (0, 3, 1, 2):
+        for df in (1, 3, 2):
+            copies.arrived(40 + ds * 3 + df - 1, at(4 - df, ds, core), first_peers[df])
+            pass_on(4 - df, ds)
     out_ref[core] = result[core]
-    copies.arrived(22, at_first(0, 1 - core), partner)
-    for d in range(1, 4):
-        copies.arrived(22 + d, at_first(4 - d, 1 - core), partner)
+    for df in range(4):
+        for ds in range(4):
+            copies.arrived(52 + df * 4 + ds, at(df, ds, 1 - core), partner)
     out_ref[1 - core] = result[1 - core]
     copies.finish()
 
@@ -805,15 +840,15 @@
             pltpu.VMEM((SUM_ROWS, PART), f32),
             pltpu.VMEM((SUM_ROWS, PART), b16),
             pltpu.VMEM((SUM_ROWS, PART), b16),
-            pltpu.VMEM((4, 320, PART), b16),
-            pltpu.VMEM((4, 320, PART), b16),
-            pltpu.VMEM((4, 80, PART), b16),
-            pltpu.VMEM((4, 80, PART), b16),
+            pltpu.VMEM((4, 4, 80, PART), b16),
+            pltpu.VMEM((4, 4, 80, PART), b16),
+            pltpu.VMEM((3, 80, PART), b16),
+            pltpu.VMEM((3, 80, PART), b16),
             pltpu.VMEM((4, 80, 128), b16),
             pltpu.VMEM((4, 80, 128), b16),
             pltpu.VMEM((2, SUM_ROWS, PART), b16),
-            pltpu.SemaphoreType.DMA((26,)),
-            pltpu.SemaphoreType.DMA((26,)),
+            pltpu.SemaphoreType.DMA((68,)),
+            pltpu.SemaphoreType.DMA((68,)),
         ],
         compiler_params=pltpu.CompilerParams(
             collective_id=3, has_side_effects=True, vmem_limit_bytes=60 * 1024 * 1024

time: 254 us -> 228 us (0.90)
  Pallas kernels: 197 us -> 172 us
    pallas_call x2, Pallas kernels: 144 us -> 126 us  [bottleneck(): pl.pallas_call(functools.partial(phase_kernel, backward), out_shape=[out,...]
    pallas_call x1, Pallas kernels: 52.5 us -> 46.3 us  [sum_everywhere(): pl.pallas_call(sum_kernel, out_shape=jax.ShapeDtypeStruct((2, SUM_ROWS, P...]
where the time goes in v3:
time: 228 us
  Pallas kernels  172 us (75%)
  local copies, waits for them, and re-layouts  25 us (11%)
  matrix products  13.3 us (6%)
  other arithmetic  9.63 us (4%)
  starting transfers between devices  6.52 us (3%)
    pallas_call x2, Pallas kernels, bottleneck(): pl.pallas_call(functools.partial(phase_kernel, backward), out_shape=[out,...  126 us
    pallas_call x1, Pallas kernels, sum_everywhere(): pl.pallas_call(sum_kernel, out_shape=jax.ShapeDtypeStruct((2, SUM_ROWS, P...  46.3 us
    dot_general x3, matrix products, contract_rows(): lax.dot_general(left_flat, right_flat, (((0,), (0,)), ((), ())), preferre...  4.66 us
  transfers between devices with their start and end apart: 4, of which 0 were waited for; matrix products, arithmetic and copies ran while one was open for 4% of the time, Pallas kernels for 0%

profile of v3, /device:TPU:1, one launch (start us, length us, event | category | flops | bytes accessed | tf_op | source)
XLA Modules:
  0.0 227.8 jit_solution(7805739546890485839)
XLA Ops:
  0.6 0.0 copy-start
  0.6 0.0 copy-start.4
  0.7 0.0 copy-start.5
  0.7 1.3 constant_dynamic-slice_fusion.1
  2.0 1.5 collective-permute-start.2
  3.5 0.8 slice_bitcast_fusion.3
  4.2 3.1 %collective-permute-start = (bf16[1,96,128]{2,1,0:T(8,128)(2,1)S(1)}, bf16[1,96,128]{2,1,0:T(8,128)(2,1)S(1)}, u32[]{:S(2)}, u32[]{:S(2)}) collective-permute-start(bf16[1,96,128]{2,1,0:T(8,128)(2,1)S(1)} %get-tuple-element.26), channel_id=1, source_target_pairs={{0,4},{4,8},{8,12},{12,16},{16,20},{20,24},{24,28},{28,32},{32,36}... | collective-permute-start | bytes 73736 | tf_op jit(solution)/shard_map/ppermute | solution.py:28
  7.3 1.9 collective-permute-start.1
  9.2 1.9 constant_dynamic-slice_fusion
  11.2 1.4 copy.38
  12.5 0.1 fusion.15
  13.0 0.0 copy-start.6
  13.0 1.1 multiply_convert_fusion.2
  14.1 0.1 copy.48
  14.3 0.4 copy-done.13
  14.7 0.3 convolution_convert_fusion.1
  15.0 0.1 reshape_reshape.19
  15.2 0.7 copy.46
  15.9 1.3 broadcast_select_fusion.3
  17.2 0.0 copy-start.7
  17.2 0.1 pad_maximum_fusion
  17.3 1.4 copy.25.refs_1_
  18.7 1.3 broadcast_select_fusion.1
  20.1 1.1 pad_maximum_fusion.1
  21.1 55.9 %forward_phase.1 = (bf16[2,96,512]{2,1,0:T(8,128)(2,1)}, f32[3072,128]{1,0:T(8,128)}, bf16[3168,384]{1,0:T(8,128)(2,1)}, bf16[3072,512]{1,0:T(8,128)(2,1)}) custom-call(bf16[2,96,512]{2,1,0:T(8,128)(2,1)} %bitcast.144, bf16[512,1152]{1,0:T(8,128)(2,1)} %copy.25.refs_1_, bf16[1152,512]{1,0:T(8,128)(2,1)} %bitcast.127), custom_call_target="tpu_custom_call" | custom-call | tf_op jit(solution)/shard_map/forward_phase/pallas_call | solution.py:683
  77.0 0.0 copy-start.18
  77.1 0.0 copy-start.20
  77.1 1.8 copy.26
  78.9 1.8 reshape.112
  80.7 1.8 convolution_bitcast_fusion.2
  82.5 0.1 copy.28
  82.6 0.0 copy-start.10
  82.6 0.7 copy-done.10
  83.3 1.0 multiply_convert_fusion.1
  84.3 0.0 copy-start.14
  84.3 0.6 copy-done.14
  84.9 0.2 convolution_exponential_fusion
  85.1 1.1 convolution_bitcast_fusion.3
  86.2 1.9 fusion.1
  88.1 1.1 rev.9
  89.2 1.1 rev.10
  90.3 1.0 copy.47
  91.4 1.7 convolution_convert_fusion
  93.1 0.1 reshape_reshape.21
  93.2 0.7 copy.45
  93.9 1.4 copy.31.refs_1_
  95.3 70.0 %backward_phase.1 = (bf16[2,96,512]{2,1,0:T(8,128)(2,1)}, f32[576,256]{1,0:T(8,128)}, f32[576,256]{1,0:T(8,128)}) custom-call(bf16[2,96,512]{2,1,0:T(8,128)(2,1)} %bitcast.153, bf16[512,1152]{1,0:T(8,128)(2,1)} %copy.31.refs_1_, bf16[1152,512]{1,0:T(8,128)(2,1)} %bitcast.130, f32[3072,128]{1,0:T(8,128)} %get-tuple-element.14.refs_3_, ...), custom_call_target="tpu_custom_call" | custom-call | tf_op jit(solution)/shard_map/backward_phase/pallas_call | solution.py:683
  165.4 1.2 copy.32
  166.7 0.1 reshape.116
  166.8 0.5 convolution_bitcast_fusion.1
  167.3 0.1 copy.35
  167.4 0.6 pad.9.class_ref
  168.1 1.3 convolution_bitcast_fusion.conv_ref
  169.3 1.8 fusion.33.up_ref
  171.1 1.8 fusion.32.down_ref
  172.9 46.3 %sum_everywhere.1 = bf16[2,1280,512]{2,1,0:T(8,128)(2,1)} custom-call(f32[512,1024]{1,0:T(8,128)} %fusion.32.down_ref, f32[1024,512]{1,0:T(8,128)} %fusion.33.up_ref, f32[1152,128]{1,0:T(8,128)} %convolution_bitcast_fusion.conv_ref, f32[16,1024]{1,0:T(8,128)} %pad.9.class_ref), custom_call_target="tpu_custom_call" | custom-call | tf_op jit(solution)/shard_map/sum_everywhere/pallas_call | solution.py:834
  219.2 1.4 slice_bitcast_fusion.1
  220.6 0.6 copy-done.2
  221.2 0.6 convert_bitcast_fusion
  221.8 1.7 bitcast_convert_fusion
  223.6 0.9 convert.4
  224.5 0.9 rev.11
  225.4 1.6 maximum_convert_fusion
  227.0 0.8 copy.65
  (61 shorter events, 0.7 us)
Async XLA Ops:
  0.6 14.1 %copy-start = (bf16[512,1024]{1,0:T(8,128)(2,1)S(1)}, bf16[512,1024]{1,0:T(8,128)(2,1)}, u32[]{:S(2)}) copy-start(bf16[512,1024]{1,0:T(8,128)(2,1)} %param.11) | copy-start | bytes 3145732
  0.6 10.5 %copy-start.4 = (bf16[1024,512]{1,0:T(8,128)(2,1)S(1)}, bf16[1024,512]{1,0:T(8,128)(2,1)}, u32[]{:S(2)}) copy-start(bf16[1024,512]{1,0:T(8,128)(2,1)} %param.14) | copy-start | bytes 3145732
  0.7 11.9 %copy-start.5 = (bf16[1,4,96,128]{3,2,1,0:T(8,128)(2,1)S(1)}, bf16[1,4,96,128]{3,2,1,0:T(8,128)(2,1)}, u32[]{:S(2)}) copy-start(bf16[1,4,96,128]{3,2,1,0:T(8,128)(2,1)} %param.8) | copy-start | bytes 294916
  2.0 13.9 %collective-permute-start.2 = (bf16[9,512,64]{1,2,0:T(8,128)(2,1)S(1)}, bf16[9,512,64]{1,2,0:T(8,128)(2,1)}, u32[]{:S(2)}, u32[]{:S(2)}) collective-permute-start(bf16[9,512,64]{1,2,0:T(8,128)(2,1)S(1)} %constant_dynamic-slice_fusion.1), channel_id=1, source_target_pairs={{0,4},{4,0},{8,12},{12,8},{16,20},{20,16},{24,28},{28,24},{32,36},... | collective-permute-start | bytes 1769480 | tf_op jit(solution)/shard_map/ppermute | solution.py:702
  4.2 8.3 %collective-permute-start = (bf16[1,96,128]{2,1,0:T(8,128)(2,1)S(1)}, bf16[1,96,128]{2,1,0:T(8,128)(2,1)S(1)}, u32[]{:S(2)}, u32[]{:S(2)}) collective-permute-start(bf16[1,96,128]{2,1,0:T(8,128)(2,1)S(1)} %get-tuple-element.26), channel_id=1, source_target_pairs={{0,4},{4,8},{8,12},{12,16},{16,20},{20,24},{24,28},{28,32},{32,36}... | collective-permute-start | bytes 73736 | tf_op jit(solution)/shard_map/ppermute | solution.py:28
  7.3 5.2 %collective-permute-start.1 = (bf16[1,96,128]{2,1,0:T(8,128)(2,1)S(1)}, bf16[1,96,128]{2,1,0:T(8,128)(2,1)S(1)}, u32[]{:S(2)}, u32[]{:S(2)}) collective-permute-start(bf16[1,96,128]{2,1,0:T(8,128)(2,1)S(1)} %get-tuple-element.27), channel_id=1, source_target_pairs={{4,0},{8,4},{12,8},{16,12},{20,16},{24,20},{28,24},{32,28},{36,32}... | collective-permute-start | bytes 73736 | tf_op jit(solution)/shard_map/ppermute | solution.py:31
  11.2 7.5 %collective-permute-start.3 = (bf16[9,64,512]{2,1,0:T(8,128)(2,1)}, bf16[9,64,512]{2,1,0:T(8,128)(2,1)}, u32[]{:S(2)}, u32[]{:S(2)}) collective-permute-start(bf16[9,64,512]{2,1,0:T(8,128)(2,1)} %constant_dynamic-slice_fusion), channel_id=1, source_target_pairs={{0,4},{4,0},{8,12},{12,8},{16,20},{20,16},{24,28},{28,24},{32,36},... | collective-permute-start | bytes 1769480 | tf_op jit(solution)/shard_map/ppermute | solution.py:702
  11.2 1.8 copy-start.19
  12.9 1.2 copy-start.16
  13.0 2.9 %copy-start.6 = (bf16[3,3,1024,64]{2,3,1,0:T(8,128)(2,1)S(1)}, bf16[3,3,1024,64]{2,3,1,0:T(8,128)(2,1)}, u32[]{:S(2)}) copy-start(bf16[3,3,1024,64]{2,3,1,0:T(8,128)(2,1)} %param.12) | copy-start | bytes 3538948
  14.1 0.6 copy-start.13
  17.2 1.5 copy-start.7
  77.0 7.9 %copy-start.18 = (bf16[128,9]{0,1:T(8,128)(2,1)S(1)}, bf16[128,9]{0,1:T(8,128)(2,1)}, u32[]{:S(2)}) copy-start(bf16[128,9]{0,1:T(8,128)(2,1)} %param.15) | copy-start | bytes 6916
  77.1 8.0 %copy-start.20 = (s32[1,4,96]{2,1,0:T(4,128)S(1)}, s32[1,4,96]{2,1,0:T(4,128)}, u32[]{:S(2)}) copy-start(s32[1,4,96]{2,1,0:T(4,128)} %param.9) | copy-start | bytes 4612
  78.9 9.2 %copy-start.1 = (bf16[9,128,512]{2,1,0:T(8,128)(2,1)S(1)}, bf16[9,128,512]{2,1,0:T(8,128)(2,1)}, u32[]{:S(2)}) copy-start(bf16[9,128,512]{2,1,0:T(8,128)(2,1)} %pad_maximum_fusion.1) | copy-start | bytes 3538948
  82.6 0.7 copy-start.10
  84.3 0.6 copy-start.14
  89.2 4.7 %copy-start.3 = (bf16[9,128,512]{2,1,0:T(8,128)(2,1)S(1)}, bf16[9,128,512]{2,1,0:T(8,128)(2,1)}, u32[]{:S(2)}) copy-start(bf16[9,128,512]{2,1,0:T(8,128)(2,1)} %rev.9) | copy-start | bytes 3538948
  165.4 2.0 copy-start.8
  165.4 2.0 copy-start.9
  165.4 2.7 %copy-start.15 = (bf16[4,96,128]{2,1,0:T(8,128)(2,1)S(1)}, bf16[4,96,128]{2,1,0:T(8,128)(2,1)}, u32[]{:S(2)}) copy-start(bf16[4,96,128]{2,1,0:T(8,128)(2,1)} %fusion.1) | copy-start | bytes 294916
  165.4 2.7 %copy-start.17 = (bf16[4,96,1152]{2,1,0:T(8,128)(2,1)S(1)}, bf16[4,96,1152]{2,1,0:T(8,128)(2,1)}, u32[]{:S(2)}) copy-start(bf16[4,96,1152]{2,1,0:T(8,128)(2,1)} %copy-done.16) | copy-start | bytes 2654212
  165.4 2.7 %copy-start.21 = (f32[4,96,128]{2,1,0:T(8,128)S(1)}, f32[4,96,128]{2,1,0:T(8,128)}, u32[]{:S(2)}) copy-start(f32[4,96,128]{2,1,0:T(8,128)} %get-tuple-element.29) | copy-start | bytes 589828
  219.2 2.1 copy-start.2
  219.2 2.7 %slice-start = ((bf16[2,1280,512]{2,1,0:T(8,128)(2,1)}), bf16[2,512,512]{2,1,0:T(8,128)(2,1)S(1)}, s32[]{:S(2)}) async-start(bf16[2,1280,512]{2,1,0:T(8,128)(2,1)} %sum_everywhere.1), calls=%async_computation | async-start | bytes 2097152 | tf_op jit(solution)/shard_map/slice | solution.py:859
  221.8 2.7 %copy-start.12 = (f32[576,256]{1,0:T(8,128)S(1)}, f32[576,256]{1,0:T(8,128)}, u32[]{:S(2)}) copy-start(f32[576,256]{1,0:T(8,128)} %get-tuple-element.18) | copy-start | bytes 1769476
  224.5 2.5 %copy-start.11 = (f32[576,256]{1,0:T(8,128)S(1)}, f32[576,256]{1,0:T(8,128)}, u32[]{:S(2)}) copy-start(f32[576,256]{1,0:T(8,128)} %get-tuple-element.19) | copy-start | bytes 1769476

commit v4 on v3

--- a/solution.py
+++ b/solution.py
@@ -9,144 +9,9 @@
 from jax.sharding import PartitionSpec as P
 
 
-def split_up(x, dim, length):
-    before, after = (x.shape[:dim], x.shape[dim + 1 :])
-    return jnp.moveaxis(x.reshape(*before, length, -1, *after), dim, 0)
-
-
-def sum_at_owner(x, axis, dim):
-    length = lax.axis_size(axis)
-    pieces = lax.all_to_all(split_up(x, dim, length), axis, 0, 0, tiled=True)
-    return jnp.sum(pieces.astype(jnp.float32), axis=0)
-
-
-def extended(block, sides, width):
-    for axis, dim in sides:
-        count = lax.axis_size(axis)
-        forward = [(i, i + 1) for i in range(count - 1)]
-        backward = [(target, source) for source, target in forward]
-        low = lax.ppermute(
-            lax.slice_in_dim(block, block.shape[dim] - width, None, axis=dim), axis, forward
-        )
-        high = lax.ppermute(lax.slice_in_dim(block, 0, width, axis=dim), axis, backward)
-        block = jnp.concatenate([low, block, high], axis=dim)
-    return block
-
-
 def silu_slope(value):
     logistic = jax.nn.sigmoid(value)
     return logistic * (1.0 + value * (1.0 - logistic))
-
-
-def pad_both(values):
-    return jnp.pad(values, ((1, 1), (1, 1), (0, 0)))
-
-
-def to_depth(grid):
-    height, across, channels = grid.shape
-    blocks = grid.reshape(height // 2, 2, across // 2, 2, channels)
-    return jnp.transpose(blocks, (0, 2, 1, 3, 4)).reshape(height // 2, across // 2, 4 * channels)
-
-
-def from_depth(grid):
-    height, across, channels = grid.shape
-    blocks = grid.reshape(height, across, 2, 2, channels // 4)
-    return jnp.transpose(blocks, (0, 2, 1, 3, 4)).reshape(2 * height, 2 * across, channels // 4)
-
-
-def taps_in(padded, height, across):
-    return jnp.concatenate(
-        [padded[p : p + height, q : q + across] for p in range(3) for q in range(3)], axis=-1
-    )
-
-
-def taps_out(values):
-    return jnp.concatenate(
-        [jnp.pad(values, ((p, 2 - p), (q, 2 - q), (0, 0))) for p in range(3) for q in range(3)],
-        axis=-1,
-    )
-
-
-def conv_padded(padded, weight):
-    height = padded.shape[0] - 2
-    across = padded.shape[1] - 2
-    inward = weight.shape[2]
-    outward = weight.shape[3]
-    if inward <= outward:
-        window = taps_in(padded, height, across).reshape(height * across, 9 * inward)
-        result = jnp.dot(
-            window, weight.reshape(9 * inward, outward), preferred_element_type=jnp.float32
-        )
-        return result.reshape(height, across, outward)
-    flattened = padded.reshape((height + 2) * (across + 2), inward)
-    stacked = jnp.transpose(weight, (2, 0, 1, 3)).reshape(inward, 9 * outward)
-    spread_out = jnp.dot(flattened, stacked, preferred_element_type=jnp.float32).reshape(
-        height + 2, across + 2, 9, outward
-    )
-    summed = spread_out[0:height, 0:across, 0]
-    for offset in range(1, 9):
-        p = offset // 3
-        q = offset % 3
-        summed = summed + spread_out[p : p + height, q : q + across, offset]
-    return summed
-
-
-def correlate(padded, values):
-    height, across, outward = values.shape
-    inward = padded.shape[-1]
-    if inward <= outward:
-        window = taps_in(padded, height, across).reshape(height * across, 9 * inward)
-        result = lax.dot_general(
-            window,
-            values.reshape(height * across, outward),
-            (((0,), (0,)), ((), ())),
-            preferred_element_type=jnp.float32,
-        )
-        return result.reshape(3, 3, inward, outward)
-    shifted = taps_out(values).reshape((height + 2) * (across + 2), 9 * outward)
-    result = lax.dot_general(
-        padded.reshape(-1, inward),
-        shifted,
-        (((0,), (0,)), ((), ())),
-        preferred_element_type=jnp.float32,
-    )
-    return jnp.transpose(result.reshape(inward, 3, 3, outward), (1, 2, 0, 3))
-
-
-def contract_rows(left, right):
-    left_flat = left.reshape(-1, left.shape[-1])
-    right_flat = right.reshape(-1, right.shape[-1])
-    return lax.dot_general(
-        left_flat, right_flat, (((0,), (0,)), ((), ())), preferred_element_type=jnp.float32
-    )
-
-
-def flip_kernel(weight):
-    return jnp.transpose(weight[::-1, ::-1], (0, 1, 3, 2))
-
-
-def keep_rows(block_rows, first_row):
-    return block_rows
-
-
-def project_rows(values, weight):
-    return jnp.dot(values, weight, preferred_element_type=jnp.float32).astype(jnp.bfloat16)
-
-
-def widen_rows(values, weight):
-    return lax.dot_general(
-        values, weight, (((2,), (1,)), ((), ())), preferred_element_type=jnp.float32
-    ).astype(jnp.bfloat16)
-
-
-def collect(values, transform):
-    return transform(lax.all_gather(values, "wide", axis=0, tiled=True), jnp.int32(0))
-
-
-def spread_sum(term_rows, row_total):
-    return sum_at_owner(
-        term_rows(jnp.int32(0), row_total * lax.axis_size("wide")).astype(jnp.bfloat16), "wide", 0
-    )
 
 
 ROWS = 64
@@ -222,19 +87,114 @@
             copy.wait_send()
 
 
+def contract_first(left, right):
+    return lax.dot_general(left, right, (((0,), (0,)), ((), ())), preferred_element_type=jnp.float32)
+
+
+def contract_last(left, right):
+    return lax.dot_general(left, right, (((1,), (1,)), ((), ())), preferred_element_type=jnp.float32)
+
+
+def multiply(left, right):
+    return jnp.dot(left, right, preferred_element_type=jnp.float32)
+
+
+def side_by_side(tall):
+    return jnp.concatenate([tall[i * HALF : (i + 1) * HALF] for i in range(4)], axis=1)
+
+
+def stacked_up(flat):
+    return jnp.concatenate([flat[:, i * INNER : (i + 1) * INNER] for i in range(4)], axis=0)
+
+
+def first_layers(wide, copies, after, before, feature_ref, halo, columns, conv_weight_ref,
+                 down_weight_ref, taps_ref, hidden_pre_ref, stacked_ref, x_ref):
+    at_left, at_right = edge_masks(ACROSS)
+
+    def row_columns(row, even, odd):
+        to = pl.ds(row * ACROSS, ACROSS)
+        even = even.astype(jnp.float32)
+        odd = odd.astype(jnp.float32)
+        columns[0, to, :] = from_left(odd, at_left).astype(jnp.bfloat16)
+        columns[1, to, :] = even.astype(jnp.bfloat16)
+        columns[2, to, :] = odd.astype(jnp.bfloat16)
+        columns[3, to, :] = from_right(even, at_right).astype(jnp.bfloat16)
+
+    for row in range(4):
+        row_columns(row + 1, feature_ref[0, row], feature_ref[1, row])
+    copies.arrived(56, halo.at[0], after)
+    copies.arrived(57, halo.at[1], before)
+    inside = jnp.where(wide > 0, 1.0, 0.0)
+    row_columns(0, halo[0, 0].astype(jnp.float32) * inside, halo[0, 1].astype(jnp.float32) * inside)
+    inside = jnp.where(wide < 31, 1.0, 0.0)
+    row_columns(5, halo[1, 0].astype(jnp.float32) * inside, halo[1, 1].astype(jnp.float32) * inside)
+    for a in range(2):
+        for b in range(2):
+            for i in range(2):
+                for p in range(3):
+                    for q in range(3):
+                        low = (a * 2 + b) * HALF + i * ACROSS
+                        source = (a + p + 2 * i) * ACROSS
+                        tap = (p * 3 + q) * INNER
+                        taps_ref[low : low + ACROSS, tap : tap + INNER] = columns[
+                            b + q, source : source + ACROSS, :
+                        ]
+    hidden_pre = multiply(taps_ref[...], conv_weight_ref[...])
+    hidden_pre = side_by_side(hidden_pre)
+    hidden_pre_ref[...] = hidden_pre
+    stacked = jax.nn.silu(hidden_pre).astype(jnp.bfloat16)
+    stacked_ref[...] = stacked
+    for half in range(2):
+        x_ref[half] = multiply(
+            stacked, down_weight_ref[:, half * PART : (half + 1) * PART]
+        ).astype(jnp.bfloat16)
+
+
+def middle(bottom_ref, stacked_ref, label_ref, up_weight_ref, class_ref, class_back_ref,
+           x_ref, upward_grad_ref, class_grad_ref):
+    loss_scale = 8.0 / math.sqrt(49152)
+    upward = multiply(bottom_ref[0], up_weight_ref[0:PART, :]) + multiply(
+        bottom_ref[1], up_weight_ref[PART:, :]
+    )
+    joined_pre = stacked_up(upward + stacked_ref[...].astype(jnp.float32))
+    joined = jax.nn.silu(joined_pre).astype(jnp.bfloat16)
+    logits = multiply(joined, class_ref[...])
+    classes = lax.broadcasted_iota(jnp.int32, logits.shape, 1)
+    exp_logits = jnp.where(classes < 9, jnp.exp(logits), 0.0)
+    probability = exp_logits / jnp.sum(exp_logits, axis=1, keepdims=True)
+    onehot = (label_ref[...] == classes).astype(jnp.float32)
+    logit_grad = ((probability - onehot) * loss_scale).astype(jnp.bfloat16)
+    joined_grad = multiply(logit_grad, class_back_ref[...])
+    upward_grad = side_by_side((joined_grad * silu_slope(joined_pre)).astype(jnp.bfloat16))
+    upward_grad_ref[...] = upward_grad
+    for half in range(2):
+        x_ref[half] = contract_last(
+            upward_grad, up_weight_ref[half * PART : (half + 1) * PART, :]
+        ).astype(jnp.bfloat16)
+    class_grad_ref[...] = contract_first(joined, logit_grad)
+
+
 def phase_kernel(backward, *refs):
     if backward:
-        (x_ref, wa_hbm, wb_hbm, pre_hbm, ef_hbm, xf_hbm, out_ref, ge_ref, gf_ref) = refs[:9]
-        scratch = refs[9:]
+        (
+            wa_hbm, wb_hbm, pre_hbm, ef_hbm, xf_hbm, bottom_ref, stacked_ref, label_ref,
+            up_weight_ref, class_ref, class_back_ref,
+            out_ref, ge_ref, gf_ref, upward_grad_ref, class_grad_ref,
+        ) = refs[:16]
+        scratch = refs[16:]
     else:
-        (x_ref, wa_hbm, wb_hbm, out_ref, pre_hbm, ef_hbm, xf_hbm) = refs[:7]
-        scratch = refs[7:]
+        (
+            feature_ref, conv_weight_ref, down_weight_ref, expand_hbm, reduce_hbm,
+            out_ref, pre_hbm, ef_hbm, xf_hbm, wa_hbm, wb_hbm, stacked_ref, hidden_pre_ref,
+            taps_ref,
+        ) = refs[:14]
+        scratch = refs[14:]
     (
         xall, wa, wb, total, pre, other, padded, chunk, window,
         far_out, up_out, down_out, far_in, up_in, down_in, reduced,
         far2_out, up2_out, down2_out, far2_in, up2_in, down2_in, swap_out, swap_in,
-        send_sems, recv_sems, local_sems,
-    ) = scratch[:27]
+        x_ref, send_sems, recv_sems, local_sems,
+    ) = scratch[:28]
     core, first, second = place()
     me = block_of(core, first, second)
     partner = me * 2 + 1 - core
@@ -244,17 +204,30 @@
     s_down = block_of(core, first, (second + 3) % 4) * 2 + core
     copies = Copies(send_sems, recv_sems)
 
-    loads = [
-        pltpu.make_async_copy(wa_hbm, wa, local_sems.at[0]),
-        pltpu.make_async_copy(wb_hbm, wb, local_sems.at[1]),
-    ]
-    if backward:
-        pre_f, ef, xf, grad, full, give, zfar_in, zup_out, zdown_out, zup_in, zdown_in = scratch[27:]
+    if backward:
+        loads = [
+            pltpu.make_async_copy(wa_hbm, wa, local_sems.at[0]),
+            pltpu.make_async_copy(wb_hbm, wb, local_sems.at[1]),
+        ]
+        pre_f, ef, xf, grad, full, give, zfar_in, zup_out, zdown_out, zup_in, zdown_in = scratch[28:]
         loads += [
             pltpu.make_async_copy(pre_hbm, pre_f, local_sems.at[2]),
             pltpu.make_async_copy(ef_hbm, ef, local_sems.at[3]),
             pltpu.make_async_copy(xf_hbm, xf, local_sems.at[4]),
         ]
+    else:
+        expand_both, reduce_both, wa_back, wb_back, halo, columns = scratch[28:]
+        lanes = pl.ds(pl.multiple_of(core * PART, PART), PART)
+        other_lanes = pl.ds(pl.multiple_of((1 - core) * PART, PART), PART)
+        own_rows = pl.ds(pl.multiple_of(core * 64, 64), 64)
+        loads = [
+            pltpu.make_async_copy(
+                expand_hbm.at[:, lanes, :], expand_both.at[core], local_sems.at[0]
+            ),
+            pltpu.make_async_copy(
+                reduce_hbm.at[:, :, lanes], reduce_both.at[:, own_rows, :], local_sems.at[1]
+            ),
+        ]
     for load in loads:
         load.start()
 
@@ -264,12 +237,33 @@
         z_up = {"samp": (depth + 1) % 4}
         z_down = {"samp": (depth + 3) % 4}
         peers += [z_up, z_down]
+    else:
+        wide = lax.axis_index("wide")
+        after = {"wide": (wide + 1) % 32}
+        before = {"wide": (wide + 31) % 32}
+        peers += [after, before]
     barrier = pltpu.get_barrier_semaphore()
     for device in peers:
         pl.semaphore_signal(
             barrier, inc=1, device_id=device, device_id_type=pl.DeviceIdType.MESH
         )
+    if backward:
+        middle(
+            bottom_ref, stacked_ref, label_ref, up_weight_ref, class_ref, class_back_ref,
+            x_ref, upward_grad_ref, class_grad_ref,
+        )
     pl.semaphore_wait(barrier, len(peers))
+    if not backward:
+        copies.start(56, feature_ref.at[:, 3], halo.at[0], after)
+        copies.start(57, feature_ref.at[:, 0], halo.at[1], before)
+        copies.start(58, expand_hbm.at[:, other_lanes, :], expand_both.at[core], partner)
+        copies.start(
+            59, reduce_hbm.at[:, :, other_lanes], reduce_both.at[:, own_rows, :], partner
+        )
+        first_layers(
+            wide, copies, after, before, feature_ref, halo, columns, conv_weight_ref,
+            down_weight_ref, taps_ref, hidden_pre_ref, stacked_ref, x_ref,
+        )
 
     mine = pl.ds(pl.multiple_of(me * PIECE + core * HALF, 32), HALF)
     theirs = pl.ds(pl.multiple_of(me * PIECE + (1 - core) * HALF, 32), HALF)
@@ -399,6 +393,27 @@
     send_second(3, first + 2)
     for load in loads:
         load.wait()
+    if not backward:
+        copies.arrived(58, expand_both.at[1 - core], partner)
+        partner_rows = pl.ds(pl.multiple_of((1 - core) * 64, 64), 64)
+        copies.arrived(59, reduce_both.at[:, partner_rows, :], partner)
+        for tap in range(9):
+            here = slice(tap * INNER, (tap + 1) * INNER)
+            back = slice((8 - tap) * INNER, (9 - tap) * INNER)
+            block = jnp.concatenate([expand_both[0, tap], expand_both[1, tap]], axis=1)
+            wa[:, here] = block
+            wb_back[back, :] = block.T
+            block = reduce_both[tap]
+            wb[here, :] = block
+            wa_back[:, back] = block.T
+        stores = [
+            pltpu.make_async_copy(wa_back, wa_hbm, local_sems.at[0]),
+            pltpu.make_async_copy(wb_back, wb_hbm, local_sems.at[1]),
+        ]
+        for store in stores:
+            store.start()
+    else:
+        stores = []
 
     def product(step, carry):
         turn = (3 * step + (step // 2) * (7 - 2 * step)) % 4
@@ -489,15 +504,15 @@
         copies.arrived(17 + quarter, other.at[pl.ds(quarter * 768, 768), :], partner)
         lax.fori_loop(quarter * 4, quarter * 4 + 4, shape, 0)
 
-    stores = []
     if not backward:
-        stores = [
+        more = [
             pltpu.make_async_copy(other, pre_hbm, local_sems.at[2]),
             pltpu.make_async_copy(padded, ef_hbm, local_sems.at[3]),
             pltpu.make_async_copy(xall, xf_hbm, local_sems.at[4]),
         ]
-        for store in stores:
+        for store in more:
             store.start()
+        stores += more
 
     if backward:
         depth_far(0)
@@ -631,19 +646,32 @@
         store.wait()
 
 
-def bottleneck(values, wa, wb, saved=None):
-    backward = saved is not None
+def bottleneck(backward, *operands):
     b16, f32 = jnp.bfloat16, jnp.float32
     vmem = pl.BlockSpec(memory_space=pltpu.VMEM)
     anywhere = pl.BlockSpec(memory_space=pl.ANY)
     padded_rows = SPOTS + 2 * ACROSS
-    keep = [
-        jax.ShapeDtypeStruct((SPOTS, INNER), f32),
-        jax.ShapeDtypeStruct((padded_rows, WIDE_ROWS), b16),
-        jax.ShapeDtypeStruct((SPOTS, PART), b16),
-    ]
-    out = jax.ShapeDtypeStruct((2, HALF, PART), b16)
-    grad = jax.ShapeDtypeStruct((9 * INNER // 2, PART // 2), f32)
+    shape = jax.ShapeDtypeStruct
+    out = shape((2, HALF, PART), b16)
+    if backward:
+        grad = shape((9 * INNER // 2, PART // 2), f32)
+        in_specs = [anywhere] * 5 + [vmem] * 6
+        out_shape = [out, grad, grad, shape((HALF, PART), b16), shape((INNER, INNER), f32)]
+        out_specs = [vmem] * 5
+    else:
+        in_specs = [vmem] * 3 + [anywhere] * 2
+        out_shape = [
+            out,
+            shape((SPOTS, INNER), f32),
+            shape((padded_rows, WIDE_ROWS), b16),
+            shape((SPOTS, PART), b16),
+            shape((PART, 9 * INNER), b16),
+            shape((9 * INNER, PART), b16),
+            shape((HALF, PART), b16),
+            shape((HALF, PART), f32),
+            shape((4 * HALF, 9 * INNER), b16),
+        ]
+        out_specs = [vmem] + [anywhere] * 5 + [vmem] * 3
     scratch = [
         pltpu.VMEM((SPOTS, PART), b16),
         pltpu.VMEM((PART, 9 * INNER), b16),
@@ -664,8 +692,9 @@
         pltpu.VMEM((PIECE, PART), b16),
         pltpu.VMEM((HALF, PART), b16),
         pltpu.VMEM((HALF, PART), b16),
-        pltpu.SemaphoreType.DMA((56,)),
-        pltpu.SemaphoreType.DMA((56,)),
+        pltpu.VMEM((2, HALF, PART), b16),
+        pltpu.SemaphoreType.DMA((60,)),
+        pltpu.SemaphoreType.DMA((60,)),
         pltpu.SemaphoreType.DMA((5,)),
     ]
     if backward:
@@ -679,12 +708,20 @@
             pltpu.VMEM((2, 2, 288, 256), b16),
             *[pltpu.VMEM((2, 576, 256), b16) for _ in range(4)],
         ]
-    blocks = jnp.transpose(values.reshape(HALF, 2, PART), (1, 0, 2))
-    results = pl.pallas_call(
+    else:
+        scratch += [
+            pltpu.VMEM((2, 9, PART, INNER // 2), b16),
+            pltpu.VMEM((9, INNER, PART), b16),
+            pltpu.VMEM((PART, 9 * INNER), b16),
+            pltpu.VMEM((9 * INNER, PART), b16),
+            pltpu.VMEM((2, 2, ACROSS, INNER), b16),
+            pltpu.VMEM((4, 6 * ACROSS, INNER), b16),
+        ]
+    return pl.pallas_call(
         functools.partial(phase_kernel, backward),
-        out_shape=[out, grad, grad] if backward else [out, *keep],
-        in_specs=[vmem] + [anywhere] * (5 if backward else 2),
-        out_specs=[vmem] * 3 if backward else [vmem] + [anywhere] * 3,
+        out_shape=out_shape,
+        in_specs=in_specs,
+        out_specs=out_specs,
         scratch_shapes=scratch,
         compiler_params=pltpu.CompilerParams(
             collective_id=2 if backward else 1,
@@ -692,27 +729,15 @@
             vmem_limit_bytes=60 * 1024 * 1024,
         ),
         name="backward_phase" if backward else "forward_phase",
-    )(blocks, wa, wb, *(saved or ()))
-    total = jnp.transpose(results[0], (1, 0, 2)).reshape(HALF, 2 * PART)
-    return total, results[1:]
-
-
-def swap_cores(values):
-    count = lax.axis_size("wide")
-    return lax.ppermute(values, "wide", [(i, i ^ 1) for i in range(count)])
-
-
-def pair_part(values, dim, core):
-    own = lax.dynamic_slice_in_dim(values, core * PART, PART, axis=dim)
-    theirs = swap_cores(lax.dynamic_slice_in_dim(values, (1 - core) * PART, PART, axis=dim))
-    return jnp.where(core == 0, own, theirs), jnp.where(core == 0, theirs, own)
+    )(*operands)
 
 
 SUM_ROWS = 1280
 
 
-def sum_kernel(down_ref, up_ref, conv_ref, class_ref, out_ref, total, give, pair_in, a_out, a_in,
-               b_out, b_in, z_out, z_in, result, send_sems, recv_sems):
+def sum_kernel(stacked_ref, coarse_grad_ref, bottom_ref, upward_grad_ref, down_weight_ref,
+               hidden_pre_ref, taps_ref, class_ref, out_ref, total, give, pair_in, a_out, a_in,
+               b_out, b_in, z_out, z_in, result, conv_ref, send_sems, recv_sems):
     core, first, second = place()
     depth = lax.axis_index("samp")
     me = block_of(core, first, second)
@@ -730,19 +755,27 @@
         pl.semaphore_signal(
             barrier, inc=1, device_id=device, device_id_type=pl.DeviceIdType.MESH
         )
-    pl.semaphore_wait(barrier, 10)
 
     def own_lanes(half, width):
         return pl.ds(pl.multiple_of(half * width, 128), width)
 
+    down_back = contract_last(coarse_grad_ref[0], down_weight_ref[:, 0:PART]) + contract_last(
+        coarse_grad_ref[1], down_weight_ref[:, PART:]
+    )
+    hidden_grad = (down_back + upward_grad_ref[...].astype(jnp.float32)) * silu_slope(
+        hidden_pre_ref[...]
+    )
+    conv_ref[...] = contract_first(taps_ref[...], stacked_up(hidden_grad.astype(jnp.bfloat16)))
+
     def pack(half, to, kind):
-        to[0:512, :] = down_ref[:, own_lanes(half, 512)].astype(kind)
-        to[512:1024, :] = up_ref[pl.ds(pl.multiple_of(half * 512, 512), 512), :].astype(kind)
+        to[0:512, :] = contract_first(stacked_ref[...], coarse_grad_ref[half]).astype(kind)
+        to[512:1024, :] = contract_first(bottom_ref[half], upward_grad_ref[...]).astype(kind)
         for piece in range(4):
             rows = pl.ds(pl.multiple_of((half * 4 + piece) * 144, 16), 144)
             to[1024:1168, piece * 128 : (piece + 1) * 128] = conv_ref[rows, :].astype(kind)
-        to[1168:1184, :] = class_ref[:, own_lanes(half, 512)].astype(kind)
-        to[1184:, :] = jnp.zeros((SUM_ROWS - 1184, PART), kind)
+            rows = slice(piece * 32, (piece + 1) * 32)
+            to[1168:1200, piece * 128 : (piece + 1) * 128] = class_ref[rows, :].astype(kind)
+        to[1200:, :] = jnp.zeros((SUM_ROWS - 1200, PART), kind)
 
     def spot(at_first, at_second):
         base = (at_first % 4) * 320 + (at_second % 4) * 80
@@ -750,6 +783,7 @@
 
     order = (2, 1, 3, 0)
     pack(1 - core, give, jnp.bfloat16)
+    pl.semaphore_wait(barrier, 10)
     for i, ds in enumerate(order):
         for df in range(4):
             part = spot(second + df, first + ds)
@@ -826,15 +860,13 @@
     copies.finish()
 
 
-def sum_everywhere(conv_grad, down_grad, up_grad, class_grad):
+def sum_everywhere(*operands):
     b16, f32 = jnp.bfloat16, jnp.float32
     vmem = pl.BlockSpec(memory_space=pltpu.VMEM)
-    classes = class_grad.shape[1]
-    small = jnp.pad(class_grad.T, ((0, 16 - classes), (0, 2 * PART - INNER)))
     out = pl.pallas_call(
         sum_kernel,
         out_shape=jax.ShapeDtypeStruct((2, SUM_ROWS, PART), b16),
-        in_specs=[vmem] * 4,
+        in_specs=[vmem] * 8,
         out_specs=vmem,
         scratch_shapes=[
             pltpu.VMEM((SUM_ROWS, PART), f32),
@@ -847,6 +879,7 @@
             pltpu.VMEM((4, 80, 128), b16),
             pltpu.VMEM((4, 80, 128), b16),
             pltpu.VMEM((2, SUM_ROWS, PART), b16),
+            pltpu.VMEM((9 * INNER, INNER), f32),
             pltpu.SemaphoreType.DMA((68,)),
             pltpu.SemaphoreType.DMA((68,)),
         ],
@@ -854,14 +887,15 @@
             collective_id=3, has_side_effects=True, vmem_limit_bytes=60 * 1024 * 1024
         ),
         name="sum_everywhere",
-    )(down_grad, up_grad, conv_grad.reshape(9 * INNER, INNER), small)
+    )(*operands)
     down = jnp.concatenate([out[0, 0:512], out[1, 0:512]], axis=1).astype(f32)
     up = out[:, 512:1024].astype(f32).reshape(2 * PART, PART)
     conv = jnp.concatenate(
         [out[h, 1024:1168, i * 128 : (i + 1) * 128] for h in range(2) for i in range(4)], axis=0
     )
-    conv = conv.astype(f32).reshape(conv_grad.shape)
-    return conv, down, up, out[0, 1168 : 1168 + classes, 0:INNER].astype(f32).T
+    conv = conv.astype(f32).reshape(3, 3, INNER, INNER)
+    small = jnp.concatenate([out[0, 1168:1200, i * 128 : i * 128 + 9] for i in range(4)], axis=0)
+    return conv, down, up, small.astype(f32)
 
 
 def local(
@@ -874,64 +908,27 @@
     up_weight,
     class_weight,
 ):
-    crop_rows = features[0]
-    label_map = labels[0]
-    height, across, channels = crop_rows.shape
-    half_rows = height // 2
-    half_across = across // 2
-    core = lax.axis_index("wide") % 2
-    pixel_count = lax.axis_size("wide") * lax.axis_size("samp") * height * across
-    loss_scale = 8.0 / math.sqrt(pixel_count)
-    classes = lax.broadcasted_iota(jnp.int32, (1, 1, class_weight.shape[1]), 2)
-
-    expand_both = jnp.concatenate(
-        pair_part(expand_weight.reshape(9, 2 * PART, INNER // 2), 1, core), axis=2
+    height, across, channels = features.shape[1:]
+    count = class_weight.shape[1]
+    columns = jnp.transpose(features.reshape(height, across // 2, 2, channels), (2, 0, 1, 3))
+    places = jnp.transpose(labels.reshape(height // 2, 2, across // 2, 2), (1, 3, 0, 2))
+    places = places.reshape(height * across, 1)
+    class_wide = jnp.pad(class_weight, ((0, 0), (0, INNER - count)))
+    class_tall = jnp.pad(class_weight.T, ((0, INNER - count), (0, 0)))
+    bottom, pre, expanded, coarse, wa_back, wb_back, stacked, hidden_pre, taps = bottleneck(
+        False,
+        columns,
+        conv_weight.reshape(9 * INNER, INNER),
+        down_weight,
+        expand_weight.reshape(9, 2 * PART, INNER // 2),
+        reduce_weight.reshape(9, INNER // 2, 2 * PART),
     )
-    reduce_both = jnp.concatenate(
-        pair_part(reduce_weight.reshape(9, INNER // 2, 2 * PART), 2, core), axis=1
+    coarse_grad, reduce_grad, expand_grad, upward_grad, class_grad = bottleneck(
+        True, wa_back, wb_back, pre, expanded, coarse, bottom, stacked, places, up_weight,
+        class_wide, class_tall,
     )
-    wa_forward = jnp.transpose(expand_both, (1, 0, 2)).reshape(PART, 9 * INNER)
-    wb_forward = reduce_both.reshape(9 * INNER, PART)
-    wa_backward = jnp.transpose(reduce_both[::-1], (2, 0, 1)).reshape(PART, 9 * INNER)
-    wb_backward = jnp.transpose(expand_both[::-1], (0, 2, 1)).reshape(9 * INNER, PART)
-
-    near_rows = extended(crop_rows, (("wide", 0),), 1)
-    padded_in = jnp.pad(near_rows, ((0, 0), (1, 1), (0, 0)))
-    hidden_pre = conv_padded(padded_in, conv_weight)
-    hidden = jax.nn.silu(hidden_pre).astype(jnp.bfloat16)
-    stacked = to_depth(hidden)
-    coarse = project_rows(stacked, down_weight)
-    bottom, saved = bottleneck(coarse.reshape(-1, 2 * PART), wa_forward, wb_forward)
-    bottom = bottom.reshape(half_rows, half_across, 2 * PART)
-    upward = from_depth(jnp.dot(bottom, up_weight, preferred_element_type=jnp.float32))
-    joined_pre = upward + hidden.astype(jnp.float32)
-    joined = jax.nn.silu(joined_pre).astype(jnp.bfloat16)
-    logits = jnp.dot(joined, class_weight, preferred_element_type=jnp.float32)
-    exp_logits = jnp.exp(logits)
-    probability = exp_logits / jnp.sum(exp_logits, axis=-1, keepdims=True)
-    onehot = (label_map[:, :, None] == classes).astype(jnp.float32)
-    logit_grad = ((probability - onehot) * loss_scale).astype(jnp.bfloat16)
-    class_grad = contract_rows(joined, logit_grad)
-    joined_grad = lax.dot_general(
-        logit_grad, class_weight, (((2,), (1,)), ((), ())), preferred_element_type=jnp.float32
-    )
-    upward_grad = (joined_grad * silu_slope(joined_pre)).astype(jnp.bfloat16)
-    stacked_grad = to_depth(upward_grad)
-    up_grad = contract_rows(bottom, stacked_grad)
-    bottom_grad = widen_rows(stacked_grad, up_weight)
-    coarse_grad, (reduce_grad, expand_grad) = bottleneck(
-        bottom_grad.reshape(-1, 2 * PART), wa_backward, wb_backward, saved
-    )
-    coarse_grad = coarse_grad.reshape(half_rows, half_across, 2 * PART)
-    down_grad = contract_rows(stacked, coarse_grad)
-    down_back = lax.dot_general(
-        coarse_grad, down_weight, (((2,), (1,)), ((), ())), preferred_element_type=jnp.float32
-    )
-    hidden_sum = from_depth(down_back) + upward_grad.astype(jnp.float32)
-    hidden_grad = (hidden_sum * silu_slope(hidden_pre)).astype(jnp.bfloat16)
-    conv_grad = correlate(padded_in, hidden_grad)
     conv_grad, down_grad, up_grad, class_grad = sum_everywhere(
-        conv_grad, down_grad, up_grad, class_grad
+        stacked, coarse_grad, bottom, upward_grad, down_weight, hidden_pre, taps, class_grad
     )
     reduce_grad = reduce_grad.reshape(3, 3, INNER // 2, -1)
     expand_grad = jnp.transpose(expand_grad.reshape(9, INNER // 2, -1)[::-1], (0, 2, 1))

time: 228 us -> 196 us (0.86)
  matrix products: 13.3 us -> 0 us
  local copies, waits for them, and re-layouts: 25 us -> 11.8 us
  starting transfers between devices: 6.52 us -> 0 us
  Pallas kernels: 172 us -> 178 us
  other arithmetic: 9.63 us -> 4.85 us
    dot_general x11 -> x0, matrix products: 13.3 us -> none  [the longest x3 4.66 us: contract_rows(): lax.dot_general(left_flat, right_flat, (((0,), (0,)), ((), ())), preferre...]
    ppermute x4 -> x0, starting transfers between devices: 6.52 us -> none  [the longest x1 3.09 us: extended(): lax.ppermute(lax.slice_in_dim(block, block.shape[dim] - width, None, axis...]
    pallas_call x2, Pallas kernels: 126 us -> 132 us  [bottleneck(): pl.pallas_call(functools.partial(phase_kernel, backward), out_shape=out_s...]
    another operation x10 -> x0, local copies, waits for them, and re-layouts: 3.71 us -> none  [the longest x1 1.81 us: local(): bottom = bottom.reshape(half_rows, half_across, 2 * PART)]
    dynamic_slice x2 -> x0, local copies, waits for them, and re-layouts: 3.18 us -> none  [pair_part(): lax.dynamic_slice_in_dim(values, (1 - core) * PART, PART, axis=dim)]
    transpose x4 -> x1, local copies, waits for them, and re-layouts: 3.26 us -> 0.09 us  [local(): jnp.transpose(labels.reshape(height // 2, 2, across // 2, 2), (1, 3, 0, 2))]
    select_n x2 -> x0, other arithmetic: 2.67 us -> none  [pair_part(): jnp.where(core == 0, own, theirs)]
    reshape x6 -> x3, local copies, waits for them, and re-layouts: 3.93 us -> 1.59 us  [the longest x1 0.82 us: local(): places = places.reshape(height * across, 1)]
  transfers between devices with their start and end apart: 4 -> 0, of which waited for: 0 -> 0; matrix products, arithmetic and copies ran while one was open for 4% -> 0% of each run, Pallas kernels for 0% -> 0%
where the time goes in v4:
time: 196 us; the launch traced here: 195 us
  Pallas kernels  178 us (91%)
  local copies, waits for them, and re-layouts  11.8 us (6%)
  other arithmetic  4.85 us (2%)
    pallas_call x2, Pallas kernels, bottleneck(): pl.pallas_call(functools.partial(phase_kernel, backward), out_shape=out_s...  132 us
    pallas_call x1, Pallas kernels, sum_everywhere(): pl.pallas_call(sum_kernel, out_shape=jax.ShapeDtypeStruct((2, SUM_ROWS, P...  45.9 us
    unnamed x22, local copies, waits for them, and re-layouts  5.6 us

profile of v4, /device:TPU:1, one launch (start us, length us, event | category | flops | bytes accessed | tf_op | source)
XLA Modules:
  0.0 195.3 jit_solution(9829210009630345543)
XLA Ops:
  0.6 0.0 copy-start.3
  0.6 3.7 %copy.25 = bf16[3,3,1024,64]{3,2,1,0:T(8,128)(2,1)} copy(bf16[3,3,1024,64]{2,3,1,0:T(8,128)(2,1)} %param.12) | data formatting | bytes 2359296 | tf_op args[4]
  4.4 0.0 copy-done.3
  4.4 0.7 copy.34
  5.0 0.0 copy-start.5
  5.0 0.0 copy-start.4
  5.0 62.3 %forward_phase.1 = (bf16[2,96,512]{2,1,0:T(8,128)(2,1)}, f32[3072,128]{1,0:T(8,128)}, bf16[3168,384]{1,0:T(8,128)(2,1)}, bf16[3072,512]{1,0:T(8,128)(2,1)}, bf16...) custom-call(bf16[2,4,48,128]{3,2,1,0:T(8,128)(2,1)} %bitcast.53, ...), custom_call_target="tpu_custom_call" | custom-call | tf_op jit(solution)/shard_map/forward_phase/pallas_call | solution.py:720
  67.3 0.0 copy-done.5
  67.3 0.1 reshape.53
  67.4 0.1 copy.26
  67.5 0.8 reshape.63.refs_7_
  68.3 0.0 copy-done.4
  68.3 0.1 copy.27
  68.5 0.6 pad.8.refs_9_
  69.1 0.6 pad.9.refs_10_
  69.7 69.8 %backward_phase.1 = (bf16[2,96,512]{2,1,0:T(8,128)(2,1)}, f32[576,256]{1,0:T(8,128)}, f32[576,256]{1,0:T(8,128)}, bf16[96,512]{1,0:T(8,128)(2,1)}, f32[128,128]{1,0:T(8,128)}) custom-call(bf16[512,1152]{1,0:T(8,128)(2,1)} %get-tuple-element.21.refs_0_, bf16[1152,512]{1,0:T(8,128)(2,1)} %get-tuple-element.22.refs_1_, f32[3072,128]{1,0:T(8,128)} %get-tuple-element.23.refs_2_, ...), custom_call_target="tpu_custom_call" | custom-call | tf_op jit(solution)/shard_map/backward_phase/pallas_call | solution.py:720
  139.5 45.9 %sum_everywhere.1 = bf16[2,1280,512]{2,1,0:T(8,128)(2,1)} custom-call(bf16[96,512]{1,0:T(8,128)(2,1)} %get-tuple-element.20.refs_6_.stacked_ref, bf16[2,96,512]{2,1,0:T(8,128)(2,1)} %get-tuple-element.27.coarse_grad_ref, bf16[2,96,512]{2,1,0:T(8,128)(2,1)} %get-tuple-element.26.refs_5_.bottom_ref, bf16[96,512]{1,0:T(8,128)(2,1)} %get-tuple-element.28.upward_grad_ref, ...), custom_call_target="tpu_custom_call" | custom-call | tf_op jit(solution)/shard_map/sum_everywhere/pallas_call | solution.py:866
  185.4 0.8 slice_bitcast_fusion.5
  186.2 0.1 copy.29
  186.2 0.1 copy.30
  186.3 0.1 copy.31
  186.4 0.1 copy.32
  186.5 0.7 maximum_convert_fusion.1
  187.2 1.3 slice_bitcast_fusion.1
  188.5 0.0 slice-start
  188.5 1.6 maximum_convert_fusion
  190.1 0.0 copy-start
  190.1 0.0 slice-done
  190.1 0.0 copy-start.2
  190.1 0.0 copy-start.1
  190.1 1.7 bitcast_convert_fusion
  191.8 0.8 copy-done
  192.7 0.9 convert.2
  193.6 0.0 copy-done.2
  193.6 0.9 rev.3
  194.5 0.0 copy-done.1
  194.5 0.8 copy.43
  (8 shorter events, 0.1 us)
Async XLA Ops:
  0.6 3.7 %copy-start.3 = (bf16[1,4,96,128]{3,2,1,0:T(8,128)(2,1)S(1)}, bf16[1,4,96,128]{3,2,1,0:T(8,128)(2,1)}, u32[]{:S(2)}) copy-start(bf16[1,4,96,128]{3,2,1,0:T(8,128)(2,1)} %param.8) | copy-start | bytes 294916
  5.0 62.3 %copy-start.5 = (s32[1,4,96]{2,1,0:T(4,128)S(1)}, s32[1,4,96]{2,1,0:T(4,128)}, u32[]{:S(2)}) copy-start(s32[1,4,96]{2,1,0:T(4,128)} %param.9) | copy-start | bytes 4612
  5.0 63.3 %copy-start.4 = (bf16[128,9]{0,1:T(8,128)(2,1)S(1)}, bf16[128,9]{0,1:T(8,128)(2,1)}, u32[]{:S(2)}) copy-start(bf16[128,9]{0,1:T(8,128)(2,1)} %param.15) | copy-start | bytes 6916
  188.5 1.6 slice-start
  190.1 2.5 %copy-start = (bf16[2,1280,512]{2,1,0:T(8,128)(2,1)S(1)}, bf16[2,1280,512]{2,1,0:T(8,128)(2,1)}, u32[]{:S(2)}) copy-start(bf16[2,1280,512]{2,1,0:T(8,128)(2,1)} %sum_everywhere.1) | copy-start | bytes 7864324
  190.1 3.5 %copy-start.2 = (f32[576,256]{1,0:T(8,128)S(1)}, f32[576,256]{1,0:T(8,128)}, u32[]{:S(2)}) copy-start(f32[576,256]{1,0:T(8,128)} %get-tuple-element.32) | copy-start | bytes 1769476
  190.1 4.4 %copy-start.1 = (f32[576,256]{1,0:T(8,128)S(1)}, f32[576,256]{1,0:T(8,128)}, u32[]{:S(2)}) copy-start(f32[576,256]{1,0:T(8,128)} %get-tuple-element.33) | copy-start | bytes 1769476

commit v5 on v4

--- a/solution.py
+++ b/solution.py
@@ -20,6 +20,7 @@
 PIECE = 192
 HALF = 96
 PART = 512
+LANES = 256
 INNER = 128
 WIDE_ROWS = 3 * INNER
 
@@ -108,26 +109,25 @@
 
 
 def first_layers(wide, copies, after, before, feature_ref, halo, columns, conv_weight_ref,
-                 down_weight_ref, taps_ref, hidden_pre_ref, stacked_ref, x_ref):
+                 taps_ref, hidden_pre_ref, stacked_ref, x_ref, spread_rows):
     at_left, at_right = edge_masks(ACROSS)
 
-    def row_columns(row, even, odd):
+    def row_columns(row, values):
+        spread_rows[pl.ds(row * 2 * ACROSS, 2 * ACROSS), :] = values
+        even = spread_rows[pl.ds(row * 2 * ACROSS, ACROSS, stride=2), :]
+        odd = spread_rows[pl.ds(row * 2 * ACROSS + 1, ACROSS, stride=2), :]
         to = pl.ds(row * ACROSS, ACROSS)
-        even = even.astype(jnp.float32)
-        odd = odd.astype(jnp.float32)
         columns[0, to, :] = from_left(odd, at_left).astype(jnp.bfloat16)
         columns[1, to, :] = even.astype(jnp.bfloat16)
         columns[2, to, :] = odd.astype(jnp.bfloat16)
         columns[3, to, :] = from_right(even, at_right).astype(jnp.bfloat16)
 
     for row in range(4):
-        row_columns(row + 1, feature_ref[0, row], feature_ref[1, row])
+        row_columns(row + 1, feature_ref[row].astype(jnp.float32))
     copies.arrived(56, halo.at[0], after)
     copies.arrived(57, halo.at[1], before)
-    inside = jnp.where(wide > 0, 1.0, 0.0)
-    row_columns(0, halo[0, 0].astype(jnp.float32) * inside, halo[0, 1].astype(jnp.float32) * inside)
-    inside = jnp.where(wide < 31, 1.0, 0.0)
-    row_columns(5, halo[1, 0].astype(jnp.float32) * inside, halo[1, 1].astype(jnp.float32) * inside)
+    row_columns(0, halo[0].astype(jnp.float32) * jnp.where(wide > 0, 1.0, 0.0))
+    row_columns(5, halo[1].astype(jnp.float32) * jnp.where(wide < 31, 1.0, 0.0))
     for a in range(2):
         for b in range(2):
             for i in range(2):
@@ -145,50 +145,64 @@
     stacked = jax.nn.silu(hidden_pre).astype(jnp.bfloat16)
     stacked_ref[...] = stacked
     for half in range(2):
-        x_ref[half] = multiply(
-            stacked, down_weight_ref[:, half * PART : (half + 1) * PART]
-        ).astype(jnp.bfloat16)
-
-
-def middle(bottom_ref, stacked_ref, label_ref, up_weight_ref, class_ref, class_back_ref,
+        x_ref[half] = stacked[:, half * LANES : (half + 1) * LANES]
+
+
+def label_column(labels):
+    values = labels.astype(jnp.float32).astype(jnp.bfloat16)
+    to = lax.broadcasted_iota(jnp.int32, (ACROSS, HALF), 0)
+    source = lax.broadcasted_iota(jnp.int32, (ACROSS, HALF), 1)
+    pieces = []
+    picked = [
+        contract_last((source == 2 * to + b).astype(jnp.float32).astype(jnp.bfloat16), values)
+        for b in range(2)
+    ]
+    for a in range(2):
+        for b in range(2):
+            for i in range(2):
+                row = a + 2 * i
+                pieces.append(picked[b][:, row : row + 1])
+    return jnp.concatenate(pieces, axis=0)
+
+
+def middle(coarse_ref, inner_ref, stacked_ref, label_ref, up_weight_ref, class_ref,
            x_ref, upward_grad_ref, class_grad_ref):
     loss_scale = 8.0 / math.sqrt(49152)
-    upward = multiply(bottom_ref[0], up_weight_ref[0:PART, :]) + multiply(
-        bottom_ref[1], up_weight_ref[PART:, :]
+    upward = multiply(coarse_ref[0], up_weight_ref[0:PART, :]) + multiply(
+        coarse_ref[1], up_weight_ref[PART:, :]
     )
+    upward = upward + jnp.concatenate([inner_ref[0], inner_ref[1]], axis=1)
     joined_pre = stacked_up(upward + stacked_ref[...].astype(jnp.float32))
     joined = jax.nn.silu(joined_pre).astype(jnp.bfloat16)
-    logits = multiply(joined, class_ref[...])
+    logits = contract_last(joined, class_ref[...])
     classes = lax.broadcasted_iota(jnp.int32, logits.shape, 1)
-    exp_logits = jnp.where(classes < 9, jnp.exp(logits), 0.0)
+    exp_logits = jnp.exp(logits)
     probability = exp_logits / jnp.sum(exp_logits, axis=1, keepdims=True)
-    onehot = (label_ref[...] == classes).astype(jnp.float32)
+    onehot = (label_column(label_ref[...]) == classes.astype(jnp.float32)).astype(jnp.float32)
     logit_grad = ((probability - onehot) * loss_scale).astype(jnp.bfloat16)
-    joined_grad = multiply(logit_grad, class_back_ref[...])
+    joined_grad = multiply(logit_grad, class_ref[...])
     upward_grad = side_by_side((joined_grad * silu_slope(joined_pre)).astype(jnp.bfloat16))
     upward_grad_ref[...] = upward_grad
     for half in range(2):
-        x_ref[half] = contract_last(
-            upward_grad, up_weight_ref[half * PART : (half + 1) * PART, :]
-        ).astype(jnp.bfloat16)
-    class_grad_ref[...] = contract_first(joined, logit_grad)
+        x_ref[half] = upward_grad[:, half * LANES : (half + 1) * LANES]
+    class_grad_ref[...] = contract_first(logit_grad, joined)
 
 
 def phase_kernel(backward, *refs):
     if backward:
         (
-            wa_hbm, wb_hbm, pre_hbm, ef_hbm, xf_hbm, bottom_ref, stacked_ref, label_ref,
-            up_weight_ref, class_ref, class_back_ref,
-            out_ref, ge_ref, gf_ref, upward_grad_ref, class_grad_ref,
-        ) = refs[:16]
-        scratch = refs[16:]
+            wa_hbm, wb_hbm, pre_hbm, ef_hbm, xf_hbm, coarse_ref, inner_ref, stacked_ref, label_ref,
+            up_weight_ref, down_weight_ref, class_ref,
+            out_ref, ge_ref, gf_ref, upward_grad_ref, class_grad_ref, bottom_grad_ref, joint_ref,
+        ) = refs[:19]
+        scratch = refs[19:]
     else:
         (
-            feature_ref, conv_weight_ref, down_weight_ref, expand_hbm, reduce_hbm,
-            out_ref, pre_hbm, ef_hbm, xf_hbm, wa_hbm, wb_hbm, stacked_ref, hidden_pre_ref,
-            taps_ref,
-        ) = refs[:14]
-        scratch = refs[14:]
+            feature_ref, conv_weight_ref, down_weight_ref, up_weight_ref, expand_hbm, reduce_hbm,
+            out_ref, pre_hbm, ef_hbm, xf_hbm, wa_hbm, wb_hbm, expand_tall_hbm, stacked_ref,
+            hidden_pre_ref, taps_ref, coarse_ref,
+        ) = refs[:17]
+        scratch = refs[17:]
     (
         xall, wa, wb, total, pre, other, padded, chunk, window,
         far_out, up_out, down_out, far_in, up_in, down_in, reduced,
@@ -209,23 +223,22 @@
             pltpu.make_async_copy(wa_hbm, wa, local_sems.at[0]),
             pltpu.make_async_copy(wb_hbm, wb, local_sems.at[1]),
         ]
-        pre_f, ef, xf, grad, full, give, zfar_in, zup_out, zdown_out, zup_in, zdown_in = scratch[28:]
+        pre_f, ef, xf, grad, full, give, zfar_in, zup_out, zdown_out, zup_in, zdown_in, joint = scratch[28:]
         loads += [
             pltpu.make_async_copy(pre_hbm, pre_f, local_sems.at[2]),
             pltpu.make_async_copy(ef_hbm, ef, local_sems.at[3]),
             pltpu.make_async_copy(xf_hbm, xf, local_sems.at[4]),
         ]
     else:
-        expand_both, reduce_both, wa_back, wb_back, halo, columns = scratch[28:]
-        lanes = pl.ds(pl.multiple_of(core * PART, PART), PART)
-        other_lanes = pl.ds(pl.multiple_of((1 - core) * PART, PART), PART)
+        expand_both, reduce_both, wa_back, wb_back, halo, columns, expand_tall, spread_rows = scratch[28:]
+        lanes = pl.ds(pl.multiple_of(core * LANES, LANES), LANES)
         own_rows = pl.ds(pl.multiple_of(core * 64, 64), 64)
         loads = [
             pltpu.make_async_copy(
-                expand_hbm.at[:, lanes, :], expand_both.at[core], local_sems.at[0]
+                expand_hbm, expand_both.at[:, own_rows, :], local_sems.at[0]
             ),
             pltpu.make_async_copy(
-                reduce_hbm.at[:, :, lanes], reduce_both.at[:, own_rows, :], local_sems.at[1]
+                reduce_hbm, reduce_both.at[:, own_rows, :], local_sems.at[1]
             ),
         ]
     for load in loads:
@@ -249,20 +262,18 @@
         )
     if backward:
         middle(
-            bottom_ref, stacked_ref, label_ref, up_weight_ref, class_ref, class_back_ref,
+            coarse_ref, inner_ref, stacked_ref, label_ref, up_weight_ref, class_ref,
             x_ref, upward_grad_ref, class_grad_ref,
         )
     pl.semaphore_wait(barrier, len(peers))
     if not backward:
-        copies.start(56, feature_ref.at[:, 3], halo.at[0], after)
-        copies.start(57, feature_ref.at[:, 0], halo.at[1], before)
-        copies.start(58, expand_hbm.at[:, other_lanes, :], expand_both.at[core], partner)
-        copies.start(
-            59, reduce_hbm.at[:, :, other_lanes], reduce_both.at[:, own_rows, :], partner
-        )
+        copies.start(56, feature_ref.at[3], halo.at[0], after)
+        copies.start(57, feature_ref.at[0], halo.at[1], before)
+        copies.start(58, expand_hbm, expand_both.at[:, own_rows, :], partner)
+        copies.start(59, reduce_hbm, reduce_both.at[:, own_rows, :], partner)
         first_layers(
             wide, copies, after, before, feature_ref, halo, columns, conv_weight_ref,
-            down_weight_ref, taps_ref, hidden_pre_ref, stacked_ref, x_ref,
+            taps_ref, hidden_pre_ref, stacked_ref, x_ref, spread_rows,
         )
 
     mine = pl.ds(pl.multiple_of(me * PIECE + core * HALF, 32), HALF)
@@ -289,7 +300,7 @@
         return carry
 
     def clear_grad(step, carry):
-        grad[pl.ds(pl.multiple_of(step * INNER, 128), INNER), :] = jnp.zeros((INNER, PART), jnp.float32)
+        grad[pl.ds(pl.multiple_of(step * INNER, 128), INNER), :] = jnp.zeros((INNER, LANES), jnp.float32)
         return carry
 
     def add_gradient():
@@ -315,12 +326,12 @@
             to = pl.ds(pl.multiple_of(tap * 64, 64), 64)
             own_rows = pl.ds(pl.multiple_of(tap * INNER + core * 64, 64), 64)
             other_rows = pl.ds(pl.multiple_of(tap * INNER + (1 - core) * 64, 64), 64)
-            full[which, core, to, :] = grad[own_rows, :].astype(jnp.bfloat16)
+            joint[which, core, to, :] = grad[own_rows, :].astype(jnp.bfloat16)
             give[which, to, :] = grad[other_rows, :].astype(jnp.bfloat16)
             return carry
 
         lax.fori_loop(0, 9, pack, 0)
-        copies.start(38 + which, give.at[which], full.at[which, core], partner)
+        copies.start(38 + which, give.at[which], joint.at[which, core], partner)
 
     def share(which, at, low, length):
         at = at % 4
@@ -328,7 +339,15 @@
         return full.at[which, at // 2, pl.ds(low, length), lanes]
 
     def depth_far(which):
-        copies.arrived(38 + which, full.at[which, 1 - core], partner)
+        copies.arrived(38 + which, joint.at[which, 1 - core], partner)
+        both = jnp.concatenate([joint[which, 0], joint[which, 1]], axis=1)
+        joint_ref[which] = both
+        for half in range(2):
+            part = slice(half * PART, (half + 1) * PART)
+            if which == 0:
+                full[which, half] = narrow(contract_last(both, up_weight_ref[part, :]))
+            else:
+                full[which, half] = narrow(multiply(both, down_weight_ref[:, part]))
         copies.start(40 + which, share(which, depth + 2, 0, 288), zfar_in.at[which, 0], z_up)
         copies.start(42 + which, share(which, depth + 2, 288, 288), zfar_in.at[which, 1], z_down)
 
@@ -376,6 +395,22 @@
         copies.arrived(9 + order, here, s_down)
         high = piece(first_at, second + 1, HALF, HALF)
         copies.start(48 + order, high, high, s_down)
+
+    for load in loads:
+        load.wait()
+    if not backward:
+        partner_rows = pl.ds(pl.multiple_of((1 - core) * 64, 64), 64)
+        copies.arrived(58, expand_both.at[:, partner_rows, :], partner)
+        copies.arrived(59, reduce_both.at[:, partner_rows, :], partner)
+        share_rows = down_weight_ref[pl.ds(pl.multiple_of(core * LANES, LANES), LANES), :]
+        joined_weight = narrow(
+            contract_last(expand_both[...].reshape(9 * INNER, 2 * PART), share_rows)
+        )
+        for tap in range(9):
+            block = joined_weight[tap * INNER : (tap + 1) * INNER, :]
+            wa[:, tap * INNER : (tap + 1) * INNER] = block.T
+            wb_back[(8 - tap) * INNER : (9 - tap) * INNER, :] = block
+            expand_tall[(8 - tap) * 64 : (9 - tap) * 64, :] = expand_both[tap, own_rows, :]
 
     left = piece(first + 3, second)
     right = piece(first + 1, second)
@@ -391,29 +426,35 @@
     copies.arrived(3, piece(first + 2, second, 0, HALF), f_up)
     copies.arrived(4, piece(first + 2, second, HALF, HALF), f_down)
     send_second(3, first + 2)
-    for load in loads:
-        load.wait()
     if not backward:
-        copies.arrived(58, expand_both.at[1 - core], partner)
-        partner_rows = pl.ds(pl.multiple_of((1 - core) * 64, 64), 64)
-        copies.arrived(59, reduce_both.at[:, partner_rows, :], partner)
+        wb[...] = narrow(
+            multiply(
+                reduce_both[...].reshape(9 * INNER, 2 * PART), up_weight_ref[:, lanes]
+            )
+        )
         for tap in range(9):
             here = slice(tap * INNER, (tap + 1) * INNER)
             back = slice((8 - tap) * INNER, (9 - tap) * INNER)
-            block = jnp.concatenate([expand_both[0, tap], expand_both[1, tap]], axis=1)
-            wa[:, here] = block
-            wb_back[back, :] = block.T
-            block = reduce_both[tap]
-            wb[here, :] = block
-            wa_back[:, back] = block.T
+            wa_back[:, back] = wb[here, :].T
+        for half in range(2):
+            coarse_ref[half] = narrow(
+                multiply(stacked_ref[...], down_weight_ref[:, half * PART : (half + 1) * PART])
+            )
         stores = [
             pltpu.make_async_copy(wa_back, wa_hbm, local_sems.at[0]),
             pltpu.make_async_copy(wb_back, wb_hbm, local_sems.at[1]),
+            pltpu.make_async_copy(expand_tall, expand_tall_hbm, local_sems.at[5]),
         ]
         for store in stores:
             store.start()
     else:
         stores = []
+        for half in range(2):
+            bottom_grad_ref[half] = narrow(
+                contract_last(
+                    upward_grad_ref[...], up_weight_ref[half * PART : (half + 1) * PART, :]
+                )
+            )
 
     def product(step, carry):
         turn = (3 * step + (step // 2) * (7 - 2 * step)) % 4
@@ -635,9 +676,9 @@
 
     swap_out[...] = narrow(settled(1 - core))
     copies.start(37, swap_out, swap_in, partner)
-    out_ref[core] = narrow(x_ref[core].astype(jnp.float32) + settled(core))
+    out_ref[core] = settled(core)
     copies.arrived(37, swap_in, partner)
-    out_ref[1 - core] = narrow(x_ref[1 - core].astype(jnp.float32) + swap_in[...].astype(jnp.float32))
+    out_ref[1 - core] = swap_in[...].astype(jnp.float32)
     if backward:
         depth_own(0, ge_ref)
         depth_own(1, gf_ref)
@@ -652,70 +693,79 @@
     anywhere = pl.BlockSpec(memory_space=pl.ANY)
     padded_rows = SPOTS + 2 * ACROSS
     shape = jax.ShapeDtypeStruct
-    out = shape((2, HALF, PART), b16)
+    out = shape((2, HALF, LANES), f32)
+    pair = shape((2, HALF, PART), b16)
     if backward:
         grad = shape((9 * INNER // 2, PART // 2), f32)
-        in_specs = [anywhere] * 5 + [vmem] * 6
-        out_shape = [out, grad, grad, shape((HALF, PART), b16), shape((INNER, INNER), f32)]
-        out_specs = [vmem] * 5
+        in_specs = [anywhere] * 5 + [vmem] * 7
+        out_shape = [
+            out, grad, grad, shape((HALF, PART), b16), shape((9, INNER), f32), pair,
+            shape((2, 9 * INNER // 2, PART), b16),
+        ]
+        out_specs = [vmem] * 7
     else:
-        in_specs = [vmem] * 3 + [anywhere] * 2
+        in_specs = [vmem] * 4 + [anywhere] * 2
         out_shape = [
             out,
             shape((SPOTS, INNER), f32),
             shape((padded_rows, WIDE_ROWS), b16),
-            shape((SPOTS, PART), b16),
-            shape((PART, 9 * INNER), b16),
-            shape((9 * INNER, PART), b16),
+            shape((SPOTS, LANES), b16),
+            shape((LANES, 9 * INNER), b16),
+            shape((9 * INNER, LANES), b16),
+            shape((9 * INNER // 2, 2 * PART), b16),
             shape((HALF, PART), b16),
             shape((HALF, PART), f32),
             shape((4 * HALF, 9 * INNER), b16),
+            pair,
         ]
-        out_specs = [vmem] + [anywhere] * 5 + [vmem] * 3
+        out_specs = [vmem] + [anywhere] * 6 + [vmem] * 4
     scratch = [
-        pltpu.VMEM((SPOTS, PART), b16),
-        pltpu.VMEM((PART, 9 * INNER), b16),
-        pltpu.VMEM((9 * INNER, PART), b16),
+        pltpu.VMEM((SPOTS, LANES), b16),
+        pltpu.VMEM((LANES, 9 * INNER), b16),
+        pltpu.VMEM((9 * INNER, LANES), b16),
         pltpu.VMEM((padded_rows, WIDE_ROWS), f32),
         pltpu.VMEM((SPOTS, INNER), f32),
         pltpu.VMEM((SPOTS, INNER), f32),
         pltpu.VMEM((padded_rows, WIDE_ROWS), b16),
-        pltpu.VMEM((4 * PIECE, PART), b16),
+        pltpu.VMEM((4 * PIECE, LANES), b16),
         pltpu.VMEM((4 * PIECE, 9 * INNER), b16),
-        *[pltpu.VMEM((4, PIECE, PART), b16) for _ in range(6)],
-        pltpu.VMEM((4, 4, PIECE, PART), f32),
-        pltpu.VMEM((2, HALF, PART), b16),
-        pltpu.VMEM((PIECE, PART), b16),
-        pltpu.VMEM((PIECE, PART), b16),
-        pltpu.VMEM((2, HALF, PART), b16),
-        pltpu.VMEM((PIECE, PART), b16),
-        pltpu.VMEM((PIECE, PART), b16),
-        pltpu.VMEM((HALF, PART), b16),
-        pltpu.VMEM((HALF, PART), b16),
-        pltpu.VMEM((2, HALF, PART), b16),
+        *[pltpu.VMEM((4, PIECE, LANES), b16) for _ in range(6)],
+        pltpu.VMEM((4, 4, PIECE, LANES), f32),
+        pltpu.VMEM((2, HALF, LANES), b16),
+        pltpu.VMEM((PIECE, LANES), b16),
+        pltpu.VMEM((PIECE, LANES), b16),
+        pltpu.VMEM((2, HALF, LANES), b16),
+        pltpu.VMEM((PIECE, LANES), b16),
+        pltpu.VMEM((PIECE, LANES), b16),
+        pltpu.VMEM((HALF, LANES), b16),
+        pltpu.VMEM((HALF, LANES), b16),
+        pltpu.VMEM((2, HALF, LANES), b16),
         pltpu.SemaphoreType.DMA((60,)),
         pltpu.SemaphoreType.DMA((60,)),
-        pltpu.SemaphoreType.DMA((5,)),
+        pltpu.SemaphoreType.DMA((6,)),
     ]
     if backward:
         scratch += [
             pltpu.VMEM((SPOTS, INNER), f32),
             pltpu.VMEM((padded_rows, WIDE_ROWS), b16),
-            pltpu.VMEM((SPOTS, PART), b16),
-            pltpu.VMEM((9 * INNER, PART), f32),
+            pltpu.VMEM((SPOTS, LANES), b16),
+            pltpu.VMEM((9 * INNER, LANES), f32),
             pltpu.VMEM((2, 2, 576, PART), b16),
-            pltpu.VMEM((2, 576, PART), b16),
+            pltpu.VMEM((2, 576, LANES), b16),
             pltpu.VMEM((2, 2, 288, 256), b16),
             *[pltpu.VMEM((2, 576, 256), b16) for _ in range(4)],
+            pltpu.VMEM((2, 2, 576, LANES), b16),
         ]
     else:
         scratch += [
-            pltpu.VMEM((2, 9, PART, INNER // 2), b16),
-            pltpu.VMEM((9, INNER, PART), b16),
-            pltpu.VMEM((PART, 9 * INNER), b16),
-            pltpu.VMEM((9 * INNER, PART), b16),
-            pltpu.VMEM((2, 2, ACROSS, INNER), b16),
+            pltpu.VMEM((9, INNER, 2 * PART), b16),
+            pltpu.VMEM((9, INNER, 2 * PART), b16),
+            pltpu.VMEM((LANES, 9 * INNER), b16),
+            pltpu.VMEM((9 * INNER, LANES), b16),
+            pltpu.VMEM((2, 2 * ACROSS, INNER), b16),
             pltpu.VMEM((4, 6 * ACROSS, INNER), b16),
+            pltpu.VMEM((9 * INNER // 2, 2 * PART), b16),
+            pltpu.VMEM((12 * ACROSS, INNER), f32),
         ]
     return pl.pallas_call(
         functools.partial(phase_kernel, backward),
@@ -735,8 +785,8 @@
 SUM_ROWS = 1280
 
 
-def sum_kernel(stacked_ref, coarse_grad_ref, bottom_ref, upward_grad_ref, down_weight_ref,
-               hidden_pre_ref, taps_ref, class_ref, out_ref, total, give, pair_in, a_out, a_in,
+def sum_kernel(stacked_ref, coarse_ref, upward_grad_ref, bottom_grad_ref, inner_ref, joint_ref,
+               reduce_ref, expand_ref, down_weight_ref, hidden_pre_ref, taps_ref, class_ref, down_out, up_out, conv_out, class_out, total, give, pair_in, a_out, a_in,
                b_out, b_in, z_out, z_in, result, conv_ref, send_sems, recv_sems):
     core, first, second = place()
     depth = lax.axis_index("samp")
@@ -759,23 +809,31 @@
     def own_lanes(half, width):
         return pl.ds(pl.multiple_of(half * width, 128), width)
 
-    down_back = contract_last(coarse_grad_ref[0], down_weight_ref[:, 0:PART]) + contract_last(
-        coarse_grad_ref[1], down_weight_ref[:, PART:]
+    down_back = contract_last(bottom_grad_ref[0], down_weight_ref[:, 0:PART]) + contract_last(
+        bottom_grad_ref[1], down_weight_ref[:, PART:]
     )
+    down_back = down_back + jnp.concatenate([inner_ref[0], inner_ref[1]], axis=1)
     hidden_grad = (down_back + upward_grad_ref[...].astype(jnp.float32)) * silu_slope(
         hidden_pre_ref[...]
     )
     conv_ref[...] = contract_first(taps_ref[...], stacked_up(hidden_grad.astype(jnp.bfloat16)))
 
     def pack(half, to, kind):
-        to[0:512, :] = contract_first(stacked_ref[...], coarse_grad_ref[half]).astype(kind)
-        to[512:1024, :] = contract_first(bottom_ref[half], upward_grad_ref[...]).astype(kind)
+        lanes = own_lanes(half, PART)
+        to[0:512, :] = (
+            contract_first(stacked_ref[...], bottom_grad_ref[half])
+            + contract_first(joint_ref[1], expand_ref[:, lanes])
+        ).astype(kind)
+        to[512:1024, :] = (
+            contract_first(coarse_ref[half], upward_grad_ref[...])
+            + contract_first(reduce_ref[:, lanes], joint_ref[0])
+        ).astype(kind)
+        to[1168:1184, :] = jnp.zeros((16, PART), kind)
+        to[1168:1177, 0:INNER] = class_ref[...].astype(kind)
         for piece in range(4):
             rows = pl.ds(pl.multiple_of((half * 4 + piece) * 144, 16), 144)
             to[1024:1168, piece * 128 : (piece + 1) * 128] = conv_ref[rows, :].astype(kind)
-            rows = slice(piece * 32, (piece + 1) * 32)
-            to[1168:1200, piece * 128 : (piece + 1) * 128] = class_ref[rows, :].astype(kind)
-        to[1200:, :] = jnp.zeros((SUM_ROWS - 1200, PART), kind)
+        to[1184:, :] = jnp.zeros((SUM_ROWS - 1184, PART), kind)
 
     def spot(at_first, at_second):
         base = (at_first % 4) * 320 + (at_second % 4) * 80
@@ -852,22 +910,35 @@
         for df in (1, 3, 2):
             copies.arrived(40 + ds * 3 + df - 1, at(4 - df, ds, core), first_peers[df])
             pass_on(4 - df, ds)
-    out_ref[core] = result[core]
+    def unpack(half):
+        down_out[:, own_lanes(half, PART)] = result[half, 0:512, :]
+        up_out[pl.ds(pl.multiple_of(half * PART, PART), PART), :] = result[half, 512:1024, :]
+        for piece in range(4):
+            rows = pl.ds(pl.multiple_of((half * 4 + piece) * 144, 16), 144)
+            conv_out[rows, :] = result[half, 1024:1168, piece * 128 : (piece + 1) * 128]
+
+    unpack(core)
     for df in range(4):
         for ds in range(4):
             copies.arrived(52 + df * 4 + ds, at(df, ds, 1 - core), partner)
-    out_ref[1 - core] = result[1 - core]
+    unpack(1 - core)
+    class_out[...] = result[0, 1168:1184, 0:INNER].astype(jnp.float32)[0:9, :]
     copies.finish()
 
 
 def sum_everywhere(*operands):
     b16, f32 = jnp.bfloat16, jnp.float32
     vmem = pl.BlockSpec(memory_space=pltpu.VMEM)
-    out = pl.pallas_call(
+    down, up, conv, small = pl.pallas_call(
         sum_kernel,
-        out_shape=jax.ShapeDtypeStruct((2, SUM_ROWS, PART), b16),
-        in_specs=[vmem] * 8,
-        out_specs=vmem,
+        out_shape=[
+            jax.ShapeDtypeStruct((PART, 2 * PART), b16),
+            jax.ShapeDtypeStruct((2 * PART, PART), b16),
+            jax.ShapeDtypeStruct((9 * INNER, INNER), b16),
+            jax.ShapeDtypeStruct((9, INNER), f32),
+        ],
+        in_specs=[vmem] * 12,
+        out_specs=[vmem] * 4,
         scratch_shapes=[
             pltpu.VMEM((SUM_ROWS, PART), f32),
             pltpu.VMEM((SUM_ROWS, PART), b16),
@@ -888,14 +959,8 @@
         ),
         name="sum_everywhere",
     )(*operands)
-    down = jnp.concatenate([out[0, 0:512], out[1, 0:512]], axis=1).astype(f32)
-    up = out[:, 512:1024].astype(f32).reshape(2 * PART, PART)
-    conv = jnp.concatenate(
-        [out[h, 1024:1168, i * 128 : (i + 1) * 128] for h in range(2) for i in range(4)], axis=0
-    )
     conv = conv.astype(f32).reshape(3, 3, INNER, INNER)
-    small = jnp.concatenate([out[0, 1168:1200, i * 128 : i * 128 + 9] for i in range(4)], axis=0)
-    return conv, down, up, small.astype(f32)
+    return conv, down.astype(f32), up.astype(f32), small.T
 
 
 def local(
@@ -908,27 +973,23 @@
     up_weight,
     class_weight,
 ):
-    height, across, channels = features.shape[1:]
-    count = class_weight.shape[1]
-    columns = jnp.transpose(features.reshape(height, across // 2, 2, channels), (2, 0, 1, 3))
-    places = jnp.transpose(labels.reshape(height // 2, 2, across // 2, 2), (1, 3, 0, 2))
-    places = places.reshape(height * across, 1)
-    class_wide = jnp.pad(class_weight, ((0, 0), (0, INNER - count)))
-    class_tall = jnp.pad(class_weight.T, ((0, INNER - count), (0, 0)))
-    bottom, pre, expanded, coarse, wa_back, wb_back, stacked, hidden_pre, taps = bottleneck(
-        False,
-        columns,
-        conv_weight.reshape(9 * INNER, INNER),
-        down_weight,
-        expand_weight.reshape(9, 2 * PART, INNER // 2),
-        reduce_weight.reshape(9, INNER // 2, 2 * PART),
+    expand = jnp.transpose(expand_weight, (0, 1, 3, 2)).reshape(9, INNER // 2, 2 * PART)
+    reduce = reduce_weight.reshape(9, INNER // 2, 2 * PART)
+    (
+        inner, pre, expanded, gathered, wa_back, wb_back, expand_tall, stacked, hidden_pre, taps,
+        coarse,
+    ) = bottleneck(
+        False, features[0], conv_weight.reshape(9 * INNER, INNER), down_weight, up_weight, expand,
+        reduce,
     )
-    coarse_grad, reduce_grad, expand_grad, upward_grad, class_grad = bottleneck(
-        True, wa_back, wb_back, pre, expanded, coarse, bottom, stacked, places, up_weight,
-        class_wide, class_tall,
+    inner_back, reduce_grad, expand_grad, upward_grad, class_grad, bottom_grad, joint = bottleneck(
+        True, wa_back, wb_back, pre, expanded, gathered, coarse, inner, stacked, labels[0], up_weight,
+        down_weight, class_weight.T,
     )
     conv_grad, down_grad, up_grad, class_grad = sum_everywhere(
-        stacked, coarse_grad, bottom, upward_grad, down_weight, hidden_pre, taps, class_grad
+        stacked, coarse, upward_grad, bottom_grad, inner_back, joint,
+        reduce.reshape(9 * INNER // 2, 2 * PART), expand_tall, down_weight, hidden_pre, taps,
+        class_grad,
     )
     reduce_grad = reduce_grad.reshape(3, 3, INNER // 2, -1)
     expand_grad = jnp.transpose(expand_grad.reshape(9, INNER // 2, -1)[::-1], (0, 2, 1))

time: 196 us -> 169 us (0.86)
  Pallas kernels: 178 us -> 161 us
  local copies, waits for them, and re-layouts: 11.8 us -> 2.3 us
    pallas_call x2, Pallas kernels: 132 us -> 112 us  [bottleneck(): pl.pallas_call(functools.partial(phase_kernel, backward), out_shape=out_s...]
    unnamed x22 -> x12, local copies, waits for them, and re-layouts: 5.6 us -> 1.43 us
    pallas_call x1, Pallas kernels: 45.9 us -> 49.5 us  [sum_everywhere(): pl.pallas_call(sum_kernel, out_shape=[jax.ShapeDtypeStruct((PART, 2 * PAR...]
    squeeze x6 -> x0, local copies, waits for them, and re-layouts: 2.36 us -> none  [the longest x1 1.27 us: sum_everywhere(): down = jnp.concatenate([out[0, 0:512], out[1, 0:512]], axis=1).astype(f32)]
where the time goes in v5:
time: 169 us
  Pallas kernels  161 us (95%)
  other arithmetic  5.09 us (3%)
  local copies, waits for them, and re-layouts  2.3 us (1%)
    pallas_call x2, Pallas kernels, bottleneck(): pl.pallas_call(functools.partial(phase_kernel, backward), out_shape=out_s...  112 us
    pallas_call x1, Pallas kernels, sum_everywhere(): pl.pallas_call(sum_kernel, out_shape=[jax.ShapeDtypeStruct((PART, 2 * PAR...  49.5 us

profile of v5, /device:TPU:1, one launch (start us, length us, event | category | flops | bytes accessed | tf_op | source)
XLA Modules:
  0.0 169.1 jit_solution(4991864379232375319)
XLA Ops:
  0.6 48.7 %forward_phase.1 = (f32[2,96,256]{2,1,0:T(8,128)}, f32[3072,128]{1,0:T(8,128)}, bf16[3168,384]{1,0:T(8,128)(2,1)}, bf16[3072,256]{1,0:T(8,128)(2,1)}, bf16[256,1...) custom-call(bf16[4,96,128]{2,1,0:T(8,128)(2,1)} %bitcast.25, ...), custom_call_target="tpu_custom_call" | custom-call | tf_op jit(solution)/shard_map/forward_phase/pallas_call | solution.py:770
  49.4 62.8 %backward_phase.1 = (f32[2,96,256]{2,1,0:T(8,128)}, f32[576,256]{1,0:T(8,128)}, f32[576,256]{1,0:T(8,128)}, bf16[96,512]{1,0:T(8,128)(2,1)}, f32[9,128]{1,0:T(8,...) custom-call(bf16[256,1152]{1,0:T(8,128)(2,1)} %get-tuple-element.30.refs_0_, ...), custom_call_target="tpu_custom_call" | custom-call | tf_op jit(solution)/shard_map/backward_phase/pallas_call | solution.py:770
  112.2 0.0 copy-start.3
  112.2 49.5 %sum_everywhere.1 = (bf16[512,1024]{1,0:T(8,128)(2,1)}, bf16[1024,512]{1,0:T(8,128)(2,1)}, bf16[1152,128]{1,0:T(8,128)(2,1)}, f32[9,128]{1,0:T(8,128)}) custom-call(bf16[96,512]{1,0:T(8,128)(2,1)} %get-tuple-element.28.refs_7_.stacked_ref, bf16[2,96,512]{2,1,0:T(8,128)(2,1)} %get-tuple-element.29.refs_5_.coarse_ref, ...), custom_call_target="tpu_custom_call" | custom-call | tf_op jit(solution)/shard_map/sum_everywhere/pallas_call | solution.py:932
  161.7 0.0 copy-start.1
  161.7 1.9 %convert.1 = f32[3,3,128,128]{3,2,1,0:T(8,128)} convert(bf16[3,3,128,128]{3,2,1,0:T(8,128)(2,1)} %bitcast.24) | non-fusion elementwise | flops 147456 | bytes 884736 | tf_op jit(solution)/shard_map/reshape | solution.py:962
  163.6 0.0 copy-done.3
  163.6 0.9 rev.3
  164.4 0.0 copy-done.1
  164.5 0.0 copy-start
  164.5 1.6 convert_element_type.7
  166.0 0.0 copy-done
  166.0 0.0 copy-start.2
  166.0 0.0 copy-start.4
  166.0 1.6 convert_element_type.8
  167.6 0.0 copy-done.2
  167.6 0.8 copy.16
  168.5 0.0 copy-done.4
  168.5 0.6 copy.17
Async XLA Ops:
  112.2 51.4 %copy-start.3 = (f32[576,256]{1,0:T(8,128)S(1)}, f32[576,256]{1,0:T(8,128)}, u32[]{:S(2)}) copy-start(f32[576,256]{1,0:T(8,128)} %get-tuple-element.46) | copy-start | bytes 1769476
  161.7 2.8 %copy-start.1 = (bf16[512,1024]{1,0:T(8,128)(2,1)S(1)}, bf16[512,1024]{1,0:T(8,128)(2,1)}, u32[]{:S(2)}) copy-start(bf16[512,1024]{1,0:T(8,128)(2,1)} %get-tuple-element.45) | copy-start | bytes 3145732
  164.5 1.6 copy-start
  166.0 1.6 copy-start.2
  166.0 2.4 %copy-start.4 = (f32[9,128]{1,0:T(8,128)S(1)}, f32[9,128]{1,0:T(8,128)}, u32[]{:S(2)}) copy-start(f32[9,128]{1,0:T(8,128)} %get-tuple-element.49) | copy-start | bytes 13828

commit v6 on v5

--- a/solution.py
+++ b/solution.py
@@ -192,10 +192,10 @@
     if backward:
         (
             wa_hbm, wb_hbm, pre_hbm, ef_hbm, xf_hbm, coarse_ref, inner_ref, stacked_ref, label_ref,
-            up_weight_ref, down_weight_ref, class_ref,
-            out_ref, ge_ref, gf_ref, upward_grad_ref, class_grad_ref, bottom_grad_ref, joint_ref,
-        ) = refs[:19]
-        scratch = refs[19:]
+            up_weight_ref, class_ref,
+            out_ref, ge_ref, upward_grad_ref, class_grad_ref, bottom_grad_ref, joint_ref,
+        ) = refs[:17]
+        scratch = refs[17:]
     else:
         (
             feature_ref, conv_weight_ref, down_weight_ref, up_weight_ref, expand_hbm, reduce_hbm,
@@ -333,21 +333,22 @@
         lax.fori_loop(0, 9, pack, 0)
         copies.start(38 + which, give.at[which], joint.at[which, core], partner)
 
+    def take_over(which):
+        copies.arrived(38 + which, joint.at[which, 1 - core], partner)
+        both = jnp.concatenate([joint[which, 0], joint[which, 1]], axis=1)
+        joint_ref[which] = both
+        return both
+
     def share(which, at, low, length):
         at = at % 4
         lanes = pl.ds(pl.multiple_of((at % 2) * 256, 256), 256)
         return full.at[which, at // 2, pl.ds(low, length), lanes]
 
     def depth_far(which):
-        copies.arrived(38 + which, joint.at[which, 1 - core], partner)
-        both = jnp.concatenate([joint[which, 0], joint[which, 1]], axis=1)
-        joint_ref[which] = both
+        both = take_over(which)
         for half in range(2):
             part = slice(half * PART, (half + 1) * PART)
-            if which == 0:
-                full[which, half] = narrow(contract_last(both, up_weight_ref[part, :]))
-            else:
-                full[which, half] = narrow(multiply(both, down_weight_ref[:, part]))
+            full[which, half] = narrow(contract_last(both, up_weight_ref[part, :]))
         copies.start(40 + which, share(which, depth + 2, 0, 288), zfar_in.at[which, 0], z_up)
         copies.start(42 + which, share(which, depth + 2, 288, 288), zfar_in.at[which, 1], z_down)
 
@@ -646,8 +647,6 @@
     copies.start(52, far2_out.at[0], far2_in.at[0], f_up)
     far2_out[1] = narrow(gathered(0, HALF, HALF))
     copies.start(53, far2_out.at[1], far2_in.at[1], f_down)
-    if backward:
-        depth_far(1)
     arrive_second(1)
     up2_out[HALF:, :] = narrow(gathered(1, HALF, HALF))
     copies.arrived(52, far2_in.at[0], f_up)
@@ -659,7 +658,7 @@
     down2_out[HALF:, :] = narrow(gathered(2, HALF, HALF) + far2_in[1].astype(jnp.float32))
     copies.start(55, down2_out, down2_in, f_down)
     if backward:
-        depth_near(1)
+        take_over(1)
     arrive_second(3)
     copies.arrived(54, up2_in, f_up)
     copies.arrived(55, down2_in, f_down)
@@ -681,7 +680,6 @@
     out_ref[1 - core] = swap_in[...].astype(jnp.float32)
     if backward:
         depth_own(0, ge_ref)
-        depth_own(1, gf_ref)
     copies.finish()
     for store in stores:
         store.wait()
@@ -697,12 +695,12 @@
     pair = shape((2, HALF, PART), b16)
     if backward:
         grad = shape((9 * INNER // 2, PART // 2), f32)
-        in_specs = [anywhere] * 5 + [vmem] * 7
+        in_specs = [anywhere] * 5 + [vmem] * 6
         out_shape = [
-            out, grad, grad, shape((HALF, PART), b16), shape((9, INNER), f32), pair,
+            out, grad, shape((HALF, PART), b16), shape((9, INNER), f32), pair,
             shape((2, 9 * INNER // 2, PART), b16),
         ]
-        out_specs = [vmem] * 7
+        out_specs = [vmem] * 6
     else:
         in_specs = [vmem] * 4 + [anywhere] * 2
         out_shape = [
@@ -786,8 +784,9 @@
 
 
 def sum_kernel(stacked_ref, coarse_ref, upward_grad_ref, bottom_grad_ref, inner_ref, joint_ref,
-               reduce_ref, expand_ref, down_weight_ref, hidden_pre_ref, taps_ref, class_ref, down_out, up_out, conv_out, class_out, total, give, pair_in, a_out, a_in,
-               b_out, b_in, z_out, z_in, result, conv_ref, send_sems, recv_sems):
+               reduce_ref, expand_ref, down_weight_ref, hidden_pre_ref, taps_ref, class_ref, down_out, up_out, conv_out, class_out, expand_out, total, give, pair_in, a_out, a_in,
+               b_out, b_in, z_out, z_in, result, conv_ref, full, zfar_in, zup_out, zdown_out,
+               zup_in, zdown_in, send_sems, recv_sems):
     core, first, second = place()
     depth = lax.axis_index("samp")
     me = block_of(core, first, second)
@@ -856,6 +855,21 @@
             )
             copies.start(16 + i * 3 + df - 1, a_out.at[df, i], a_in.at[df, i], first_peers[df])
 
+    z_up, z_down = depth_peers[1], depth_peers[3]
+
+    def share(at, low, length):
+        at = at % 4
+        return full.at[at // 2, pl.ds(low, length), own_lanes(at % 2, 256)]
+
+    def plus(left, right):
+        return left.astype(jnp.float32) + right.astype(jnp.float32)
+
+    for half in range(2):
+        part = slice(half * PART, (half + 1) * PART)
+        full[half] = multiply(joint_ref[1], down_weight_ref[:, part]).astype(jnp.bfloat16)
+    copies.start(68, share(depth + 2, 0, 288), zfar_in.at[0], z_up)
+    copies.start(69, share(depth + 2, 288, 288), zfar_in.at[1], z_down)
+
     def after_first(i):
         part = spot(first, second + order[i])
         copies.arrived(i * 4, pair_in.at[part, :], partner)
@@ -869,6 +883,12 @@
         b_out[i] = after_first(i).astype(jnp.bfloat16)
         copies.start(28 + i, b_out.at[i], b_in.at[i], second_peers[order[i]])
     total[0:80, :] = after_first(3)
+    zup_out[288:576, :] = share(depth + 1, 288, 288)[...]
+    zdown_out[0:288, :] = share(depth + 3, 0, 288)[...]
+    copies.arrived(68, zfar_in.at[0], z_up)
+    zup_out[0:288, :] = plus(share(depth + 1, 0, 288)[...], zfar_in[0]).astype(jnp.bfloat16)
+    copies.arrived(69, zfar_in.at[1], z_down)
+    zdown_out[288:576, :] = plus(share(depth + 3, 288, 288)[...], zfar_in[1]).astype(jnp.bfloat16)
     for i in range(3):
         copies.arrived(28 + i, b_in.at[i], second_peers[order[i]])
         total[0:80, :] += b_in[i].astype(jnp.float32)
@@ -898,6 +918,8 @@
         copies.start(33 + d, at_depth(0), at_depth(0), depth_peers[d])
     for d in range(1, 4):
         copies.arrived(33 + d, at_depth(4 - d), depth_peers[d])
+    copies.start(70, zup_out, zup_in, z_up)
+    copies.start(71, zdown_out, zdown_in, z_down)
     for ds in range(1, 4):
         copies.start(36 + ds, at(0, 0, core), at(0, 0, core), second_peers[ds])
     along_first(0)
@@ -910,6 +932,12 @@
         for df in (1, 3, 2):
             copies.arrived(40 + ds * 3 + df - 1, at(4 - df, ds, core), first_peers[df])
             pass_on(4 - df, ds)
+    copies.arrived(70, zup_in, z_up)
+    copies.arrived(71, zdown_in, z_down)
+    expand_out[...] = plus(share(depth, 0, 576)[...], zup_in[...]) + zdown_in[...].astype(
+        jnp.float32
+    )
+
     def unpack(half):
         down_out[:, own_lanes(half, PART)] = result[half, 0:512, :]
         up_out[pl.ds(pl.multiple_of(half * PART, PART), PART), :] = result[half, 512:1024, :]
@@ -929,16 +957,17 @@
 def sum_everywhere(*operands):
     b16, f32 = jnp.bfloat16, jnp.float32
     vmem = pl.BlockSpec(memory_space=pltpu.VMEM)
-    down, up, conv, small = pl.pallas_call(
+    down, up, conv, small, expand = pl.pallas_call(
         sum_kernel,
         out_shape=[
             jax.ShapeDtypeStruct((PART, 2 * PART), b16),
             jax.ShapeDtypeStruct((2 * PART, PART), b16),
             jax.ShapeDtypeStruct((9 * INNER, INNER), b16),
             jax.ShapeDtypeStruct((9, INNER), f32),
+            jax.ShapeDtypeStruct((9 * INNER // 2, PART // 2), f32),
         ],
         in_specs=[vmem] * 12,
-        out_specs=[vmem] * 4,
+        out_specs=[vmem] * 5,
         scratch_shapes=[
             pltpu.VMEM((SUM_ROWS, PART), f32),
             pltpu.VMEM((SUM_ROWS, PART), b16),
@@ -951,8 +980,11 @@
             pltpu.VMEM((4, 80, 128), b16),
             pltpu.VMEM((2, SUM_ROWS, PART), b16),
             pltpu.VMEM((9 * INNER, INNER), f32),
-            pltpu.SemaphoreType.DMA((68,)),
-            pltpu.SemaphoreType.DMA((68,)),
+            pltpu.VMEM((2, 576, PART), b16),
+            pltpu.VMEM((2, 288, 256), b16),
+            *[pltpu.VMEM((576, 256), b16) for _ in range(4)],
+            pltpu.SemaphoreType.DMA((72,)),
+            pltpu.SemaphoreType.DMA((72,)),
         ],
         compiler_params=pltpu.CompilerParams(
             collective_id=3, has_side_effects=True, vmem_limit_bytes=60 * 1024 * 1024
@@ -960,7 +992,7 @@
         name="sum_everywhere",
     )(*operands)
     conv = conv.astype(f32).reshape(3, 3, INNER, INNER)
-    return conv, down.astype(f32), up.astype(f32), small.T
+    return conv, down.astype(f32), up.astype(f32), small.T, expand
 
 
 def local(
@@ -982,11 +1014,11 @@
         False, features[0], conv_weight.reshape(9 * INNER, INNER), down_weight, up_weight, expand,
         reduce,
     )
-    inner_back, reduce_grad, expand_grad, upward_grad, class_grad, bottom_grad, joint = bottleneck(
+    inner_back, reduce_grad, upward_grad, class_grad, bottom_grad, joint = bottleneck(
         True, wa_back, wb_back, pre, expanded, gathered, coarse, inner, stacked, labels[0], up_weight,
-        down_weight, class_weight.T,
+        class_weight.T,
     )
-    conv_grad, down_grad, up_grad, class_grad = sum_everywhere(
+    conv_grad, down_grad, up_grad, class_grad, expand_grad = sum_everywhere(
         stacked, coarse, upward_grad, bottom_grad, inner_back, joint,
         reduce.reshape(9 * INNER // 2, 2 * PART), expand_tall, down_weight, hidden_pre, taps,
         class_grad,

time: 169 us -> 158 us (0.935)
  Pallas kernels: 161 us -> 149 us
    pallas_call x2, Pallas kernels: 112 us -> 101 us  [bottleneck(): pl.pallas_call(functools.partial(phase_kernel, backward), out_shape=out_s...]
where the time goes in v6:
time: 158 us
  Pallas kernels  149 us (94%)
  other arithmetic  5.09 us (3%)
  local copies, waits for them, and re-layouts  3.34 us (2%)
    pallas_call x2, Pallas kernels, bottleneck(): pl.pallas_call(functools.partial(phase_kernel, backward), out_shape=out_s...  101 us
    pallas_call x1, Pallas kernels, sum_everywhere(): pl.pallas_call(sum_kernel, out_shape=[jax.ShapeDtypeStruct((PART, 2 * PAR...  48.5 us
    convert_element_type x2, other arithmetic, sum_everywhere(): return (conv, down.astype(f32), up.astype(f32), small.T, expand)  3.18 us

profile of v6, /device:TPU:1, one launch (start us, length us, event | category | flops | bytes accessed | tf_op | source)
XLA Modules:
  0.0 158.2 jit_solution(12204138393356336480)
XLA Ops:
  0.6 48.8 %forward_phase.1 = (f32[2,96,256]{2,1,0:T(8,128)}, f32[3072,128]{1,0:T(8,128)}, bf16[3168,384]{1,0:T(8,128)(2,1)}, bf16[3072,256]{1,0:T(8,128)(2,1)}, bf16[256,1...) custom-call(bf16[4,96,128]{2,1,0:T(8,128)(2,1)} %bitcast.25, ...), custom_call_target="tpu_custom_call" | custom-call | tf_op jit(solution)/shard_map/forward_phase/pallas_call | solution.py:768
  49.4 51.8 %backward_phase.1 = (f32[2,96,256]{2,1,0:T(8,128)}, f32[576,256]{1,0:T(8,128)}, bf16[96,512]{1,0:T(8,128)(2,1)}, f32[9,128]{1,0:T(8,128)}, bf16[2,96,512]{2,1,0:T(8,128)(2,1)}, /*index=5*/bf16[2,576,512]{2,1,0:T(8,128)(2,1)}) custom-call(bf16[256,1152]{1,0:T(8,128)(2,1)} %get-tuple-element.30.refs_0_, bf16[1152,256]{1,0:T(8,128)(2,1)} %get-tuple-element.31.refs_1_, ...), custom_call_target="tpu_custom_call" | custom-call | tf_op jit(solution)/shard_map/backward_phase/pallas_call | solution.py:768
  101.2 48.5 %sum_everywhere.1 = (bf16[512,1024]{1,0:T(8,128)(2,1)}, bf16[1024,512]{1,0:T(8,128)(2,1)}, bf16[1152,128]{1,0:T(8,128)(2,1)}, f32[9,128]{1,0:T(8,128)}, f32[576,256]{1,0:T(8,128)}) custom-call(bf16[96,512]{1,0:T(8,128)(2,1)} %get-tuple-element.28.refs_7_.stacked_ref, bf16[2,96,512]{2,1,0:T(8,128)(2,1)} %get-tuple-element.29.refs_5_.coarse_ref, ...), custom_call_target="tpu_custom_call" | custom-call | tf_op jit(solution)/shard_map/sum_everywhere/pallas_call | solution.py:960
  149.8 0.0 copy-start.1
  149.8 1.9 %convert.1 = f32[3,3,128,128]{3,2,1,0:T(8,128)} convert(bf16[3,3,128,128]{3,2,1,0:T(8,128)(2,1)} %bitcast.24) | non-fusion elementwise | flops 147456 | bytes 884736 | tf_op jit(solution)/shard_map/reshape | solution.py:994
  151.7 1.9 %rev.3 = f32[9,64,256]{2,1,0:T(8,128)} reverse(f32[9,64,256]{2,1,0:T(8,128)} %bitcast.22), dimensions={0} | reverse | bytes 1179648 | tf_op jit(solution)/shard_map/rev | solution.py:1027
  153.6 0.0 copy-done.1
  153.6 0.0 copy-start
  153.6 1.6 convert_element_type.7
  155.2 0.0 copy-done
  155.2 0.0 copy-start.2
  155.2 0.0 copy-start.3
  155.2 1.6 %convert_element_type.8 = f32[1024,512]{1,0:T(8,128)} convert(bf16[1024,512]{1,0:T(8,128)(2,1)S(1)} %copy-done) | non-fusion elementwise | flops 524288 | bytes 3145728 | tf_op jit(solution)/shard_map/convert_element_type | solution.py:995
  156.8 0.0 copy-done.2
  156.8 0.8 copy.16
  157.6 0.0 copy-done.3
  157.6 0.6 copy.17
Async XLA Ops:
  149.8 3.8 %copy-start.1 = (bf16[512,1024]{1,0:T(8,128)(2,1)S(1)}, bf16[512,1024]{1,0:T(8,128)(2,1)}, u32[]{:S(2)}) copy-start(bf16[512,1024]{1,0:T(8,128)(2,1)} %get-tuple-element.45) | copy-start | bytes 3145732
  153.6 1.6 copy-start
  155.2 1.6 %copy-start.2 = (f32[576,256]{1,0:T(8,128)S(1)}, f32[576,256]{1,0:T(8,128)}, u32[]{:S(2)}) copy-start(f32[576,256]{1,0:T(8,128)} %get-tuple-element.47) | copy-start | bytes 1769476
  155.2 2.4 %copy-start.3 = (f32[9,128]{1,0:T(8,128)S(1)}, f32[9,128]{1,0:T(8,128)}, u32[]{:S(2)}) copy-start(f32[9,128]{1,0:T(8,128)} %get-tuple-element.49) | copy-start | bytes 13828

commit v7 on v6

--- a/solution.py
+++ b/solution.py
@@ -842,12 +842,12 @@
     pack(1 - core, give, jnp.bfloat16)
     pl.semaphore_wait(barrier, 10)
     for i, ds in enumerate(order):
-        for df in range(4):
+        for df in (2, 1, 3, 0):
             part = spot(second + df, first + ds)
             copies.start(i * 4 + df, give.at[part, :], pair_in.at[part, :], partner)
     pack(core, total, jnp.float32)
     for i, ds in enumerate(order):
-        for df in range(1, 4):
+        for df in (2, 1, 3):
             part = spot(first + df, second + ds)
             copies.arrived(i * 4 + df, pair_in.at[part, :], partner)
             a_out[df, i] = (total[part, :] + pair_in[part, :].astype(jnp.float32)).astype(
@@ -910,7 +910,7 @@
         copies.start(52 + df * 4 + ds, at(df, ds, core), at(df, ds, core), partner)
 
     def along_first(ds):
-        for df in range(1, 4):
+        for df in (2, 1, 3):
             copies.start(40 + ds * 3 + df - 1, at(0, ds, core), at(0, ds, core), first_peers[df])
 
     at_depth(0)[...] = value.astype(jnp.bfloat16)

time: 158 us -> 158 us (level)
  no operation moved by 1% of the time
where the time goes in v7:
time: 158 us
  Pallas kernels  149 us (94%)
  other arithmetic  5.09 us (3%)
  local copies, waits for them, and re-layouts  3.34 us (2%)
    pallas_call x2, Pallas kernels, bottleneck(): pl.pallas_call(functools.partial(phase_kernel, backward), out_shape=out_s...  101 us
    pallas_call x1, Pallas kernels, sum_everywhere(): pl.pallas_call(sum_kernel, out_shape=[jax.ShapeDtypeStruct((PART, 2 * PAR...  48.5 us
    convert_element_type x2, other arithmetic, sum_everywhere(): return (conv, down.astype(f32), up.astype(f32), small.T, expand)  3.18 us

profile of v7, /device:TPU:1, one launch (start us, length us, event | category | flops | bytes accessed | tf_op | source)
XLA Modules:
  0.0 158.2 jit_solution(349761080924968749)
XLA Ops:
  0.6 48.8 %forward_phase.1 = (f32[2,96,256]{2,1,0:T(8,128)}, f32[3072,128]{1,0:T(8,128)}, bf16[3168,384]{1,0:T(8,128)(2,1)}, bf16[3072,256]{1,0:T(8,128)(2,1)}, bf16[256,1...) custom-call(bf16[4,96,128]{2,1,0:T(8,128)(2,1)} %bitcast.25, ...), custom_call_target="tpu_custom_call" | custom-call | tf_op jit(solution)/shard_map/forward_phase/pallas_call | solution.py:768
  49.4 51.8 %backward_phase.1 = (f32[2,96,256]{2,1,0:T(8,128)}, f32[576,256]{1,0:T(8,128)}, bf16[96,512]{1,0:T(8,128)(2,1)}, f32[9,128]{1,0:T(8,128)}, bf16[2,96,512]{2,1,0:T(8,128)(2,1)}, /*index=5*/bf16[2,576,512]{2,1,0:T(8,128)(2,1)}) custom-call(bf16[256,1152]{1,0:T(8,128)(2,1)} %get-tuple-element.30.refs_0_, bf16[1152,256]{1,0:T(8,128)(2,1)} %get-tuple-element.31.refs_1_, ...), custom_call_target="tpu_custom_call" | custom-call | tf_op jit(solution)/shard_map/backward_phase/pallas_call | solution.py:768
  101.2 48.5 %sum_everywhere.1 = (bf16[512,1024]{1,0:T(8,128)(2,1)}, bf16[1024,512]{1,0:T(8,128)(2,1)}, bf16[1152,128]{1,0:T(8,128)(2,1)}, f32[9,128]{1,0:T(8,128)}, f32[576,256]{1,0:T(8,128)}) custom-call(bf16[96,512]{1,0:T(8,128)(2,1)} %get-tuple-element.28.refs_7_.stacked_ref, bf16[2,96,512]{2,1,0:T(8,128)(2,1)} %get-tuple-element.29.refs_5_.coarse_ref, ...), custom_call_target="tpu_custom_call" | custom-call | tf_op jit(solution)/shard_map/sum_everywhere/pallas_call | solution.py:960
  149.7 0.0 copy-start.1
  149.7 1.9 %convert.1 = f32[3,3,128,128]{3,2,1,0:T(8,128)} convert(bf16[3,3,128,128]{3,2,1,0:T(8,128)(2,1)} %bitcast.24) | non-fusion elementwise | flops 147456 | bytes 884736 | tf_op jit(solution)/shard_map/reshape | solution.py:994
  151.6 1.9 %rev.3 = f32[9,64,256]{2,1,0:T(8,128)} reverse(f32[9,64,256]{2,1,0:T(8,128)} %bitcast.22), dimensions={0} | reverse | bytes 1179648 | tf_op jit(solution)/shard_map/rev | solution.py:1027
  153.5 0.0 copy-done.1
  153.5 0.0 copy-start
  153.5 1.6 convert_element_type.7
  155.1 0.0 copy-done
  155.1 0.0 copy-start.2
  155.1 0.0 copy-start.3
  155.1 1.6 %convert_element_type.8 = f32[1024,512]{1,0:T(8,128)} convert(bf16[1024,512]{1,0:T(8,128)(2,1)S(1)} %copy-done) | non-fusion elementwise | flops 524288 | bytes 3145728 | tf_op jit(solution)/shard_map/convert_element_type | solution.py:995
  156.7 0.0 copy-done.2
  156.7 0.8 copy.16
  157.5 0.0 copy-done.3
  157.6 0.6 copy.17
Async XLA Ops:
  149.7 3.8 %copy-start.1 = (bf16[512,1024]{1,0:T(8,128)(2,1)S(1)}, bf16[512,1024]{1,0:T(8,128)(2,1)}, u32[]{:S(2)}) copy-start(bf16[512,1024]{1,0:T(8,128)(2,1)} %get-tuple-element.45) | copy-start | bytes 3145732
  153.5 1.6 copy-start
  155.1 1.6 %copy-start.2 = (f32[576,256]{1,0:T(8,128)S(1)}, f32[576,256]{1,0:T(8,128)}, u32[]{:S(2)}) copy-start(f32[576,256]{1,0:T(8,128)} %get-tuple-element.47) | copy-start | bytes 1769476
  155.1 2.4 %copy-start.3 = (f32[9,128]{1,0:T(8,128)S(1)}, f32[9,128]{1,0:T(8,128)}, u32[]{:S(2)}) copy-start(f32[9,128]{1,0:T(8,128)} %get-tuple-element.49) | copy-start | bytes 13828
